TPU v7x, 256 devices: a whole 4x4x8 slice. The times are simulated.
256 devices in a mesh: kv: 4 (over y), leaf: 64 (over x, z, core).
Axes of the slice: x: 4, y: 4, z: 8, core: 2. Of those that a mesh axis runs over, the one named last changes fastest.
Arguments:
- queries: bfloat16 [2, 256, 4, 2048], P(None, 'leaf', 'kv'), may hold values from -8 to 8
- query_gain: float32 [128], replicated, may hold values from 0.5 to 1.5
- new_keys: bfloat16 [2, 256, 4, 128], P(None, 'leaf', 'kv'), may hold values from -12 to 12
- new_values: bfloat16 [2, 256, 4, 128], P(None, 'leaf', 'kv'), may hold values from -6 to 6
- root_keys: bfloat16 [32768, 4, 128], P('leaf', 'kv'), may hold values from -40 to 40
- root_values: bfloat16 [32768, 4, 128], P('leaf', 'kv'), may hold values from -6 to 6
- branch_keys: bfloat16 [131072, 4, 128], P('leaf', 'kv'), may hold values from -9 to 9
- branch_values: bfloat16 [131072, 4, 128], P('leaf', 'kv'), may hold values from -6 to 6
- suffix_keys: bfloat16 [256, 512, 4, 128], P('leaf', None, 'kv'), may hold values from -9 to 9
- suffix_values: bfloat16 [256, 512, 4, 128], P('leaf', None, 'kv'), may hold values from -6 to 6
- out_weight: bfloat16 [8192, 4096], P('kv', 'leaf'), may hold values from -0.0625 to 0.0625
- request_branch: int32 [256], replicated, may hold values from 0 to 15
- branch_blocks: int32 [16], replicated, may hold values from 1 to 128, 512 in all
- suffix_length: int32 [256], P('leaf'), may hold values from 1 to 512, 65536 in all
- block_slot: int32 [512], replicated, may hold values from 0 to 511, each once
Outputs:
- attn_out: float32 [2, 256, 4, 2048], P(None, 'leaf', 'kv')
- log_total: float32 [2, 256, 4, 16], P(None, 'leaf', 'kv')
- layer_out: float32 [2, 256, 4096], P(None, 'kv', 'leaf')
Inputs may be any that keep to these rules, and one draw needn't show every extreme that they name: `branch_blocks`: every branch has one block or more; they sum to 512; the largest is exactly 128. `suffix_length`: they sum to 65536; the largest is exactly 512. `block_slot`: a permutation of 0 .. 511.
All inputs are finite; a program needn't handle non-finite values. No bound on the sum of `suffix_length` on one device may be relied on, other than what follows from the above.
Results may differ from a plain program's by a relative error of at most 0.014.
Values may be sent and summed in bfloat16 or wider, within the bound.
No kernel may reach another device: no remote copies, remote signals or barrier semaphores. Data moves between devices by JAX's collectives and lax.ppermute only.
A program may use at most 64 MiB of HBM per device.

v0:
```python
import math

import jax
import jax.numpy as jnp
from jax import lax
from jax.sharding import PartitionSpec as P

HD = 128
BLK = 256
SUF = 512
STEPS = 2


def norm_heads(raw_query, query_gain):
    mean_square = jnp.mean(raw_query * raw_query, axis=-1, keepdims=True)
    return (raw_query * lax.rsqrt(mean_square + 1e-06) * query_gain).astype(jnp.bfloat16)


def token_branch(branch_blocks, block_slot, slot_ids):
    block_count = block_slot.shape[0]
    block_ids = jnp.arange(block_count, dtype=jnp.int32)
    slot_block = jnp.sum(
        jnp.where(block_slot[:, None] == slot_ids[None, :], block_ids[:, None], 0), axis=0
    )
    cum_end = jnp.cumsum(branch_blocks)
    block_branch = jnp.sum((cum_end[None, :] <= slot_block[:, None]).astype(jnp.int32), axis=1)
    return jnp.repeat(block_branch, BLK)


def shards(
    queries,
    query_gain,
    new_keys,
    new_values,
    root_keys,
    root_values,
    branch_keys,
    branch_values,
    suffix_keys,
    suffix_values,
    out_weight,
    request_branch,
    branch_blocks,
    suffix_length,
    block_slot,
):
    leaves = lax.axis_size("leaf")
    owned_rows = queries.shape[1]
    heads_kv = queries.shape[2]
    group_size = queries.shape[3] // HD
    requests = request_branch.shape[0]
    score_scale = 1.0 / math.sqrt(HD)
    slots_here = branch_keys.shape[0] // BLK
    slot_ids = lax.axis_index("leaf") * slots_here + jnp.arange(slots_here, dtype=jnp.int32)
    shared_branch = jnp.concatenate(
        [
            jnp.full((root_keys.shape[0],), -1, jnp.int32),
            token_branch(branch_blocks, block_slot, slot_ids),
        ]
    )
    shared_keys = jnp.concatenate([root_keys, branch_keys], 0)
    shared_values = jnp.concatenate([root_values, branch_values], 0)
    rows_block = math.gcd(requests, max(1, 512 // (heads_kv * group_size)))
    blocks_count = requests // rows_block
    own_keys = jnp.concatenate([suffix_keys, jnp.transpose(new_keys, (1, 0, 2, 3))], axis=1)
    own_values = jnp.concatenate([suffix_values, jnp.transpose(new_values, (1, 0, 2, 3))], axis=1)
    positions = jnp.arange(SUF + STEPS, dtype=jnp.int32)
    branch_rows = request_branch.reshape(blocks_count, rows_block)
    attn_steps = []
    lse_steps = []
    layer_steps = []
    for step_index in range(STEPS):
        raw_query = (
            queries[step_index].astype(jnp.float32).reshape(owned_rows, heads_kv, group_size, HD)
        )
        normed = norm_heads(raw_query, query_gain)
        everyone = lax.all_gather(
            normed.reshape(owned_rows, heads_kv, group_size * HD), "leaf", axis=0, tiled=True
        )
        everyone = everyone.reshape(blocks_count, rows_block, heads_kv, group_size, HD)

        def shared_part(block_item):
            query_rows, block_branch = block_item
            scores = (
                jnp.einsum(
                    "rhgd,thd->rhgt", query_rows, shared_keys, preferred_element_type=jnp.float32
                )
                * score_scale
            )
            seen = (shared_branch[None, :] == -1) | (
                shared_branch[None, :] == block_branch[:, None]
            )
            scores = jnp.where(seen[:, None, None, :], scores, -jnp.inf)
            row_top = jnp.max(scores, -1)
            weights = jnp.exp(scores - row_top[..., None])
            sum_exp = jnp.sum(weights, -1)
            numerator = jnp.einsum(
                "rhgt,thd->rhgd",
                weights.astype(jnp.bfloat16),
                shared_values,
                preferred_element_type=jnp.float32,
            )
            return (numerator, row_top, sum_exp)

        numerator, row_top, sum_exp = lax.map(shared_part, (everyone, branch_rows))
        numerator = numerator.reshape(requests, heads_kv, group_size, HD)
        row_top = row_top.reshape(requests, heads_kv, group_size)
        sum_exp = sum_exp.reshape(requests, heads_kv, group_size)
        own_scores = (
            jnp.einsum("rhgd,rthd->rhgt", normed, own_keys, preferred_element_type=jnp.float32)
            * score_scale
        )
        own_seen = (positions[None, :] < suffix_length[:, None]) | (positions[None, :] >= SUF) & (
            positions[None, :] <= SUF + step_index
        )
        own_scores = jnp.where(own_seen[:, None, None, :], own_scores, -jnp.inf)
        own_top = jnp.max(own_scores, -1)
        own_weights = jnp.exp(own_scores - own_top[..., None])
        own_sum = jnp.sum(own_weights, -1)
        own_numerator = jnp.einsum(
            "rhgt,rthd->rhgd",
            own_weights.astype(jnp.bfloat16),
            own_values,
            preferred_element_type=jnp.float32,
        )
        part_numerator, part_top, part_sum = (
            lax.all_to_all(
                numerator.reshape(leaves, owned_rows, heads_kv, group_size, HD),
                "leaf",
                split_axis=0,
                concat_axis=0,
                tiled=True,
            ),
            lax.all_to_all(
                row_top.reshape(leaves, owned_rows, heads_kv, group_size),
                "leaf",
                split_axis=0,
                concat_axis=0,
                tiled=True,
            ),
            lax.all_to_all(
                sum_exp.reshape(leaves, owned_rows, heads_kv, group_size),
                "leaf",
                split_axis=0,
                concat_axis=0,
                tiled=True,
            ),
        )
        best_max = jnp.max(part_top, 0)
        factor = jnp.exp(part_top - best_max[None])
        merged_sum = jnp.sum(part_sum * factor, 0)
        merged_numerator = jnp.sum(part_numerator * factor[..., None], 0)
        final_top = jnp.maximum(best_max, own_top)
        old_factor = jnp.exp(best_max - final_top)
        new_factor = jnp.exp(own_top - final_top)
        final_sum = merged_sum * old_factor + own_sum * new_factor
        final_numerator = (
            merged_numerator * old_factor[..., None] + own_numerator * new_factor[..., None]
        )
        lse_steps.append(final_top + jnp.log(final_sum))
        attended_full = (final_numerator / final_sum[..., None]).reshape(
            owned_rows, heads_kv, group_size * HD
        )
        attn_steps.append(attended_full)
        attended = attended_full.astype(jnp.bfloat16)
        piece_rows = lax.all_gather(attended, "leaf", axis=0, tiled=True)
        head_terms = jnp.dot(
            piece_rows.reshape(piece_rows.shape[0], -1),
            out_weight,
            preferred_element_type=jnp.float32,
        )
        layer_steps.append(lax.psum_scatter(head_terms, "kv", scatter_dimension=0, tiled=True))
    return (jnp.stack(attn_steps), jnp.stack(lse_steps), jnp.stack(layer_steps))


def solution(mesh):
    in_specs = (
        P(None, "leaf", "kv", None),
        P(),
        P(None, "leaf", "kv", None),
        P(None, "leaf", "kv", None),
        P("leaf", "kv", None),
        P("leaf", "kv", None),
        P("leaf", "kv", None),
        P("leaf", "kv", None),
        P("leaf", None, "kv", None),
        P("leaf", None, "kv", None),
        P("kv", "leaf"),
        P(),
        P(),
        P("leaf"),
        P(),
    )
    out_specs = (P(None, "leaf", "kv", None), P(None, "leaf", "kv", None), P(None, "kv", "leaf"))
    return jax.shard_map(shards, mesh=mesh, in_specs=in_specs, out_specs=out_specs, check_vma=False)
```

profile of v0, /device:TPU:40, one launch (start us, length us, event | category | flops | bytes accessed | tf_op | source)
XLA Modules:
  0.0 542.0 jit_solution(3388346239900200380)
XLA Ops:
  16.5 73.7 %all-gather.5.cloned.1.call-done = bf16[256,1,2048]{2,1,0:T(2,128)(2,1)} async-done(((bf16[4,1,2048]{2,1,0:T(2,128)(2,1)}), bf16[256,1,2048]{2,1,0:T(2,128)(2,1)}) %all-gather.5.cloned.1.call-update) | async-done | bytes 1048592 | tf_op jit(solution)/shard_map/all_gather | solution.py:77
  90.2 7.4 %reduce.23 = bf16[256,2048]{1,0:T(8,128)(2,1)S(1)} reduce(bf16[256,1,2048]{2,1,0:T(2,128)(2,1)} %all-gather.5.cloned.1.call-done, bf16[]{:T(256)} %constant.84), dimensions={1}, to_apply=%all_gather.12.reduce_sub_computation | reduce | bytes 2097154 | tf_op jit(solution)/shard_map/all_gather | solution.py:77
  101.6 41.5 %while.28 = (s32[]{:T(128)}, f32[8,32,1,16,128]{4,3,1,2,0:T(8,128)}, f32[8,32,1,16]{3,1,2,0:T(8,128)}, f32[8,32,1,16]{3,1,2,0:T(8,128)}, s32[2560]{0:T(1024)S(1)...) while((s32[]{:T(128)}, ...), condition=%wide.region_7.8_spmd, body=%wide.region_4.7_spmd.sunk | while | flops 680429056 | bytes 17669096 | solution.py:105
  101.7 2.0 fusion.120
  105.2 1.6 fusion.121
  106.9 2.0 fusion.120
  112.1 2.0 fusion.120
  117.3 2.0 fusion.120
  120.7 1.6 fusion.121
  122.5 2.0 fusion.120
  125.9 1.6 fusion.121
  127.7 2.0 fusion.120
  131.1 1.6 fusion.121
  132.9 2.0 fusion.120
  138.0 2.0 fusion.120
  141.5 1.6 fusion.121
  143.1 7.8 %all-to-all-start.1 = ((f32[64,4,1,16]{3,1,2,0:T(4,128)}), f32[64,4,1,16]{3,1,2,0:T(4,128)S(1)}, u32[]{:S(2)}, u32[]{:S(2)}) async-start(f32[64,4,1,16]{3,1,2,0:T(4,128)} %bitcast.39), calls=%async_computation.1 | async-start | bytes 262144 | tf_op jit(solution)/shard_map/all_to_all | solution.py:134
  150.9 18.2 %all-gather.7.cloned.1.call-done = bf16[256,1,2048]{2,1,0:T(2,128)(2,1)} async-done(((bf16[4,1,2048]{2,1,0:T(2,128)(2,1)}), bf16[256,1,2048]{2,1,0:T(2,128)(2,1)}) %all-gather.7.cloned.1.call-update) | async-done | bytes 1048592 | tf_op jit(solution)/shard_map/all_gather | solution.py:77
  169.1 7.4 %reduce.24 = bf16[256,2048]{1,0:T(8,128)(2,1)S(1)} reduce(bf16[256,1,2048]{2,1,0:T(2,128)(2,1)} %all-gather.7.cloned.1.call-done, bf16[]{:T(256)} %constant.84), dimensions={1}, to_apply=%all_gather.13.reduce_sub_computation | reduce | bytes 2097154 | tf_op jit(solution)/shard_map/all_gather | solution.py:77
  177.7 7.8 %all-to-all-start.2 = ((f32[64,4,1,16]{3,1,2,0:T(4,128)}), f32[64,4,1,16]{3,1,2,0:T(4,128)S(1)}, u32[]{:S(2)}, u32[]{:S(2)}) async-start(f32[64,4,1,16]{3,1,2,0:T(4,128)} %bitcast.49), calls=%async_computation.2 | async-start | bytes 262144 | tf_op jit(solution)/shard_map/all_to_all | solution.py:141
  187.1 36.6 %while.29 = (s32[]{:T(128)}, f32[8,32,1,16,128]{4,3,1,2,0:T(8,128)}, f32[8,32,1,16]{3,1,2,0:T(8,128)S(1)}, f32[8,32,1,16]{3,1,2,0:T(8,128)S(1)}, s32[2560]{0:T(1...) while((s32[]{:T(128)}, ...), condition=%wide.region_17.18_spmd, body=%wide.region_14.17_spmd.sunk | while | flops 680429056 | bytes 17697260 | solution.py:105
  187.2 2.0 fusion.126
  191.8 2.0 fusion.126
  194.6 1.6 fusion.127
  196.4 2.0 fusion.126
  199.2 1.6 fusion.127
  200.9 2.0 fusion.126
  203.8 1.6 fusion.127
  205.5 2.0 fusion.126
  208.3 1.6 fusion.127
  210.1 2.0 fusion.126
  212.9 1.6 fusion.127
  214.7 2.0 fusion.126
  217.5 1.6 fusion.127
  219.3 2.0 fusion.126
  222.1 1.6 fusion.127
  223.7 20.1 %all_to_all.30 = f32[64,4,1,16]{3,1,2,0:T(4,128)S(1)} all-to-all(f32[64,4,1,16]{3,1,2,0:T(4,128)S(1)} %bitcast.265), channel_id=1, replica_groups=mesh['kv'=4,'leaf'=64] {'leaf'}, dimensions={0} | all-to-all | bytes 32768 | tf_op jit(solution)/shard_map/all_to_all | solution.py:134
  243.9 15.0 %all_to_all.31 = f32[64,4,1,16]{3,1,2,0:T(4,128)S(1)} all-to-all(f32[64,4,1,16]{3,1,2,0:T(4,128)S(1)} %bitcast.266), channel_id=1, replica_groups=mesh['kv'=4,'leaf'=64] {'leaf'}, dimensions={0} | all-to-all | bytes 32768 | tf_op jit(solution)/shard_map/all_to_all | solution.py:141
  258.9 55.3 %all_to_all.32 = f32[64,4,1,16,128]{4,3,1,2,0:T(8,128)} all-to-all(f32[64,4,1,16,128]{4,3,1,2,0:T(8,128)} %bitcast.38), channel_id=1, replica_groups=mesh['kv'=4,'leaf'=64] {'leaf'}, dimensions={0} | all-to-all | bytes 4194304 | tf_op jit(solution)/shard_map/all_to_all | solution.py:127
  314.2 7.6 %all-to-all-start.3 = ((f32[64,4,1,16,128]{4,3,1,2,0:T(8,128)}), f32[64,4,1,16,128]{4,3,1,2,0:T(8,128)S(1)}, u32[]{:S(2)}, u32[]{:S(2)}) async-start(f32[64,4,1,16,128]{4,3,1,2,0:T(8,128)} %bitcast.55), calls=%async_computation.3 | async-start | bytes 4194304 | tf_op jit(solution)/shard_map/all_to_all | solution.py:127
  323.9 2.0 multiply_reduce_fusion.1
  328.6 44.2 %all-to-all-done.3 = f32[64,4,1,16,128]{4,3,1,2,0:T(8,128)S(1)} async-done(((f32[64,4,1,16,128]{4,3,1,2,0:T(8,128)}), f32[64,4,1,16,128]{4,3,1,2,0:T(8,128)S(1)}, u32[]{:S(2)}, u32[]{:S(2)}) %all-to-all-start.3) | async-done | bytes 2097184 | tf_op jit(solution)/shard_map/all_to_all | solution.py:127
  376.2 31.9 %all-gather.9.cloned.1.call-done = bf16[256,1,2048]{2,1,0:T(2,128)(2,1)} async-done(((bf16[4,1,2048]{2,1,0:T(2,128)(2,1)}), bf16[256,1,2048]{2,1,0:T(2,128)(2,1)}) %all-gather.9.cloned.1.call-update) | async-done | bytes 1048592 | tf_op jit(solution)/shard_map/all_gather | solution.py:166
  408.2 2.9 fusion.45
  411.2 75.2 %all-gather.11.cloned.1.call-done = bf16[256,1,2048]{2,1,0:T(2,128)(2,1)} async-done(((bf16[4,1,2048]{2,1,0:T(2,128)(2,1)}), bf16[256,1,2048]{2,1,0:T(2,128)(2,1)}) %all-gather.11.cloned.1.call-update) | async-done | bytes 1048592 | tf_op jit(solution)/shard_map/all_gather | solution.py:166
  486.4 2.9 fusion.42
  490.0 18.5 %reduce-scatter.3.cloned.1.call-done = f32[64,64]{1,0:T(8,128)} async-done(((f32[256,64]{1,0:T(8,128)}), f32[64,64]{1,0:T(8,128)}) %reduce-scatter.3.cloned.1.call-update) | async-done | bytes 16400 | tf_op jit(solution)/shard_map/reduce_scatter | solution.py:172
  508.5 25.2 %reduce-scatter.5.cloned.1.call-done = f32[64,64]{1,0:T(8,128)} async-done(((f32[256,64]{1,0:T(8,128)}), f32[64,64]{1,0:T(8,128)}) %reduce-scatter.5.cloned.1.call-update) | async-done | bytes 16400 | tf_op jit(solution)/shard_map/reduce_scatter | solution.py:172
  (166 shorter events, 53.3 us)
Async XLA Ops:
  7.2 401.0 %copy-start = (bf16[2048,64]{0,1:T(8,128)(2,1)S(1)}, bf16[2048,64]{0,1:T(8,128)(2,1)}, u32[]{:S(2)}) copy-start(bf16[2048,64]{0,1:T(8,128)(2,1)} %param.29) | copy-start | bytes 786436
  7.2 83.0 %all-gather.5.cloned.1.call-start = ((), (), s32[]{:S(2)}) async-start(), calls=%async_computation.8 | async-start | bytes 2129920 | tf_op jit(solution)/shard_map/all_gather | solution.py:77
  9.8 159.3 %all-gather.7.cloned.1.call-start = ((), (), s32[]{:S(2)}) async-start(), calls=%async_computation.9 | async-start | bytes 2129920 | tf_op jit(solution)/shard_map/all_gather | solution.py:77
  143.1 34.6 %all-to-all-start.1 = ((f32[64,4,1,16]{3,1,2,0:T(4,128)}), f32[64,4,1,16]{3,1,2,0:T(4,128)S(1)}, u32[]{:S(2)}, u32[]{:S(2)}) async-start(f32[64,4,1,16]{3,1,2,0:T(4,128)} %bitcast.39), calls=%async_computation.1 | async-start | bytes 262144 | tf_op jit(solution)/shard_map/all_to_all | solution.py:134
  177.7 46.0 %all-to-all-start.2 = ((f32[64,4,1,16]{3,1,2,0:T(4,128)}), f32[64,4,1,16]{3,1,2,0:T(4,128)S(1)}, u32[]{:S(2)}, u32[]{:S(2)}) async-start(f32[64,4,1,16]{3,1,2,0:T(4,128)} %bitcast.49), calls=%async_computation.2 | async-start | bytes 262144 | tf_op jit(solution)/shard_map/all_to_all | solution.py:141
  314.2 7.7 %copy-start.1 = (bf16[2,4,1,128]{3,1,2,0:T(4,128)(2,1)S(1)}, bf16[2,4,1,128]{3,1,2,0:T(4,128)(2,1)}, u32[]{:S(2)}) copy-start(bf16[2,4,1,128]{3,1,2,0:T(4,128)(2,1)} %param.21) | copy-start | bytes 6148
  314.2 7.7 %copy-start.2 = (bf16[2,4,1,128]{3,1,2,0:T(4,128)(2,1)S(1)}, bf16[2,4,1,128]{3,1,2,0:T(4,128)(2,1)}, u32[]{:S(2)}) copy-start(bf16[2,4,1,128]{3,1,2,0:T(4,128)(2,1)} %param.22) | copy-start | bytes 6148
  314.2 7.7 %copy-start.4 = (s32[4]{0:T(128)S(1)}, s32[4]{0:T(128)}, u32[]{:S(2)}) copy-start(s32[4]{0:T(128)} %param.32) | copy-start | bytes 52
  314.2 7.9 %copy-start.3 = (f32[128]{0:T(128)S(1)}, f32[128]{0:T(128)}, u32[]{:S(2)}) copy-start(f32[128]{0:T(128)} %param.20) | copy-start | bytes 1540
  314.2 58.6 %all-to-all-start.3 = ((f32[64,4,1,16,128]{4,3,1,2,0:T(8,128)}), f32[64,4,1,16,128]{4,3,1,2,0:T(8,128)S(1)}, u32[]{:S(2)}, u32[]{:S(2)}) async-start(f32[64,4,1,16,128]{4,3,1,2,0:T(8,128)} %bitcast.55), calls=%async_computation.3 | async-start | bytes 4194304 | tf_op jit(solution)/shard_map/all_to_all | solution.py:127
  321.8 86.3 %all-gather.9.cloned.1.call-start = ((), (), s32[]{:S(2)}) async-start(), calls=%async_computation.10 | async-start | bytes 2129920 | tf_op jit(solution)/shard_map/all_gather | solution.py:166
  323.8 2.1 copy-start.5
  326.8 159.6 %all-gather.11.cloned.1.call-start = ((), (), s32[]{:S(2)}) async-start(), calls=%async_computation.12 | async-start | bytes 2129920 | tf_op jit(solution)/shard_map/all_gather | solution.py:166
  375.5 133.0 %reduce-scatter.3.cloned.1.call-start = ((), (), s32[]{:S(2)}) async-start(), calls=%async_computation.11 | async-start | bytes 163840 | tf_op jit(solution)/shard_map/reduce_scatter | solution.py:172
  411.1 122.6 %reduce-scatter.5.cloned.1.call-start = ((), (), s32[]{:S(2)}) async-start(), calls=%async_computation.13 | async-start | bytes 163840 | tf_op jit(solution)/shard_map/reduce_scatter | solution.py:172
Sparse Core Ops, SparseCore 0:
  11.4 78.7 all-gather.4
  93.6 75.5 all-gather.6
  326.9 81.1 all-gather.8
  411.4 74.9 all-gather.10
  488.7 19.7 reduce-scatter.2
  511.0 22.6 reduce-scatter.4
where the time goes:
time: 546 us; the launch traced here: 542 us
  waiting for transfers between devices  288 us (53%)
  blocking collectives  90.5 us (17%)
  matrix products  67.5 us (12%)
  other arithmetic  38.5 us (7%)
  starting transfers between devices  23.5 us (4%)
  local copies, waits for them, and re-layouts  19.7 us (4%)
  between operations  14.3 us (3%)
    all_gather x2, waiting for transfers between devices, shards(): piece_rows = lax.all_gather(attended, 'leaf', axis=0, tiled=True)  107 us
    all_gather x2, waiting for transfers between devices, shards(): lax.all_gather(normed.reshape(owned_rows, heads_kv, group_size * HD), 'le...  91.9 us
    all_to_all x1, blocking collectives, shards(): lax.all_to_all(numerator.reshape(leaves, owned_rows, heads_kv, group_size...  55.3 us
    all_to_all x1, waiting for transfers between devices, shards(): lax.all_to_all(numerator.reshape(leaves, owned_rows, heads_kv, group_size...  44.2 us
    reduce_scatter x2, waiting for transfers between devices, shards(): lax.psum_scatter(head_terms, 'kv', scatter_dimension=0, tiled=True)  43.7 us
    dot_general x16, matrix products, shared_part(): jnp.einsum('rhgd,thd->rhgt', query_rows, shared_keys, preferred_element_t...  31.4 us
    dot_general x16, matrix products, shared_part(): jnp.einsum('rhgt,thd->rhgd', weights.astype(jnp.bfloat16), shared_values,...  25.8 us
    all_to_all x1, blocking collectives, shards(): lax.all_to_all(row_top.reshape(leaves, owned_rows, heads_kv, group_size),...  20.1 us
  transfers between devices with their start and end apart: 9, of which 7 were waited for; matrix products, arithmetic and copies ran while one was open for 22% of the time, Pallas kernels for 0%

commit v1 on v0

v1 whole, which is shorter than its diff:
```python
import functools
import math

import jax
import jax.numpy as jnp
from jax import lax
from jax.experimental import pallas as pl
from jax.experimental.pallas import tpu as pltpu
from jax.sharding import Mesh
from jax.sharding import PartitionSpec as P

HD = 128
GROUP = 16
BLK = 256
SUF = 512
STEPS = 2
OWN = 4
REQ_ROWS = STEPS * GROUP
PIECE = OWN * REQ_ROWS
STAT = 16
PACK = PIECE + STAT
NX, NZ = 4, 8
PIECES = NX * NZ
LOCAL = PIECES * OWN
SCALE = 1.0 / math.sqrt(HD)
EXP2 = SCALE * math.log2(math.e)
ITEM = 8
BATCH = 4
SLOTS = 16
VMEM = pl.BlockSpec(memory_space=pltpu.VMEM)
SMEM = pl.BlockSpec(memory_space=pltpu.SMEM)
ANY = pl.BlockSpec(memory_space=pl.ANY)
PARAMS = pltpu.CompilerParams(vmem_limit_bytes=44 * 1024 * 1024)
f32, bf16 = jnp.float32, jnp.bfloat16


def swap(a, axis, n, k):
    return lax.ppermute(a, axis, [(i, i ^ k) for i in range(n)])


def nt(a, b):
    return lax.dot_general(a, b, (((1,), (1,)), ((), ())), preferred_element_type=f32)


def nn(a, b):
    return jnp.dot(a, b, preferred_element_type=f32)


def diagonal():
    rows = lax.broadcasted_iota(jnp.int32, (PIECE, PIECE), 0)
    return rows == lax.broadcasted_iota(jnp.int32, (PIECE, PIECE), 1)


def to_lanes(column, diag):
    return jnp.sum(jnp.where(diag, column, 0.0), axis=0, keepdims=True)


def to_rows(lanes, diag):
    return jnp.sum(jnp.where(diag, lanes, 0.0), axis=1, keepdims=True)


def pack_lse(lanes):
    row = lax.broadcasted_iota(jnp.int32, (STAT, PIECE), 0)
    high = lanes.astype(bf16).astype(f32)
    middle = (lanes - high).astype(bf16).astype(f32)
    low = lanes - high - middle
    stat = jnp.where(row == 0, high, jnp.where(row == 1, middle, jnp.where(row == 2, low, 0.0)))
    return stat.astype(bf16)


def unpack_lse(stat):
    stat = stat.astype(f32)
    return stat[0:1] + stat[1:2] + stat[2:3]


def merge(parts, lses, diag):
    top = functools.reduce(jnp.maximum, lses)
    factors = [jnp.exp(lse - top) for lse in lses]
    total = functools.reduce(jnp.add, factors)
    out = 0.0
    for part, factor in zip(parts, factors):
        out = out + part() * to_rows(factor / total, diag)
    return out, top + jnp.log(total)


def norm_kernel(q_ref, gain_ref, out_ref):
    x = q_ref[...].astype(f32)
    mean_square = jnp.mean(x * x, axis=-1, keepdims=True)
    out_ref[...] = (x * lax.rsqrt(mean_square + 1e-06) * gain_ref[...]).astype(bf16)


def own_kernel(length_ref, q_ref, sk_ref, sv_ref, nk_ref, nv_ref, out_ref, lse_ref):
    q = q_ref[...]
    pad = jnp.zeros((PIECE - STEPS * OWN, HD), f32)
    new_keys = jnp.concatenate([nk_ref[...].astype(f32), pad], 0).astype(bf16)
    new_values = jnp.concatenate([nv_ref[...].astype(f32), pad], 0).astype(bf16)
    row = lax.broadcasted_iota(jnp.int32, (PIECE, PIECE), 0)
    token = lax.broadcasted_iota(jnp.int32, (PIECE, PIECE), 1)
    seen = (token < STEPS * OWN) & ((token & (OWN - 1)) == (row >> 5))
    seen = seen & ((token >> 2) <= ((row >> 4) & 1))
    new_scores = jnp.where(seen, nt(q, new_keys), -jnp.inf)
    position = lax.broadcasted_iota(jnp.int32, (REQ_ROWS, SUF), 1)
    outs, lses = [], []
    for i in range(OWN):
        rows = slice(i * REQ_ROWS, (i + 1) * REQ_ROWS)
        scores = jnp.where(position < length_ref[i], nt(q[rows], sk_ref[i]), -jnp.inf)
        fresh = new_scores[rows]
        top = jnp.maximum(
            jnp.max(scores, axis=1, keepdims=True), jnp.max(fresh, axis=1, keepdims=True)
        )
        weights = jnp.exp2((scores - top) * EXP2)
        fresh_weights = jnp.exp2((fresh - top) * EXP2)
        total = jnp.sum(weights, axis=1, keepdims=True) + jnp.sum(
            fresh_weights, axis=1, keepdims=True
        )
        out = nn(weights.astype(bf16), sv_ref[i]) + nn(fresh_weights.astype(bf16), new_values)
        outs.append(out / total)
        lses.append(top * SCALE + jnp.log(total))
    out_ref[...] = jnp.concatenate(outs, 0)
    lse = to_lanes(jnp.concatenate(lses, 0), diagonal())
    lse_ref[...] = jnp.broadcast_to(lse, lse_ref.shape)


def shared_kernel(
    meta_ref, q0, q1, q2, q3, rk0, rk1, rv0, rv1, bk0, bk1, bv0, bv1,
    out0, out1, out2, out3,
    item_block, item_part, bk, bv, q_all, acc, top_all, sum_all, part, part_top, part_sum, sems,
):
    half = bk.shape[0] // 2
    copies = []
    for n, (src, dst) in enumerate(((bk0, bk), (bk1, bk), (bv0, bv), (bv1, bv))):
        copies.append(
            pltpu.make_async_copy(src, dst.at[pl.ds((n % 2) * half, half)], sems.at[n])
        )
    for copy in copies:
        copy.start()

    def list_block(j, n):
        parts = (meta_ref[LOCAL + j] + (ITEM - 1)) >> 3

        def put(k, carry):
            item_block[n + k] = j
            item_part[n + k] = k
            return carry

        lax.fori_loop(0, parts, put, 0)
        return n + parts

    items = lax.fori_loop(0, SLOTS, list_block, 0)
    for u in range(BATCH - 1):
        item_block[items + u] = 0
        item_part[items + u] = LOCAL

    q_all[pl.ds(LOCAL * REQ_ROWS, REQ_ROWS), :] = jnp.zeros((REQ_ROWS, HD), bf16)
    acc[pl.ds(LOCAL * REQ_ROWS, REQ_ROWS), :] = jnp.zeros((REQ_ROWS, HD), f32)
    top_all[pl.ds(LOCAL * REQ_ROWS, REQ_ROWS), :] = jnp.zeros((REQ_ROWS, HD), f32)
    sum_all[pl.ds(LOCAL * REQ_ROWS, REQ_ROWS), :] = jnp.ones((REQ_ROWS, HD), f32)

    tile = 256
    quarter = NZ * PIECE
    for g, q_ref in enumerate((q0, q1, q2, q3)):

        def root_tile(t, carry):
            q = q_ref[pl.ds(pl.multiple_of(t * tile, tile), tile), :]
            rows = pl.ds(pl.multiple_of(g * quarter + t * tile, tile), tile)
            q_all[rows, :] = q
            s0 = nt(q, rk0[...])
            s1 = nt(q, rk1[...])
            top = jnp.max(jnp.maximum(s0, s1), axis=1, keepdims=True)
            w0 = jnp.exp2((s0 - top) * EXP2)
            w1 = jnp.exp2((s1 - top) * EXP2)
            total = jnp.sum(w0 + w1, axis=1, keepdims=True)
            acc[rows, :] = nn(w0.astype(bf16), rv0[...]) + nn(w1.astype(bf16), rv1[...])
            top_all[rows, :] = jnp.broadcast_to(top, (tile, HD))
            sum_all[rows, :] = jnp.broadcast_to(total, (tile, HD))
            return carry

        lax.fori_loop(0, quarter // tile, root_tile, 0, unroll=2)

    for copy in copies:
        copy.wait()

    def request_rows(block, index):
        place = meta_ref[LOCAL + SLOTS + block] + index
        found = meta_ref[jnp.minimum(place, LOCAL - 1)]
        request = jnp.where(index < meta_ref[LOCAL + block], found, LOCAL)
        return pl.ds(pl.multiple_of(request * REQ_ROWS, REQ_ROWS), REQ_ROWS)

    def batch(b, carry):
        places = []
        for u in range(BATCH):
            block = item_block[b * BATCH + u]
            first = item_part[b * BATCH + u] * ITEM
            rows = [request_rows(block, first + e) for e in range(ITEM)]
            tokens = pl.ds(pl.multiple_of(block * BLK, BLK), BLK)
            q = jnp.concatenate([q_all[r, :] for r in rows], 0)
            scores = nt(q, bk[tokens, :])
            top = jnp.max(scores, axis=1, keepdims=True)
            weights = jnp.exp2((scores - top) * EXP2)
            total = jnp.sum(weights, axis=1, keepdims=True)
            part[u] = nn(weights.astype(bf16), bv[tokens, :])
            part_top[u] = jnp.broadcast_to(top, (ITEM * REQ_ROWS, HD))
            part_sum[u] = jnp.broadcast_to(total, (ITEM * REQ_ROWS, HD))
            places.append(rows)
        for u in range(BATCH):
            rows = places[u]
            old_top = jnp.concatenate([top_all[r, :] for r in rows], 0)
            old_sum = jnp.concatenate([sum_all[r, :] for r in rows], 0)
            old_acc = jnp.concatenate([acc[r, :] for r in rows], 0)
            top = jnp.maximum(old_top, part_top[u])
            keep = jnp.exp2((old_top - top) * EXP2)
            add = jnp.exp2((part_top[u] - top) * EXP2)
            new_sum = old_sum * keep + part_sum[u] * add
            new_acc = old_acc * keep + part[u] * add
            for e, r in enumerate(rows):
                piece = slice(e * REQ_ROWS, (e + 1) * REQ_ROWS)
                top_all[r, :] = top[piece]
                sum_all[r, :] = new_sum[piece]
                acc[r, :] = new_acc[piece]
        return carry

    lax.fori_loop(0, (items + BATCH - 1) >> 2, batch, 0)

    diag = diagonal()
    for g, out in enumerate((out0, out1, out2, out3)):

        def finish(n, carry):
            rows = pl.ds(pl.multiple_of(g * quarter + n * PIECE, PIECE), PIECE)
            total = sum_all[rows, :]
            start = pl.multiple_of(n * PACK, 16)
            out[pl.ds(start, PIECE), :] = (acc[rows, :] / total).astype(bf16)
            lse = top_all[rows, :] * SCALE + jnp.log(total)
            out[pl.ds(start + PIECE, STAT), :] = pack_lse(to_lanes(lse, diag))
            return carry

        lax.fori_loop(0, NZ, finish, 0, unroll=2)


def merge_kernel(a, b, c, d, *outs):
    diag = diagonal()
    refs = (a, b, c, d)
    for n, out in enumerate(outs):
        body = slice(n * PACK, n * PACK + PIECE)
        stat = slice(n * PACK + PIECE, (n + 1) * PACK)
        merged, lse = merge(
            [lambda ref=ref: ref[body, :].astype(f32) for ref in refs],
            [unpack_lse(ref[stat, :]) for ref in refs],
            diag,
        )
        out[0:PIECE, :] = merged.astype(bf16)
        out[PIECE:PACK, :] = pack_lse(lse)


def final_kernel(*refs):
    parts, (own, own_lse, attn, attn_low, lse_out, rows) = refs[:NZ], refs[NZ:]
    diag = diagonal()
    merged, lse = merge(
        [lambda ref=ref: ref[0:PIECE, :].astype(f32) for ref in parts] + [lambda: own[...]],
        [unpack_lse(ref[PIECE:PACK, :]) for ref in parts] + [own_lse[0:1, :]],
        diag,
    )
    rows[...] = merged
    lse_out[...] = jnp.broadcast_to(lse, lse_out.shape)
    for s in range(STEPS):
        for h in range(GROUP):
            attn[s * OWN:(s + 1) * OWN, h * HD:(h + 1) * HD] = rows[
                pl.ds(s * GROUP + h, OWN, stride=REQ_ROWS), :
            ]
    attn_low[...] = attn[...].astype(bf16)


def project_kernel(where_ref, *refs):
    rows, weights, outs, terms = refs[:2 * NZ], refs[2 * NZ:2 * NZ + NX], refs[2 * NZ + NX:-1], refs[-1]
    left = jnp.concatenate([r[...].astype(f32) for r in rows], 0).astype(bf16)
    depth = left.shape[1] // 2
    for n, weight in enumerate(weights):
        low = nn(left[:, :depth], weight[...])
        high = nn(left[:, depth:], weight[...])
        columns = low.shape[1] // 2
        term = low[:, :columns] + high[:, columns:]
        count = term.shape[0] // 2
        terms[n] = jnp.concatenate([term[:count], term[count:]], 1)
    for n, out in enumerate(outs):
        out[...] = terms[where_ref[0] ^ n]


def gather_kernel(where_ref, a, b, c, d, out):
    total = a[...] + b[...] + c[...] + d[...]
    columns = out.shape[2]
    first = where_ref[1] == 0
    for n in range(NZ):
        for s in range(STEPS):
            rows = slice(n * STEPS * OWN + s * OWN, n * STEPS * OWN + (s + 1) * OWN)
            mine, other = total[rows, :columns], total[rows, columns:]
            pair = jnp.concatenate(
                [jnp.where(first, mine, other), jnp.where(first, other, mine)], 0
            )
            place = pl.multiple_of((where_ref[0] ^ n) * 2 * OWN, 2 * OWN)
            out[s, pl.ds(place, 2 * OWN), :] = pair


def plan(request_branch, branch_blocks, block_slot, x, z, core):
    leaf = (x * NZ + z) * 2 + core
    here = SLOTS // 2
    block_ids = jnp.arange(block_slot.shape[0], dtype=jnp.int32)
    offsets = jnp.arange(here, dtype=jnp.int32)
    slot_ids = jnp.concatenate([leaf * here + offsets, (leaf ^ 1) * here + offsets])
    slot_block = jnp.sum(
        jnp.where(block_slot[:, None] == slot_ids[None, :], block_ids[:, None], 0), axis=0
    )
    cum_end = jnp.cumsum(branch_blocks)
    slot_branch = jnp.sum((cum_end[None, :] <= slot_block[:, None]).astype(jnp.int32), axis=1)
    n = jnp.arange(LOCAL, dtype=jnp.int32)
    owner = ((x ^ (n >> 5)) * NZ + (z ^ ((n >> 2) & (NZ - 1)))) * 2 + core
    request = owner * OWN + (n & (OWN - 1))
    every = jnp.arange(request_branch.shape[0], dtype=jnp.int32)
    branch = jnp.sum(jnp.where(request[:, None] == every[None, :], request_branch[None, :], 0), 1)
    before = (branch[None, :] < branch[:, None]) | (
        (branch[None, :] == branch[:, None]) & (n[None, :] < n[:, None])
    )
    rank = jnp.sum(before.astype(jnp.int32), axis=1)
    ordered = jnp.sum(jnp.where(rank[:, None] == n[None, :], n[:, None], 0), axis=0)
    count = jnp.sum((slot_branch[:, None] == branch[None, :]).astype(jnp.int32), axis=1)
    start = jnp.sum((branch[None, :] < slot_branch[:, None]).astype(jnp.int32), axis=1)
    return jnp.concatenate([ordered, count, start]).astype(jnp.int32)


def struct(shape, dtype):
    return jax.ShapeDtypeStruct(shape, dtype)


def shards(
    queries,
    query_gain,
    new_keys,
    new_values,
    root_keys,
    root_values,
    branch_keys,
    branch_values,
    suffix_keys,
    suffix_values,
    out_weight,
    request_branch,
    branch_blocks,
    suffix_length,
    block_slot,
):
    kv, x, z, core = (lax.axis_index(name) for name in ("kv", "x", "z", "core"))
    raw = queries.reshape(STEPS, OWN, GROUP, HD).transpose(1, 0, 2, 3).reshape(PIECE, HD)
    normed = pl.pallas_call(
        norm_kernel, out_shape=struct((PIECE, HD), bf16), in_specs=[VMEM, VMEM], out_specs=VMEM
    )(raw, query_gain.reshape(1, HD))
    near = jnp.concatenate([normed] + [swap(normed, "z", NZ, k) for k in range(1, NZ)], 0)
    quarters = [near] + [swap(near, "x", NX, k) for k in range(1, NX)]

    shared = []
    for a in (root_keys, root_values, branch_keys, branch_values):
        flat = a.reshape(a.shape[0], HD)
        shared += [flat, swap(flat, "core", 2, 1)]
    depth = out_weight.shape[0] // 2
    folded = jnp.concatenate([out_weight[:depth], out_weight[depth:]], 1)
    weights = [folded] + [swap(folded, "x", NX, k) for k in range(1, NX)]
    meta = plan(request_branch, branch_blocks, block_slot, x, z, core)

    own, own_lse = pl.pallas_call(
        own_kernel,
        out_shape=[struct((PIECE, HD), f32), struct((8, PIECE), f32)],
        in_specs=[SMEM] + [VMEM] * 5,
        out_specs=[VMEM, VMEM],
        compiler_params=PARAMS,
    )(
        suffix_length,
        normed,
        suffix_keys.reshape(OWN, SUF, HD),
        suffix_values.reshape(OWN, SUF, HD),
        new_keys.reshape(STEPS * OWN, HD),
        new_values.reshape(STEPS * OWN, HD),
    )

    rows = LOCAL * REQ_ROWS
    spare = rows + REQ_ROWS
    branch_rows = SLOTS * BLK
    partials = pl.pallas_call(
        shared_kernel,
        out_shape=[struct((NZ * PACK, HD), bf16)] * NX,
        in_specs=[SMEM] + [VMEM] * 8 + [ANY] * 4,
        out_specs=[VMEM] * NX,
        scratch_shapes=[
            pltpu.SMEM((SLOTS * LOCAL // ITEM + BATCH,), jnp.int32),
            pltpu.SMEM((SLOTS * LOCAL // ITEM + BATCH,), jnp.int32),
            pltpu.VMEM((branch_rows, HD), bf16),
            pltpu.VMEM((branch_rows, HD), bf16),
            pltpu.VMEM((spare, HD), bf16),
            pltpu.VMEM((spare, HD), f32),
            pltpu.VMEM((spare, HD), f32),
            pltpu.VMEM((spare, HD), f32),
            pltpu.VMEM((BATCH, ITEM * REQ_ROWS, HD), f32),
            pltpu.VMEM((BATCH, ITEM * REQ_ROWS, HD), f32),
            pltpu.VMEM((BATCH, ITEM * REQ_ROWS, HD), f32),
            pltpu.SemaphoreType.DMA((4,)),
        ],
        compiler_params=PARAMS,
        cost_estimate=pl.CostEstimate(
            flops=4 * rows * HD * 2048, bytes_accessed=6 << 20, transcendentals=rows * 2048
        ),
    )(meta, *quarters, *shared)

    returned = [partials[0]] + [swap(partials[k], "x", NX, k) for k in range(1, NX)]
    merged = pl.pallas_call(
        merge_kernel,
        out_shape=[struct((PACK, HD), bf16)] * NZ,
        in_specs=[VMEM] * NX,
        out_specs=[VMEM] * NZ,
        compiler_params=PARAMS,
    )(*returned)
    landed = [merged[0]] + [swap(merged[k], "z", NZ, k) for k in range(1, NZ)]
    attn, attn_low, lse = pl.pallas_call(
        final_kernel,
        out_shape=[
            struct((STEPS * OWN, GROUP * HD), f32),
            struct((STEPS * OWN, GROUP * HD), bf16),
            struct((8, PIECE), f32),
        ],
        in_specs=[VMEM] * (NZ + 2),
        out_specs=[VMEM] * 3,
        scratch_shapes=[pltpu.VMEM((PIECE, HD), f32)],
        compiler_params=PARAMS,
    )(*landed, own, own_lse)
    attn_out = attn.reshape(STEPS, OWN, 1, GROUP * HD)
    log_total = lse[0].reshape(OWN, STEPS, GROUP).transpose(1, 0, 2).reshape(STEPS, OWN, 1, GROUP)

    held = [attn_low] + [swap(attn_low, "z", NZ, k) for k in range(1, NZ)]
    stacked = jnp.stack(held)
    across = swap(stacked, "core", 2, 1)
    columns = out_weight.shape[1]
    term = struct((NZ * STEPS * OWN, 2 * columns), f32)
    terms = pl.pallas_call(
        project_kernel,
        out_shape=[term] * NX,
        in_specs=[SMEM] + [VMEM] * (2 * NZ + NX),
        out_specs=[VMEM] * NX,
        scratch_shapes=[pltpu.VMEM((NX,) + term.shape, f32)],
        compiler_params=PARAMS,
    )((x ^ kv).reshape(1), *held, *[across[k] for k in range(NZ)], *weights)
    arrived = []
    for k in range(NX):
        pairs = [(v * NX + c, c * NX + (v ^ k)) for v in range(NX) for c in range(NX)]
        arrived.append(lax.ppermute(terms[k], ("kv", "x"), pairs))
    layer_out = pl.pallas_call(
        gather_kernel,
        out_shape=struct((STEPS, NZ * 2 * OWN, columns), f32),
        in_specs=[SMEM] + [VMEM] * NX,
        out_specs=VMEM,
        compiler_params=PARAMS,
    )(jnp.stack([z, core]), *arrived)
    return attn_out, log_total, layer_out


def solution(mesh):
    fine = Mesh(mesh.devices.reshape(4, NX, NZ, 2), ("kv", "x", "z", "core"))
    leaf = ("x", "z", "core")
    in_specs = (
        P(None, leaf, "kv", None),
        P(),
        P(None, leaf, "kv", None),
        P(None, leaf, "kv", None),
        P(leaf, "kv", None),
        P(leaf, "kv", None),
        P(leaf, "kv", None),
        P(leaf, "kv", None),
        P(leaf, None, "kv", None),
        P(leaf, None, "kv", None),
        P("kv", leaf),
        P(),
        P(),
        P(leaf),
        P(),
    )
    out_specs = (P(None, leaf, "kv", None), P(None, leaf, "kv", None), P(None, "kv", leaf))
    return jax.shard_map(shards, mesh=fine, in_specs=in_specs, out_specs=out_specs, check_vma=False)
```

time: 546 us -> 152 us (0.28)
  waiting for transfers between devices: 288 us -> 51 us
  blocking collectives: 90.5 us -> 0 us
  matrix products: 67.5 us -> 0 us
  starting transfers between devices: 23.5 us -> 69.4 us
  other arithmetic: 38.5 us -> 1.55 us
  Pallas kernels: 0 us -> 23.1 us
  between operations: 14.3 us -> 0.99 us
  local copies, waits for them, and re-layouts: 19.7 us -> 6.65 us
    all_gather x4 -> x0, waiting for transfers between devices: 199 us -> none  [the longest x2 107 us: shards(): piece_rows = lax.all_gather(attended, 'leaf', axis=0, tiled=True)]
    all_to_all x3 -> x0, blocking collectives: 90.5 us -> none  [the longest x1 55.3 us: shards(): lax.all_to_all(numerator.reshape(leaves, owned_rows, heads_kv, group_size...]
    ppermute x0 -> x39, starting transfers between devices: none -> 69.4 us  [the longest x35 60.5 us: swap(): return lax.ppermute(a, axis, [(i, i ^ k) for i in range(n)])]
    dot_general x38 -> x0, matrix products: 67.5 us -> none  [the longest x16 31.4 us: shared_part(): jnp.einsum('rhgd,thd->rhgt', query_rows, shared_keys, preferred_element_t...]
    ppermute x0 -> x39, waiting for transfers between devices: none -> 51 us  [the longest x35 46.1 us: swap(): return lax.ppermute(a, axis, [(i, i ^ k) for i in range(n)])]
    all_to_all x3 -> x0, waiting for transfers between devices: 44.2 us -> none  [the longest x1 44.2 us: shards(): lax.all_to_all(numerator.reshape(leaves, owned_rows, heads_kv, group_size...]
    reduce_scatter x2 -> x0, waiting for transfers between devices: 43.7 us -> none  [shards(): lax.psum_scatter(head_terms, 'kv', scatter_dimension=0, tiled=True)]
    all_to_all x3 -> x0, starting transfers between devices: 23.2 us -> none  [the longest x1 7.83 us: shards(): lax.all_to_all(row_top.reshape(leaves, owned_rows, heads_kv, group_size),...]
  transfers between devices with their start and end apart: 9 -> 39, of which waited for: 7 -> 15; matrix products, arithmetic and copies ran while one was open for 22% -> 2% of each run, Pallas kernels for 0% -> 1%
where the time goes in v1:
time: 152 us; the launch traced here: 153 us
  starting transfers between devices  69.4 us (46%)
  waiting for transfers between devices  51 us (34%)
  Pallas kernels  23.1 us (15%)
  local copies, waits for them, and re-layouts  6.65 us (4%)
  other arithmetic  1.55 us (1%)
    ppermute x35, starting transfers between devices, swap(): return lax.ppermute(a, axis, [(i, i ^ k) for i in range(n)])  60.5 us
    ppermute x35, waiting for transfers between devices, swap(): return lax.ppermute(a, axis, [(i, i ^ k) for i in range(n)])  46.1 us
    pallas_call x1, Pallas kernels, shards(): pl.pallas_call(shared_kernel, out_shape=[struct((NZ * PACK, HD), bf16)] *...  16.7 us
    ppermute x4, starting transfers between devices, shards(): arrived.append(lax.ppermute(terms[k], ('kv', 'x'), pairs))  8.99 us
    ppermute x4, waiting for transfers between devices, shards(): arrived.append(lax.ppermute(terms[k], ('kv', 'x'), pairs))  4.89 us
    unnamed x45, local copies, waits for them, and re-layouts  4.3 us
  transfers between devices with their start and end apart: 39, of which 15 were waited for; matrix products, arithmetic and copies ran while one was open for 2% of the time, Pallas kernels for 1%

profile of v1, /device:TPU:40, one launch (start us, length us, event | category | flops | bytes accessed | tf_op | source)
XLA Modules:
  0.0 152.8 jit_solution(7819001573392270584)
XLA Ops:
  0.6 0.8 reshape.99
  2.0 1.5 shard_map.166.q_ref
  3.6 3.3 %collective-permute-start.1 = (bf16[128,128]{1,0:T(8,128)(2,1)}, bf16[128,128]{1,0:T(8,128)(2,1)S(1)}, u32[]{:S(2)}, u32[]{:S(2)}) collective-permute-start(bf16[128,128]{1,0:T(8,128)(2,1)} %shard_map.166.q_ref), channel_id=1, source_target_pairs={{0,4},{2,6},{4,0},{6,2},{8,12},{10,14},{12,8},{14,10},{1,5},{3,7},... | collective-permute-start | bytes 98312 | tf_op jit(solution)/shard_map/ppermute | solution.py:38
  7.4 5.9 %collective-permute-start.3 = (bf16[128,128]{1,0:T(8,128)(2,1)}, bf16[128,128]{1,0:T(8,128)(2,1)S(1)}, u32[]{:S(2)}, u32[]{:S(2)}) collective-permute-start(bf16[128,128]{1,0:T(8,128)(2,1)} %shard_map.166.q_ref), channel_id=1, source_target_pairs={{0,8},{2,10},{4,12},{6,14},{8,0},{10,2},{12,4},{14,6},{1,9},{3,11}... | collective-permute-start | bytes 98312 | tf_op jit(solution)/shard_map/ppermute | solution.py:38
  15.5 4.2 %collective-permute-start.5 = (bf16[128,128]{1,0:T(8,128)(2,1)S(1)}, bf16[128,128]{1,0:T(8,128)(2,1)S(1)}, u32[]{:S(2)}, u32[]{:S(2)}) collective-permute-start(bf16[128,128]{1,0:T(8,128)(2,1)S(1)} %copy-done.2), channel_id=1, source_target_pairs={{0,12},{2,14},{4,8},{6,10},{8,4},{10,6},{12,0},{14,2},{1,13},{3,15... | collective-permute-start | bytes 98312 | tf_op jit(solution)/shard_map/ppermute | solution.py:38
  19.7 1.5 collective-permute-start.6
  22.7 4.1 %collective-permute-done.6 = bf16[128,128]{1,0:T(8,128)(2,1)S(1)} collective-permute-done((bf16[128,128]{1,0:T(8,128)(2,1)S(1)}, bf16[128,128]{1,0:T(8,128)(2,1)S(1)}, u32[]{:S(2)}, u32[]{:S(2)}) %collective-permute-start.6) | collective-permute-done | bytes 32800 | tf_op jit(solution)/shard_map/ppermute | solution.py:38
  26.8 1.5 collective-permute-start.7
  28.3 2.7 %collective-permute-start.8 = (bf16[1024,128]{1,0:T(8,128)(2,1)S(1)}, bf16[1024,128]{1,0:T(8,128)(2,1)S(1)}, u32[]{:S(2)}, u32[]{:S(2)}) collective-permute-start(bf16[1024,128]{1,0:T(8,128)(2,1)S(1)} %constant_dynamic-update-slice_fusion.q0), channel_id=1, source_target_pairs={{0,32},{16,48},{32,0},{48,16},{1,33},{17,49},{33,1},{49,17},{2,34}... | collective-permute-start | bytes 786440 | tf_op jit(solution)/shard_map/ppermute | solution.py:38
  31.8 3.0 %collective-permute-done.7.q1 = bf16[1024,128]{1,0:T(8,128)(2,1)S(1)} collective-permute-done((bf16[1024,128]{1,0:T(8,128)(2,1)S(1)}, bf16[1024,128]{1,0:T(8,128)(2,1)S(1)}, u32[]{:S(2)}, u32[]{:S(2)}) %collective-permute-start.7) | collective-permute-done | bytes 262176 | tf_op jit(solution)/shard_map/ppermute | solution.py:38
  34.8 5.1 %collective-permute-done.8.q2 = bf16[1024,128]{1,0:T(8,128)(2,1)S(1)} collective-permute-done((bf16[1024,128]{1,0:T(8,128)(2,1)S(1)}, bf16[1024,128]{1,0:T(8,128)(2,1)S(1)}, u32[]{:S(2)}, u32[]{:S(2)}) %collective-permute-start.8) | collective-permute-done | bytes 262176 | tf_op jit(solution)/shard_map/ppermute | solution.py:38
  39.9 2.5 %collective-permute-done.9.q3 = bf16[1024,128]{1,0:T(8,128)(2,1)S(1)} collective-permute-done((bf16[1024,128]{1,0:T(8,128)(2,1)S(1)}, bf16[1024,128]{1,0:T(8,128)(2,1)S(1)}, u32[]{:S(2)}, u32[]{:S(2)}) %collective-permute-start.9) | collective-permute-done | bytes 262176 | tf_op jit(solution)/shard_map/ppermute | solution.py:38
  42.5 1.0 copy-done.7
  43.5 0.9 copy-done.9
  44.4 16.7 %shard_map.167 = (bf16[1152,128]{1,0:T(8,128)(2,1)S(1)}, bf16[1152,128]{1,0:T(8,128)(2,1)S(1)}, bf16[1152,128]{1,0:T(8,128)(2,1)S(1)}, bf16[1152,128]{1,0:T(8,128)(2,1)S(1)}) custom-call(s32[160]{0:T(256)S(1)} %pad_add_fusion.meta_ref, bf16[1024,128]{1,0:T(8,128)(2,1)S(1)} %constant_dynamic-update-slice_fusion.q0, ...), custom_call_target="tpu_custom_call" | custom-call | flops 4294967296 | bytes 6291456 | tf_op jit(solution)/shard_map/pallas_call | solution.py:384
  61.3 1.6 %collective-permute-start.15 = (bf16[1152,128]{1,0:T(8,128)(2,1)S(1)}, bf16[1152,128]{1,0:T(8,128)(2,1)S(1)}, u32[]{:S(2)}, u32[]{:S(2)}) collective-permute-start(bf16[1152,128]{1,0:T(8,128)(2,1)S(1)} %get-tuple-element.26), channel_id=1, source_target_pairs={{0,32},{16,48},{32,0},{48,16},{1,33},{17,49},{33,1},{49,17},{2,34}... | collective-permute-start | bytes 884744 | tf_op jit(solution)/shard_map/ppermute | solution.py:38
  62.9 3.1 %collective-permute-start.16 = (bf16[1152,128]{1,0:T(8,128)(2,1)S(1)}, bf16[1152,128]{1,0:T(8,128)(2,1)S(1)}, u32[]{:S(2)}, u32[]{:S(2)}) collective-permute-start(bf16[1152,128]{1,0:T(8,128)(2,1)S(1)} %get-tuple-element.27), channel_id=1, source_target_pairs={{0,48},{16,32},{32,16},{48,0},{1,49},{17,33},{33,17},{49,1},{2,50}... | collective-permute-start | bytes 884744 | tf_op jit(solution)/shard_map/ppermute | solution.py:38
  66.0 5.2 %collective-permute-done.14.b = bf16[1152,128]{1,0:T(8,128)(2,1)S(1)} collective-permute-done((bf16[1152,128]{1,0:T(8,128)(2,1)S(1)}, bf16[1152,128]{1,0:T(8,128)(2,1)S(1)}, u32[]{:S(2)}, u32[]{:S(2)}) %collective-permute-start.14) | collective-permute-done | bytes 294944 | tf_op jit(solution)/shard_map/ppermute | solution.py:38
  71.2 2.1 %collective-permute-done.15.c = bf16[1152,128]{1,0:T(8,128)(2,1)S(1)} collective-permute-done((bf16[1152,128]{1,0:T(8,128)(2,1)S(1)}, bf16[1152,128]{1,0:T(8,128)(2,1)S(1)}, u32[]{:S(2)}, u32[]{:S(2)}) %collective-permute-start.15) | collective-permute-done | bytes 294944 | tf_op jit(solution)/shard_map/ppermute | solution.py:38
  73.3 3.2 %collective-permute-done.16.d = bf16[1152,128]{1,0:T(8,128)(2,1)S(1)} collective-permute-done((bf16[1152,128]{1,0:T(8,128)(2,1)S(1)}, bf16[1152,128]{1,0:T(8,128)(2,1)S(1)}, u32[]{:S(2)}, u32[]{:S(2)}) %collective-permute-start.16) | collective-permute-done | bytes 294944 | tf_op jit(solution)/shard_map/ppermute | solution.py:38
  76.5 0.7 shard_map.168
  77.2 1.8 %collective-permute-start.17 = (bf16[144,128]{1,0:T(8,128)(2,1)S(1)}, bf16[144,128]{1,0:T(8,128)(2,1)S(1)}, u32[]{:S(2)}, u32[]{:S(2)}) collective-permute-start(bf16[144,128]{1,0:T(8,128)(2,1)S(1)} %get-tuple-element.29), channel_id=1, source_target_pairs={{0,2},{2,0},{4,6},{6,4},{8,10},{10,8},{12,14},{14,12},{1,3},{3,1},... | collective-permute-start | bytes 110600 | tf_op jit(solution)/shard_map/ppermute | solution.py:38
  79.0 1.2 collective-permute-start.18
  80.2 0.6 collective-permute-start.19
  80.8 5.3 %collective-permute-start.20 = (bf16[144,128]{1,0:T(8,128)(2,1)S(1)}, bf16[144,128]{1,0:T(8,128)(2,1)S(1)}, u32[]{:S(2)}, u32[]{:S(2)}) collective-permute-start(bf16[144,128]{1,0:T(8,128)(2,1)S(1)} %get-tuple-element.32), channel_id=1, source_target_pairs={{0,8},{2,10},{4,12},{6,14},{8,0},{10,2},{12,4},{14,6},{1,9},{3,11}... | collective-permute-start | bytes 110600 | tf_op jit(solution)/shard_map/ppermute | solution.py:38
  86.1 1.7 %collective-permute-start.21 = (bf16[144,128]{1,0:T(8,128)(2,1)S(1)}, bf16[144,128]{1,0:T(8,128)(2,1)S(1)}, u32[]{:S(2)}, u32[]{:S(2)}) collective-permute-start(bf16[144,128]{1,0:T(8,128)(2,1)S(1)} %get-tuple-element.33), channel_id=1, source_target_pairs={{0,10},{2,8},{4,14},{6,12},{8,2},{10,0},{12,6},{14,4},{1,11},{3,9}... | collective-permute-start | bytes 110600 | tf_op jit(solution)/shard_map/ppermute | solution.py:38
  87.8 3.7 %collective-permute-start.22 = (bf16[144,128]{1,0:T(8,128)(2,1)S(1)}, bf16[144,128]{1,0:T(8,128)(2,1)S(1)}, u32[]{:S(2)}, u32[]{:S(2)}) collective-permute-start(bf16[144,128]{1,0:T(8,128)(2,1)S(1)} %get-tuple-element.34), channel_id=1, source_target_pairs={{0,12},{2,14},{4,8},{6,10},{8,4},{10,6},{12,0},{14,2},{1,13},{3,15... | collective-permute-start | bytes 110600 | tf_op jit(solution)/shard_map/ppermute | solution.py:38
  91.5 0.8 collective-permute-start.23
  92.3 0.7 copy-done.4
  93.0 1.8 %shard_map.169 = (f32[128,128]{1,0:T(8,128)S(1)}, f32[8,128]{1,0:T(8,128)S(1)}) custom-call(s32[4]{0:T(128)S(1)} %copy-done.5, bf16[128,128]{1,0:T(8,128)(2,1)S(1)} %copy-done.2, bf16[4,512,128]{2,1,0:T(8,128)(2,1)S(1)} %bitcast.53, bf16[4,512,128]{2,1,0:T(8,128)(2,1)S(1)} %bitcast.54, bf16[8,128]{1,0:T(8,128)(2,1)S(1)} %bitcast.55, bf16[8,128]{1,0:T(8,128)(2,1)S(1)} %bitcast.56), custom_call_target="tpu_custom_call" | custom-call | tf_op jit(solution)/shard_map/pallas_call | solution.py:366
  94.8 3.8 %collective-permute-done.23.refs_7_ = bf16[144,128]{1,0:T(8,128)(2,1)S(1)} collective-permute-done((bf16[144,128]{1,0:T(8,128)(2,1)S(1)}, bf16[144,128]{1,0:T(8,128)(2,1)S(1)}, u32[]{:S(2)}, u32[]{:S(2)}) %collective-permute-start.23) | collective-permute-done | bytes 36896 | tf_op jit(solution)/shard_map/ppermute | solution.py:38
  99.3 1.5 collective-permute-start.25
  100.8 2.0 %collective-permute-start.26 = (bf16[8,2048]{1,0:T(8,128)(2,1)S(1)}, bf16[8,2048]{1,0:T(8,128)(2,1)S(1)}, u32[]{:S(2)}, u32[]{:S(2)}) collective-permute-start(bf16[8,2048]{1,0:T(8,128)(2,1)S(1)} %get-tuple-element.40.refs_0_), channel_id=1, source_target_pairs={{0,6},{2,4},{4,2},{6,0},{8,14},{10,12},{12,10},{14,8},{1,7},{3,5},... | collective-permute-start | bytes 98312 | tf_op jit(solution)/shard_map/ppermute | solution.py:38
  102.7 1.6 %collective-permute-start.27 = (bf16[8,2048]{1,0:T(8,128)(2,1)S(1)}, bf16[8,2048]{1,0:T(8,128)(2,1)S(1)}, u32[]{:S(2)}, u32[]{:S(2)}) collective-permute-start(bf16[8,2048]{1,0:T(8,128)(2,1)S(1)} %get-tuple-element.40.refs_0_), channel_id=1, source_target_pairs={{0,8},{2,10},{4,12},{6,14},{8,0},{10,2},{12,4},{14,6},{1,9},{3,11}... | collective-permute-start | bytes 98312 | tf_op jit(solution)/shard_map/ppermute | solution.py:38
  104.4 3.9 %collective-permute-start.28 = (bf16[8,2048]{1,0:T(8,128)(2,1)S(1)}, bf16[8,2048]{1,0:T(8,128)(2,1)S(1)}, u32[]{:S(2)}, u32[]{:S(2)}) collective-permute-start(bf16[8,2048]{1,0:T(8,128)(2,1)S(1)} %get-tuple-element.40.refs_0_), channel_id=1, source_target_pairs={{0,10},{2,8},{4,14},{6,12},{8,2},{10,0},{12,6},{14,4},{1,11},{3,9}... | collective-permute-start | bytes 98312 | tf_op jit(solution)/shard_map/ppermute | solution.py:38
  108.5 4.3 %collective-permute-start.30 = (bf16[8,2048]{1,0:T(8,128)(2,1)S(1)}, bf16[8,2048]{1,0:T(8,128)(2,1)S(1)}, u32[]{:S(2)}, u32[]{:S(2)}) collective-permute-start(bf16[8,2048]{1,0:T(8,128)(2,1)S(1)} %get-tuple-element.40.refs_0_), channel_id=1, source_target_pairs={{0,14},{2,12},{4,10},{6,8},{8,6},{10,4},{12,2},{14,0},{1,15},{3,13... | collective-permute-start | bytes 98312 | tf_op jit(solution)/shard_map/ppermute | solution.py:38
  112.9 1.4 collective-permute-done.29.refs_6_
  114.3 1.2 collective-permute-done.30.refs_7_
  116.1 4.2 %collective-permute-start.33 = (bf16[1024,128]{1,0:T(8,128)(2,1)S(1)}, bf16[1024,128]{1,0:T(8,128)(2,1)S(1)}, u32[]{:S(2)}, u32[]{:S(2)}) collective-permute-start(bf16[1024,128]{1,0:T(8,128)(2,1)S(1)} %pad_maximum_fusion.refs_16_), channel_id=1, source_target_pairs={{0,32},{16,48},{32,0},{48,16},{1,33},{17,49},{33,1},{49,17},{2,34}... | collective-permute-start | bytes 786440 | tf_op jit(solution)/shard_map/ppermute | solution.py:38
  120.9 4.3 %collective-permute-done.32.refs_17_ = bf16[1024,128]{1,0:T(8,128)(2,1)S(1)} collective-permute-done((bf16[1024,128]{1,0:T(8,128)(2,1)S(1)}, bf16[1024,128]{1,0:T(8,128)(2,1)S(1)}, u32[]{:S(2)}, u32[]{:S(2)}) %collective-permute-start.32) | collective-permute-done | bytes 262176 | tf_op jit(solution)/shard_map/ppermute | solution.py:38
  125.1 7.5 %collective-permute-done.33.refs_18_ = bf16[1024,128]{1,0:T(8,128)(2,1)S(1)} collective-permute-done((bf16[1024,128]{1,0:T(8,128)(2,1)S(1)}, bf16[1024,128]{1,0:T(8,128)(2,1)S(1)}, u32[]{:S(2)}, u32[]{:S(2)}) %collective-permute-start.33) | collective-permute-done | bytes 262176 | tf_op jit(solution)/shard_map/ppermute | solution.py:38
  132.7 2.6 %collective-permute-done.34.refs_19_ = bf16[1024,128]{1,0:T(8,128)(2,1)S(1)} collective-permute-done((bf16[1024,128]{1,0:T(8,128)(2,1)S(1)}, bf16[1024,128]{1,0:T(8,128)(2,1)S(1)}, u32[]{:S(2)}, u32[]{:S(2)}) %collective-permute-start.34) | collective-permute-done | bytes 262176 | tf_op jit(solution)/shard_map/ppermute | solution.py:38
  135.3 0.8 shard_map.171
  136.1 1.9 %collective-permute-start.35 = (f32[64,128]{1,0:T(8,128)S(1)}, f32[64,128]{1,0:T(8,128)S(1)}, u32[]{:S(2)}, u32[]{:S(2)}) collective-permute-start(f32[64,128]{1,0:T(8,128)S(1)} %get-tuple-element.41), channel_id=1, source_target_pairs={{0,0},{16,64},{32,128},{48,192},{64,16},{80,80},{96,144},{112,208}... | collective-permute-start | bytes 98312 | tf_op jit(solution)/shard_map/ppermute | solution.py:449
  138.1 7.0 %collective-permute-start.37 = (f32[64,128]{1,0:T(8,128)S(1)}, f32[64,128]{1,0:T(8,128)S(1)}, u32[]{:S(2)}, u32[]{:S(2)}) collective-permute-start(f32[64,128]{1,0:T(8,128)S(1)} %get-tuple-element.43), channel_id=1, source_target_pairs={{0,32},{16,96},{32,160},{48,224},{64,48},{80,112},{96,176},{112,24... | collective-permute-start | bytes 98312 | tf_op jit(solution)/shard_map/ppermute | solution.py:449
  145.1 0.7 reshape.113
  146.7 4.7 %collective-permute-done.38.d = f32[64,128]{1,0:T(8,128)S(1)} collective-permute-done((f32[64,128]{1,0:T(8,128)S(1)}, f32[64,128]{1,0:T(8,128)S(1)}, u32[]{:S(2)}, u32[]{:S(2)}) %collective-permute-start.38) | collective-permute-done | bytes 32800 | tf_op jit(solution)/shard_map/ppermute | solution.py:449
  151.4 1.3 shard_map.172
  (106 shorter events, 8.8 us)
Async XLA Ops:
  1.4 20.5 %copy-start.8 = (bf16[512,1,128]{2,0,1:T(8,128)(2,1)S(1)}, bf16[512,1,128]{2,0,1:T(8,128)(2,1)}, u32[]{:S(2)}) copy-start(bf16[512,1,128]{2,0,1:T(8,128)(2,1)} %param.19) | copy-start | bytes 393220
  3.5 12.0 %collective-permute-start = (bf16[128,128]{1,0:T(8,128)(2,1)}, bf16[128,128]{1,0:T(8,128)(2,1)S(1)}, u32[]{:S(2)}, u32[]{:S(2)}) collective-permute-start(bf16[128,128]{1,0:T(8,128)(2,1)} %shard_map.166.q_ref), channel_id=1, source_target_pairs={{0,2},{2,0},{4,6},{6,4},{8,10},{10,8},{12,14},{14,12},{1,3},{3,1},... | collective-permute-start | bytes 98312 | tf_op jit(solution)/shard_map/ppermute | solution.py:38
  3.6 16.1 %collective-permute-start.1 = (bf16[128,128]{1,0:T(8,128)(2,1)}, bf16[128,128]{1,0:T(8,128)(2,1)S(1)}, u32[]{:S(2)}, u32[]{:S(2)}) collective-permute-start(bf16[128,128]{1,0:T(8,128)(2,1)} %shard_map.166.q_ref), channel_id=1, source_target_pairs={{0,4},{2,6},{4,0},{6,2},{8,12},{10,14},{12,8},{14,10},{1,5},{3,7},... | collective-permute-start | bytes 98312 | tf_op jit(solution)/shard_map/ppermute | solution.py:38
  6.9 14.3 %collective-permute-start.2 = (bf16[128,128]{1,0:T(8,128)(2,1)}, bf16[128,128]{1,0:T(8,128)(2,1)S(1)}, u32[]{:S(2)}, u32[]{:S(2)}) collective-permute-start(bf16[128,128]{1,0:T(8,128)(2,1)} %shard_map.166.q_ref), channel_id=1, source_target_pairs={{0,6},{2,4},{4,2},{6,0},{8,14},{10,12},{12,10},{14,8},{1,7},{3,5},... | collective-permute-start | bytes 98312 | tf_op jit(solution)/shard_map/ppermute | solution.py:38
  7.4 14.0 %collective-permute-start.3 = (bf16[128,128]{1,0:T(8,128)(2,1)}, bf16[128,128]{1,0:T(8,128)(2,1)S(1)}, u32[]{:S(2)}, u32[]{:S(2)}) collective-permute-start(bf16[128,128]{1,0:T(8,128)(2,1)} %shard_map.166.q_ref), channel_id=1, source_target_pairs={{0,8},{2,10},{4,12},{6,14},{8,0},{10,2},{12,4},{14,6},{1,9},{3,11}... | collective-permute-start | bytes 98312 | tf_op jit(solution)/shard_map/ppermute | solution.py:38
  13.3 8.6 %collective-permute-start.4 = (bf16[128,128]{1,0:T(8,128)(2,1)}, bf16[128,128]{1,0:T(8,128)(2,1)S(1)}, u32[]{:S(2)}, u32[]{:S(2)}) collective-permute-start(bf16[128,128]{1,0:T(8,128)(2,1)} %shard_map.166.q_ref), channel_id=1, source_target_pairs={{0,10},{2,8},{4,14},{6,12},{8,2},{10,0},{12,6},{14,4},{1,11},{3,9}... | collective-permute-start | bytes 98312 | tf_op jit(solution)/shard_map/ppermute | solution.py:38
  13.8 1.4 copy-start.11
  13.8 1.7 %copy-start.2 = (bf16[128,128]{1,0:T(8,128)(2,1)S(1)}, bf16[128,128]{1,0:T(8,128)(2,1)}, u32[]{:S(2)}) copy-start(bf16[128,128]{1,0:T(8,128)(2,1)} %shard_map.166.q_ref) | copy-start | bytes 98308
  13.8 28.7 %copy-start.6 = (bf16[2048,1,128]{2,0,1:T(8,128)(2,1)S(1)}, bf16[2048,1,128]{2,0,1:T(8,128)(2,1)}, u32[]{:S(2)}) copy-start(bf16[2048,1,128]{2,0,1:T(8,128)(2,1)} %param.21) | copy-start | bytes 1572868
  15.5 6.6 %collective-permute-start.5 = (bf16[128,128]{1,0:T(8,128)(2,1)S(1)}, bf16[128,128]{1,0:T(8,128)(2,1)S(1)}, u32[]{:S(2)}, u32[]{:S(2)}) collective-permute-start(bf16[128,128]{1,0:T(8,128)(2,1)S(1)} %copy-done.2), channel_id=1, source_target_pairs={{0,12},{2,14},{4,8},{6,10},{8,4},{10,6},{12,0},{14,2},{1,13},{3,15... | collective-permute-start | bytes 98312 | tf_op jit(solution)/shard_map/ppermute | solution.py:38
  19.7 7.0 %collective-permute-start.6 = (bf16[128,128]{1,0:T(8,128)(2,1)S(1)}, bf16[128,128]{1,0:T(8,128)(2,1)S(1)}, u32[]{:S(2)}, u32[]{:S(2)}) collective-permute-start(bf16[128,128]{1,0:T(8,128)(2,1)S(1)} %copy-done.2), channel_id=1, source_target_pairs={{0,14},{2,12},{4,10},{6,8},{8,6},{10,4},{12,2},{14,0},{1,15},{3,13... | collective-permute-start | bytes 98312 | tf_op jit(solution)/shard_map/ppermute | solution.py:38
  21.2 21.3 %collective-permute-start.12 = (bf16[2048,128]{1,0:T(8,128)(2,1)}, bf16[2048,128]{1,0:T(8,128)(2,1)S(1)}, u32[]{:S(2)}, u32[]{:S(2)}) collective-permute-start(bf16[2048,128]{1,0:T(8,128)(2,1)} %bitcast.57), channel_id=1, source_target_pairs={{0,1},{1,0},{2,3},{3,2},{4,5},{5,4},{6,7},{7,6},{8,9},{9,8},{10,11... | collective-permute-start | bytes 1572872 | tf_op jit(solution)/shard_map/ppermute | solution.py:38
  21.4 21.1 %collective-permute-start.13 = (bf16[2048,128]{1,0:T(8,128)(2,1)}, bf16[2048,128]{1,0:T(8,128)(2,1)S(1)}, u32[]{:S(2)}, u32[]{:S(2)}) collective-permute-start(bf16[2048,128]{1,0:T(8,128)(2,1)} %bitcast.59), channel_id=1, source_target_pairs={{0,1},{1,0},{2,3},{3,2},{4,5},{5,4},{6,7},{7,6},{8,9},{9,8},{10,11... | collective-permute-start | bytes 1572872 | tf_op jit(solution)/shard_map/ppermute | solution.py:38
  21.9 6.3 %collective-permute-start.10 = (bf16[512,128]{1,0:T(8,128)(2,1)S(1)}, bf16[512,128]{1,0:T(8,128)(2,1)S(1)}, u32[]{:S(2)}, u32[]{:S(2)}) collective-permute-start(bf16[512,128]{1,0:T(8,128)(2,1)S(1)} %bitcast.61), channel_id=1, source_target_pairs={{0,1},{1,0},{2,3},{3,2},{4,5},{5,4},{6,7},{7,6},{8,9},{9,8},{10,11... | collective-permute-start | bytes 393224 | tf_op jit(solution)/shard_map/ppermute | solution.py:38
  22.1 8.9 %collective-permute-start.11 = (bf16[512,128]{1,0:T(8,128)(2,1)}, bf16[512,128]{1,0:T(8,128)(2,1)S(1)}, u32[]{:S(2)}, u32[]{:S(2)}) collective-permute-start(bf16[512,128]{1,0:T(8,128)(2,1)} %bitcast.63), channel_id=1, source_target_pairs={{0,1},{1,0},{2,3},{3,2},{4,5},{5,4},{6,7},{7,6},{8,9},{9,8},{10,11... | collective-permute-start | bytes 393224 | tf_op jit(solution)/shard_map/ppermute | solution.py:38
  26.8 8.1 %collective-permute-start.7 = (bf16[1024,128]{1,0:T(8,128)(2,1)S(1)}, bf16[1024,128]{1,0:T(8,128)(2,1)S(1)}, u32[]{:S(2)}, u32[]{:S(2)}) collective-permute-start(bf16[1024,128]{1,0:T(8,128)(2,1)S(1)} %constant_dynamic-update-slice_fusion.q0), channel_id=1, source_target_pairs={{0,16},{16,0},{32,48},{48,32},{1,17},{17,1},{33,49},{49,33},{2,18}... | collective-permute-start | bytes 786440 | tf_op jit(solution)/shard_map/ppermute | solution.py:38
  28.3 11.7 %collective-permute-start.8 = (bf16[1024,128]{1,0:T(8,128)(2,1)S(1)}, bf16[1024,128]{1,0:T(8,128)(2,1)S(1)}, u32[]{:S(2)}, u32[]{:S(2)}) collective-permute-start(bf16[1024,128]{1,0:T(8,128)(2,1)S(1)} %constant_dynamic-update-slice_fusion.q0), channel_id=1, source_target_pairs={{0,32},{16,48},{32,0},{48,16},{1,33},{17,49},{33,1},{49,17},{2,34}... | collective-permute-start | bytes 786440 | tf_op jit(solution)/shard_map/ppermute | solution.py:38
  31.0 11.5 %collective-permute-start.9 = (bf16[1024,128]{1,0:T(8,128)(2,1)S(1)}, bf16[1024,128]{1,0:T(8,128)(2,1)S(1)}, u32[]{:S(2)}, u32[]{:S(2)}) collective-permute-start(bf16[1024,128]{1,0:T(8,128)(2,1)S(1)} %constant_dynamic-update-slice_fusion.q0), channel_id=1, source_target_pairs={{0,48},{16,32},{32,16},{48,0},{1,49},{17,33},{33,17},{49,1},{2,50}... | collective-permute-start | bytes 786440 | tf_op jit(solution)/shard_map/ppermute | solution.py:38
  42.5 1.0 copy-start.7
  43.5 0.9 copy-start.9
  61.2 10.0 %collective-permute-start.14 = (bf16[1152,128]{1,0:T(8,128)(2,1)S(1)}, bf16[1152,128]{1,0:T(8,128)(2,1)S(1)}, u32[]{:S(2)}, u32[]{:S(2)}) collective-permute-start(bf16[1152,128]{1,0:T(8,128)(2,1)S(1)} %get-tuple-element.25), channel_id=1, source_target_pairs={{0,16},{16,0},{32,48},{48,32},{1,17},{17,1},{33,49},{49,33},{2,18}... | collective-permute-start | bytes 884744 | tf_op jit(solution)/shard_map/ppermute | solution.py:38
  61.3 12.1 %collective-permute-start.15 = (bf16[1152,128]{1,0:T(8,128)(2,1)S(1)}, bf16[1152,128]{1,0:T(8,128)(2,1)S(1)}, u32[]{:S(2)}, u32[]{:S(2)}) collective-permute-start(bf16[1152,128]{1,0:T(8,128)(2,1)S(1)} %get-tuple-element.26), channel_id=1, source_target_pairs={{0,32},{16,48},{32,0},{48,16},{1,33},{17,49},{33,1},{49,17},{2,34}... | collective-permute-start | bytes 884744 | tf_op jit(solution)/shard_map/ppermute | solution.py:38
  62.9 13.6 %collective-permute-start.16 = (bf16[1152,128]{1,0:T(8,128)(2,1)S(1)}, bf16[1152,128]{1,0:T(8,128)(2,1)S(1)}, u32[]{:S(2)}, u32[]{:S(2)}) collective-permute-start(bf16[1152,128]{1,0:T(8,128)(2,1)S(1)} %get-tuple-element.27), channel_id=1, source_target_pairs={{0,48},{16,32},{32,16},{48,0},{1,49},{17,33},{33,17},{49,1},{2,50}... | collective-permute-start | bytes 884744 | tf_op jit(solution)/shard_map/ppermute | solution.py:38
  76.5 15.8 %copy-start = (bf16[4,512,1,128]{3,1,2,0:T(8,128)(2,1)S(1)}, bf16[4,512,1,128]{3,1,2,0:T(8,128)(2,1)}, u32[]{:S(2)}) copy-start(bf16[4,512,1,128]{3,1,2,0:T(8,128)(2,1)} %param.23) | copy-start | bytes 1572868
  76.5 15.8 %copy-start.1 = (bf16[4,512,1,128]{3,1,2,0:T(8,128)(2,1)S(1)}, bf16[4,512,1,128]{3,1,2,0:T(8,128)(2,1)}, u32[]{:S(2)}) copy-start(bf16[4,512,1,128]{3,1,2,0:T(8,128)(2,1)} %param.24) | copy-start | bytes 1572868
  77.2 10.6 %collective-permute-start.17 = (bf16[144,128]{1,0:T(8,128)(2,1)S(1)}, bf16[144,128]{1,0:T(8,128)(2,1)S(1)}, u32[]{:S(2)}, u32[]{:S(2)}) collective-permute-start(bf16[144,128]{1,0:T(8,128)(2,1)S(1)} %get-tuple-element.29), channel_id=1, source_target_pairs={{0,2},{2,0},{4,6},{6,4},{8,10},{10,8},{12,14},{14,12},{1,3},{3,1},... | collective-permute-start | bytes 110600 | tf_op jit(solution)/shard_map/ppermute | solution.py:38
  79.0 12.6 %collective-permute-start.18 = (bf16[144,128]{1,0:T(8,128)(2,1)S(1)}, bf16[144,128]{1,0:T(8,128)(2,1)S(1)}, u32[]{:S(2)}, u32[]{:S(2)}) collective-permute-start(bf16[144,128]{1,0:T(8,128)(2,1)S(1)} %get-tuple-element.30), channel_id=1, source_target_pairs={{0,4},{2,6},{4,0},{6,2},{8,12},{10,14},{12,8},{14,10},{1,5},{3,7},... | collective-permute-start | bytes 110600 | tf_op jit(solution)/shard_map/ppermute | solution.py:38
  80.2 14.6 %collective-permute-start.19 = (bf16[144,128]{1,0:T(8,128)(2,1)S(1)}, bf16[144,128]{1,0:T(8,128)(2,1)S(1)}, u32[]{:S(2)}, u32[]{:S(2)}) collective-permute-start(bf16[144,128]{1,0:T(8,128)(2,1)S(1)} %get-tuple-element.31), channel_id=1, source_target_pairs={{0,6},{2,4},{4,2},{6,0},{8,14},{10,12},{12,10},{14,8},{1,7},{3,5},... | collective-permute-start | bytes 110600 | tf_op jit(solution)/shard_map/ppermute | solution.py:38
  80.8 14.0 %collective-permute-start.20 = (bf16[144,128]{1,0:T(8,128)(2,1)S(1)}, bf16[144,128]{1,0:T(8,128)(2,1)S(1)}, u32[]{:S(2)}, u32[]{:S(2)}) collective-permute-start(bf16[144,128]{1,0:T(8,128)(2,1)S(1)} %get-tuple-element.32), channel_id=1, source_target_pairs={{0,8},{2,10},{4,12},{6,14},{8,0},{10,2},{12,4},{14,6},{1,9},{3,11}... | collective-permute-start | bytes 110600 | tf_op jit(solution)/shard_map/ppermute | solution.py:38
  86.1 8.7 %collective-permute-start.21 = (bf16[144,128]{1,0:T(8,128)(2,1)S(1)}, bf16[144,128]{1,0:T(8,128)(2,1)S(1)}, u32[]{:S(2)}, u32[]{:S(2)}) collective-permute-start(bf16[144,128]{1,0:T(8,128)(2,1)S(1)} %get-tuple-element.33), channel_id=1, source_target_pairs={{0,10},{2,8},{4,14},{6,12},{8,2},{10,0},{12,6},{14,4},{1,11},{3,9}... | collective-permute-start | bytes 110600 | tf_op jit(solution)/shard_map/ppermute | solution.py:38
  87.8 7.0 %collective-permute-start.22 = (bf16[144,128]{1,0:T(8,128)(2,1)S(1)}, bf16[144,128]{1,0:T(8,128)(2,1)S(1)}, u32[]{:S(2)}, u32[]{:S(2)}) collective-permute-start(bf16[144,128]{1,0:T(8,128)(2,1)S(1)} %get-tuple-element.34), channel_id=1, source_target_pairs={{0,12},{2,14},{4,8},{6,10},{8,4},{10,6},{12,0},{14,2},{1,13},{3,15... | collective-permute-start | bytes 110600 | tf_op jit(solution)/shard_map/ppermute | solution.py:38
  91.5 7.1 %collective-permute-start.23 = (bf16[144,128]{1,0:T(8,128)(2,1)S(1)}, bf16[144,128]{1,0:T(8,128)(2,1)S(1)}, u32[]{:S(2)}, u32[]{:S(2)}) collective-permute-start(bf16[144,128]{1,0:T(8,128)(2,1)S(1)} %get-tuple-element.35), channel_id=1, source_target_pairs={{0,14},{2,12},{4,10},{6,8},{8,6},{10,4},{12,2},{14,0},{1,15},{3,13... | collective-permute-start | bytes 110600 | tf_op jit(solution)/shard_map/ppermute | solution.py:38
  98.9 16.5 %copy-start.10 = (bf16[2048,64]{0,1:T(8,128)(2,1)S(1)}, bf16[2048,64]{0,1:T(8,128)(2,1)}, u32[]{:S(2)}) copy-start(bf16[2048,64]{0,1:T(8,128)(2,1)} %param.25) | copy-start | bytes 786436
  98.9 9.3 %collective-permute-start.24 = (bf16[8,2048]{1,0:T(8,128)(2,1)S(1)}, bf16[8,2048]{1,0:T(8,128)(2,1)S(1)}, u32[]{:S(2)}, u32[]{:S(2)}) collective-permute-start(bf16[8,2048]{1,0:T(8,128)(2,1)S(1)} %get-tuple-element.40.refs_0_), channel_id=1, source_target_pairs={{0,2},{2,0},{4,6},{6,4},{8,10},{10,8},{12,14},{14,12},{1,3},{3,1},... | collective-permute-start | bytes 98312 | tf_op jit(solution)/shard_map/ppermute | solution.py:38
  99.3 9.2 %collective-permute-start.25 = (bf16[8,2048]{1,0:T(8,128)(2,1)S(1)}, bf16[8,2048]{1,0:T(8,128)(2,1)S(1)}, u32[]{:S(2)}, u32[]{:S(2)}) collective-permute-start(bf16[8,2048]{1,0:T(8,128)(2,1)S(1)} %get-tuple-element.40.refs_0_), channel_id=1, source_target_pairs={{0,4},{2,6},{4,0},{6,2},{8,12},{10,14},{12,8},{14,10},{1,5},{3,7},... | collective-permute-start | bytes 98312 | tf_op jit(solution)/shard_map/ppermute | solution.py:38
  100.8 12.0 %collective-permute-start.26 = (bf16[8,2048]{1,0:T(8,128)(2,1)S(1)}, bf16[8,2048]{1,0:T(8,128)(2,1)S(1)}, u32[]{:S(2)}, u32[]{:S(2)}) collective-permute-start(bf16[8,2048]{1,0:T(8,128)(2,1)S(1)} %get-tuple-element.40.refs_0_), channel_id=1, source_target_pairs={{0,6},{2,4},{4,2},{6,0},{8,14},{10,12},{12,10},{14,8},{1,7},{3,5},... | collective-permute-start | bytes 98312 | tf_op jit(solution)/shard_map/ppermute | solution.py:38
  102.7 10.1 %collective-permute-start.27 = (bf16[8,2048]{1,0:T(8,128)(2,1)S(1)}, bf16[8,2048]{1,0:T(8,128)(2,1)S(1)}, u32[]{:S(2)}, u32[]{:S(2)}) collective-permute-start(bf16[8,2048]{1,0:T(8,128)(2,1)S(1)} %get-tuple-element.40.refs_0_), channel_id=1, source_target_pairs={{0,8},{2,10},{4,12},{6,14},{8,0},{10,2},{12,4},{14,6},{1,9},{3,11}... | collective-permute-start | bytes 98312 | tf_op jit(solution)/shard_map/ppermute | solution.py:38
  104.4 8.5 %collective-permute-start.28 = (bf16[8,2048]{1,0:T(8,128)(2,1)S(1)}, bf16[8,2048]{1,0:T(8,128)(2,1)S(1)}, u32[]{:S(2)}, u32[]{:S(2)}) collective-permute-start(bf16[8,2048]{1,0:T(8,128)(2,1)S(1)} %get-tuple-element.40.refs_0_), channel_id=1, source_target_pairs={{0,10},{2,8},{4,14},{6,12},{8,2},{10,0},{12,6},{14,4},{1,11},{3,9}... | collective-permute-start | bytes 98312 | tf_op jit(solution)/shard_map/ppermute | solution.py:38
  108.2 6.0 %collective-permute-start.29 = (bf16[8,2048]{1,0:T(8,128)(2,1)S(1)}, bf16[8,2048]{1,0:T(8,128)(2,1)S(1)}, u32[]{:S(2)}, u32[]{:S(2)}) collective-permute-start(bf16[8,2048]{1,0:T(8,128)(2,1)S(1)} %get-tuple-element.40.refs_0_), channel_id=1, source_target_pairs={{0,12},{2,14},{4,8},{6,10},{8,4},{10,6},{12,0},{14,2},{1,13},{3,15... | collective-permute-start | bytes 98312 | tf_op jit(solution)/shard_map/ppermute | solution.py:38
  108.5 6.9 %collective-permute-start.30 = (bf16[8,2048]{1,0:T(8,128)(2,1)S(1)}, bf16[8,2048]{1,0:T(8,128)(2,1)S(1)}, u32[]{:S(2)}, u32[]{:S(2)}) collective-permute-start(bf16[8,2048]{1,0:T(8,128)(2,1)S(1)} %get-tuple-element.40.refs_0_), channel_id=1, source_target_pairs={{0,14},{2,12},{4,10},{6,8},{8,6},{10,4},{12,2},{14,0},{1,15},{3,13... | collective-permute-start | bytes 98312 | tf_op jit(solution)/shard_map/ppermute | solution.py:38
  115.4 5.4 %collective-permute-start.31 = (bf16[8,8,2048]{2,1,0:T(8,128)(2,1)S(1)}, bf16[8,8,2048]{2,1,0:T(8,128)(2,1)S(1)}, u32[]{:S(2)}, u32[]{:S(2)}) collective-permute-start(bf16[8,8,2048]{2,1,0:T(8,128)(2,1)S(1)} %constant_dynamic-update-slice_fusion.8), channel_id=1, source_target_pairs={{0,1},{1,0},{2,3},{3,2},{4,5},{5,4},{6,7},{7,6},{8,9},{9,8},{10,11... | collective-permute-start | bytes 786440 | tf_op jit(solution)/shard_map/ppermute | solution.py:38
  116.0 9.2 %collective-permute-start.32 = (bf16[1024,128]{1,0:T(8,128)(2,1)S(1)}, bf16[1024,128]{1,0:T(8,128)(2,1)S(1)}, u32[]{:S(2)}, u32[]{:S(2)}) collective-permute-start(bf16[1024,128]{1,0:T(8,128)(2,1)S(1)} %pad_maximum_fusion.refs_16_), channel_id=1, source_target_pairs={{0,16},{16,0},{32,48},{48,32},{1,17},{17,1},{33,49},{49,33},{2,18}... | collective-permute-start | bytes 786440 | tf_op jit(solution)/shard_map/ppermute | solution.py:38
  116.1 16.6 %collective-permute-start.33 = (bf16[1024,128]{1,0:T(8,128)(2,1)S(1)}, bf16[1024,128]{1,0:T(8,128)(2,1)S(1)}, u32[]{:S(2)}, u32[]{:S(2)}) collective-permute-start(bf16[1024,128]{1,0:T(8,128)(2,1)S(1)} %pad_maximum_fusion.refs_16_), channel_id=1, source_target_pairs={{0,32},{16,48},{32,0},{48,16},{1,33},{17,49},{33,1},{49,17},{2,34}... | collective-permute-start | bytes 786440 | tf_op jit(solution)/shard_map/ppermute | solution.py:38
  120.3 15.0 %collective-permute-start.34 = (bf16[1024,128]{1,0:T(8,128)(2,1)S(1)}, bf16[1024,128]{1,0:T(8,128)(2,1)S(1)}, u32[]{:S(2)}, u32[]{:S(2)}) collective-permute-start(bf16[1024,128]{1,0:T(8,128)(2,1)S(1)} %pad_maximum_fusion.refs_16_), channel_id=1, source_target_pairs={{0,48},{16,32},{32,16},{48,0},{1,49},{17,33},{33,17},{49,1},{2,50}... | collective-permute-start | bytes 786440 | tf_op jit(solution)/shard_map/ppermute | solution.py:38
  136.1 10.4 %collective-permute-start.35 = (f32[64,128]{1,0:T(8,128)S(1)}, f32[64,128]{1,0:T(8,128)S(1)}, u32[]{:S(2)}, u32[]{:S(2)}) collective-permute-start(f32[64,128]{1,0:T(8,128)S(1)} %get-tuple-element.41), channel_id=1, source_target_pairs={{0,0},{16,64},{32,128},{48,192},{64,16},{80,80},{96,144},{112,208}... | collective-permute-start | bytes 98312 | tf_op jit(solution)/shard_map/ppermute | solution.py:449
  138.0 8.5 %collective-permute-start.36 = (f32[64,128]{1,0:T(8,128)S(1)}, f32[64,128]{1,0:T(8,128)S(1)}, u32[]{:S(2)}, u32[]{:S(2)}) collective-permute-start(f32[64,128]{1,0:T(8,128)S(1)} %get-tuple-element.42), channel_id=1, source_target_pairs={{0,16},{16,80},{32,144},{48,208},{64,0},{80,64},{96,128},{112,192}... | collective-permute-start | bytes 98312 | tf_op jit(solution)/shard_map/ppermute | solution.py:449
  138.1 8.6 %collective-permute-start.37 = (f32[64,128]{1,0:T(8,128)S(1)}, f32[64,128]{1,0:T(8,128)S(1)}, u32[]{:S(2)}, u32[]{:S(2)}) collective-permute-start(f32[64,128]{1,0:T(8,128)S(1)} %get-tuple-element.43), channel_id=1, source_target_pairs={{0,32},{16,96},{32,160},{48,224},{64,48},{80,112},{96,176},{112,24... | collective-permute-start | bytes 98312 | tf_op jit(solution)/shard_map/ppermute | solution.py:449
  145.1 6.3 %collective-permute-start.38 = (f32[64,128]{1,0:T(8,128)S(1)}, f32[64,128]{1,0:T(8,128)S(1)}, u32[]{:S(2)}, u32[]{:S(2)}) collective-permute-start(f32[64,128]{1,0:T(8,128)S(1)} %get-tuple-element.44), channel_id=1, source_target_pairs={{0,48},{16,112},{32,176},{48,240},{64,32},{80,96},{96,160},{112,22... | collective-permute-start | bytes 98312 | tf_op jit(solution)/shard_map/ppermute | solution.py:449
  (5 other events, 3.6 us)

commit v2 on v1

--- a/solution.py
+++ b/solution.py
@@ -20,13 +20,17 @@
 STAT = 16
 PACK = PIECE + STAT
 NX, NZ = 4, 8
-PIECES = NX * NZ
-LOCAL = PIECES * OWN
+NEAR = NZ // 2
+LOCAL = NX * NEAR * OWN
 SCALE = 1.0 / math.sqrt(HD)
 EXP2 = SCALE * math.log2(math.e)
-ITEM = 8
-BATCH = 4
+ITEM = 4
+BATCH = 8
 SLOTS = 16
+ROOT = 512
+HELD = SLOTS // 2 * BLK
+CHUNKS = 4
+QUARTER = NEAR * PIECE
 VMEM = pl.BlockSpec(memory_space=pltpu.VMEM)
 SMEM = pl.BlockSpec(memory_space=pltpu.SMEM)
 ANY = pl.BlockSpec(memory_space=pl.ANY)
@@ -121,22 +125,31 @@
     lse_ref[...] = jnp.broadcast_to(lse, lse_ref.shape)
 
 
-def shared_kernel(
-    meta_ref, q0, q1, q2, q3, rk0, rk1, rv0, rv1, bk0, bk1, bv0, bv1,
-    out0, out1, out2, out3,
-    item_block, item_part, bk, bv, q_all, acc, top_all, sum_all, part, part_top, part_sum, sems,
-):
-    half = bk.shape[0] // 2
+def shared_kernel(second, meta_ref, *refs):
+    limbs, refs = refs[:2], refs[2:]
+    if second:
+        before, outs = refs[:4], refs[4:4 + NX]
+        q_all, acc, top_all, sum_all = refs[4 + NX:8 + NX]
+        refs = refs[8 + NX:]
+    else:
+        qs, roots = refs[:NX], refs[NX:NX + 2]
+        q_all, acc, top_all, sum_all = refs[2 + NX:6 + NX]
+        refs = refs[6 + NX:]
+    item_block, item_part, held, part, part_top, part_sum, sems = refs
+
     copies = []
-    for n, (src, dst) in enumerate(((bk0, bk), (bk1, bk), (bv0, bv), (bv1, bv))):
+    for n in range(2):
         copies.append(
-            pltpu.make_async_copy(src, dst.at[pl.ds((n % 2) * half, half)], sems.at[n])
+            pltpu.make_async_copy(limbs[n], held.at[pl.ds(n * 2 * HELD, 2 * HELD)], sems.at[n])
         )
+    if second:
+        for n, (src, dst) in enumerate(zip(before, (q_all, acc, top_all, sum_all))):
+            copies.append(pltpu.make_async_copy(src, dst, sems.at[2 + n]))
     for copy in copies:
         copy.start()
 
     def list_block(j, n):
-        parts = (meta_ref[LOCAL + j] + (ITEM - 1)) >> 3
+        parts = (meta_ref[LOCAL + j] + (ITEM - 1)) // ITEM
 
         def put(k, carry):
             item_block[n + k] = j
@@ -151,31 +164,35 @@
         item_block[items + u] = 0
         item_part[items + u] = LOCAL
 
-    q_all[pl.ds(LOCAL * REQ_ROWS, REQ_ROWS), :] = jnp.zeros((REQ_ROWS, HD), bf16)
-    acc[pl.ds(LOCAL * REQ_ROWS, REQ_ROWS), :] = jnp.zeros((REQ_ROWS, HD), f32)
-    top_all[pl.ds(LOCAL * REQ_ROWS, REQ_ROWS), :] = jnp.zeros((REQ_ROWS, HD), f32)
-    sum_all[pl.ds(LOCAL * REQ_ROWS, REQ_ROWS), :] = jnp.ones((REQ_ROWS, HD), f32)
-
     tile = 256
-    quarter = NZ * PIECE
-    for g, q_ref in enumerate((q0, q1, q2, q3)):
-
-        def root_tile(t, carry):
-            q = q_ref[pl.ds(pl.multiple_of(t * tile, tile), tile), :]
-            rows = pl.ds(pl.multiple_of(g * quarter + t * tile, tile), tile)
-            q_all[rows, :] = q
-            s0 = nt(q, rk0[...])
-            s1 = nt(q, rk1[...])
-            top = jnp.max(jnp.maximum(s0, s1), axis=1, keepdims=True)
-            w0 = jnp.exp2((s0 - top) * EXP2)
-            w1 = jnp.exp2((s1 - top) * EXP2)
-            total = jnp.sum(w0 + w1, axis=1, keepdims=True)
-            acc[rows, :] = nn(w0.astype(bf16), rv0[...]) + nn(w1.astype(bf16), rv1[...])
-            top_all[rows, :] = jnp.broadcast_to(top, (tile, HD))
-            sum_all[rows, :] = jnp.broadcast_to(total, (tile, HD))
-            return carry
-
-        lax.fori_loop(0, quarter // tile, root_tile, 0, unroll=2)
+    if not second:
+        spare = pl.ds(LOCAL * REQ_ROWS, REQ_ROWS)
+        q_all[spare, :] = jnp.zeros((REQ_ROWS, HD), bf16)
+        acc[spare, :] = jnp.zeros((REQ_ROWS, HD), f32)
+        top_all[spare, :] = jnp.zeros((REQ_ROWS, HD), f32)
+        sum_all[spare, :] = jnp.ones((REQ_ROWS, HD), f32)
+        keys, values = [], []
+        for ref in roots:
+            for n in range(CHUNKS // 2):
+                keys.append(ref.at[pl.ds(2 * n * ROOT, ROOT)])
+                values.append(ref.at[pl.ds((2 * n + 1) * ROOT, ROOT)])
+        for g, q_ref in enumerate(qs):
+
+            def root_tile(t, carry):
+                q = q_ref[pl.ds(pl.multiple_of(t * tile, tile), tile), :]
+                rows = pl.ds(pl.multiple_of(g * QUARTER + t * tile, tile), tile)
+                q_all[rows, :] = q
+                scores = [nt(q, ref[...]) for ref in keys]
+                top = jnp.max(functools.reduce(jnp.maximum, scores), axis=1, keepdims=True)
+                weights = [jnp.exp2((score - top) * EXP2) for score in scores]
+                total = jnp.sum(functools.reduce(jnp.add, weights), axis=1, keepdims=True)
+                out = [nn(w.astype(bf16), ref[...]) for w, ref in zip(weights, values)]
+                acc[rows, :] = functools.reduce(jnp.add, out)
+                top_all[rows, :] = jnp.broadcast_to(top, (tile, HD))
+                sum_all[rows, :] = jnp.broadcast_to(total, (tile, HD))
+                return carry
+
+            lax.fori_loop(0, QUARTER // tile, root_tile, 0, unroll=2)
 
     for copy in copies:
         copy.wait()
@@ -192,13 +209,15 @@
             block = item_block[b * BATCH + u]
             first = item_part[b * BATCH + u] * ITEM
             rows = [request_rows(block, first + e) for e in range(ITEM)]
-            tokens = pl.ds(pl.multiple_of(block * BLK, BLK), BLK)
+            offset = (block >> 3) * 2 * HELD + (block & 7) * BLK
+            keys = held[pl.ds(pl.multiple_of(offset, BLK), BLK), :]
+            values = held[pl.ds(pl.multiple_of(offset + HELD, BLK), BLK), :]
             q = jnp.concatenate([q_all[r, :] for r in rows], 0)
-            scores = nt(q, bk[tokens, :])
+            scores = nt(q, keys)
             top = jnp.max(scores, axis=1, keepdims=True)
             weights = jnp.exp2((scores - top) * EXP2)
             total = jnp.sum(weights, axis=1, keepdims=True)
-            part[u] = nn(weights.astype(bf16), bv[tokens, :])
+            part[u] = nn(weights.astype(bf16), values)
             part_top[u] = jnp.broadcast_to(top, (ITEM * REQ_ROWS, HD))
             part_sum[u] = jnp.broadcast_to(total, (ITEM * REQ_ROWS, HD))
             places.append(rows)
@@ -219,13 +238,15 @@
                 acc[r, :] = new_acc[piece]
         return carry
 
-    lax.fori_loop(0, (items + BATCH - 1) >> 2, batch, 0)
+    lax.fori_loop(0, (items + BATCH - 1) // BATCH, batch, 0)
+    if not second:
+        return
 
     diag = diagonal()
-    for g, out in enumerate((out0, out1, out2, out3)):
+    for g, out in enumerate(outs):
 
         def finish(n, carry):
-            rows = pl.ds(pl.multiple_of(g * quarter + n * PIECE, PIECE), PIECE)
+            rows = pl.ds(pl.multiple_of(g * QUARTER + n * PIECE, PIECE), PIECE)
             total = sum_all[rows, :]
             start = pl.multiple_of(n * PACK, 16)
             out[pl.ds(start, PIECE), :] = (acc[rows, :] / total).astype(bf16)
@@ -233,7 +254,7 @@
             out[pl.ds(start + PIECE, STAT), :] = pack_lse(to_lanes(lse, diag))
             return carry
 
-        lax.fori_loop(0, NZ, finish, 0, unroll=2)
+        lax.fori_loop(0, NEAR, finish, 0, unroll=2)
 
 
 def merge_kernel(a, b, c, d, *outs):
@@ -252,7 +273,7 @@
 
 
 def final_kernel(*refs):
-    parts, (own, own_lse, attn, attn_low, lse_out, rows) = refs[:NZ], refs[NZ:]
+    parts, (own, own_lse, attn, attn_low, lse_out, rows) = refs[:NEAR], refs[NEAR:]
     diag = diagonal()
     merged, lse = merge(
         [lambda ref=ref: ref[0:PIECE, :].astype(f32) for ref in parts] + [lambda: own[...]],
@@ -269,15 +290,27 @@
     attn_low[...] = attn[...].astype(bf16)
 
 
-def project_kernel(where_ref, *refs):
-    rows, weights, outs, terms = refs[:2 * NZ], refs[2 * NZ:2 * NZ + NX], refs[2 * NZ + NX:-1], refs[-1]
-    left = jnp.concatenate([r[...].astype(f32) for r in rows], 0).astype(bf16)
-    depth = left.shape[1] // 2
+def project_kernel(where_ref, pair_ref, here_ref, there_ref, *refs):
+    weights, outs, terms = refs[:NX], refs[NX:-1], refs[-1]
+    one = STEPS * OWN
+    pair, here, there = [ref[...].astype(f32) for ref in (pair_ref, here_ref, there_ref)]
+    first = where_ref[1] == 0
+    low, high = jnp.where(first, here, there), jnp.where(first, there, here)
+    left = [pair[:one]]
+    other = [pair[one:]]
+    for source in (low, high):
+        own_side = [source[2 * n * one:(2 * n + 1) * one] for n in range(NEAR - 1)]
+        other_side = [source[(2 * n + 1) * one:(2 * n + 2) * one] for n in range(NEAR - 1)]
+        swapped = first if source is high else jnp.logical_not(first)
+        for a, b in zip(own_side, other_side):
+            left.append(jnp.where(swapped, b, a))
+            other.append(jnp.where(swapped, a, b))
+        if source is low:
+            left.append(here[2 * (NEAR - 1) * one:])
+            other.append(there[2 * (NEAR - 1) * one:])
+    left = jnp.concatenate(left + other, 0).astype(bf16)
     for n, weight in enumerate(weights):
-        low = nn(left[:, :depth], weight[...])
-        high = nn(left[:, depth:], weight[...])
-        columns = low.shape[1] // 2
-        term = low[:, :columns] + high[:, columns:]
+        term = nt(left, weight[...])
         count = term.shape[0] // 2
         terms[n] = jnp.concatenate([term[:count], term[count:]], 1)
     for n, out in enumerate(outs):
@@ -303,15 +336,16 @@
     leaf = (x * NZ + z) * 2 + core
     here = SLOTS // 2
     block_ids = jnp.arange(block_slot.shape[0], dtype=jnp.int32)
-    offsets = jnp.arange(here, dtype=jnp.int32)
-    slot_ids = jnp.concatenate([leaf * here + offsets, (leaf ^ 1) * here + offsets])
+    j = jnp.arange(2 * SLOTS, dtype=jnp.int32)
+    slot_ids = (leaf ^ (j >> 3)) * here + (j & (here - 1))
     slot_block = jnp.sum(
         jnp.where(block_slot[:, None] == slot_ids[None, :], block_ids[:, None], 0), axis=0
     )
-    cum_end = jnp.cumsum(branch_blocks)
+    k = jnp.arange(branch_blocks.shape[0], dtype=jnp.int32)
+    cum_end = jnp.sum(jnp.where(k[:, None] <= k[None, :], branch_blocks[:, None], 0), axis=0)
     slot_branch = jnp.sum((cum_end[None, :] <= slot_block[:, None]).astype(jnp.int32), axis=1)
     n = jnp.arange(LOCAL, dtype=jnp.int32)
-    owner = ((x ^ (n >> 5)) * NZ + (z ^ ((n >> 2) & (NZ - 1)))) * 2 + core
+    owner = ((x ^ (n >> 4)) * NZ + (z ^ (((n >> 2) & (NEAR - 1)) * 2))) * 2 + core
     request = owner * OWN + (n & (OWN - 1))
     every = jnp.arange(request_branch.shape[0], dtype=jnp.int32)
     branch = jnp.sum(jnp.where(request[:, None] == every[None, :], request_branch[None, :], 0), 1)
@@ -322,7 +356,10 @@
     ordered = jnp.sum(jnp.where(rank[:, None] == n[None, :], n[:, None], 0), axis=0)
     count = jnp.sum((slot_branch[:, None] == branch[None, :]).astype(jnp.int32), axis=1)
     start = jnp.sum((branch[None, :] < slot_branch[:, None]).astype(jnp.int32), axis=1)
-    return jnp.concatenate([ordered, count, start]).astype(jnp.int32)
+    return [
+        jnp.concatenate([ordered, count[half], start[half]]).astype(jnp.int32)
+        for half in (slice(0, SLOTS), slice(SLOTS, 2 * SLOTS))
+    ]
 
 
 def struct(shape, dtype):
@@ -351,18 +388,43 @@
     normed = pl.pallas_call(
         norm_kernel, out_shape=struct((PIECE, HD), bf16), in_specs=[VMEM, VMEM], out_specs=VMEM
     )(raw, query_gain.reshape(1, HD))
-    near = jnp.concatenate([normed] + [swap(normed, "z", NZ, k) for k in range(1, NZ)], 0)
+    near = jnp.concatenate([normed] + [swap(normed, "z", NZ, 2 * k) for k in range(1, NEAR)], 0)
     quarters = [near] + [swap(near, "x", NX, k) for k in range(1, NX)]
 
-    shared = []
-    for a in (root_keys, root_values, branch_keys, branch_values):
-        flat = a.reshape(a.shape[0], HD)
-        shared += [flat, swap(flat, "core", 2, 1)]
-    depth = out_weight.shape[0] // 2
-    folded = jnp.concatenate([out_weight[:depth], out_weight[depth:]], 1)
-    weights = [folded] + [swap(folded, "x", NX, k) for k in range(1, NX)]
+    root = jnp.concatenate([root_keys.reshape(ROOT, HD), root_values.reshape(ROOT, HD)], 0)
+    limb = jnp.concatenate([branch_keys.reshape(HELD, HD), branch_values.reshape(HELD, HD)], 0)
+    far = swap(limb, "z", NZ, 1)
+    roots = jnp.concatenate([root, swap(root, "z", NZ, 1)], 0)
+    roots = [roots, swap(roots, "core", 2, 1)]
+    limbs = [limb, swap(limb, "core", 2, 1)]
     meta = plan(request_branch, branch_blocks, block_slot, x, z, core)
 
+    rows = LOCAL * REQ_ROWS
+    spare = rows + REQ_ROWS
+    state = [struct((spare, HD), bf16)] + [struct((spare, HD), f32)] * 3
+    most = SLOTS * LOCAL // ITEM + BATCH
+    scratch = [
+        pltpu.SMEM((most,), jnp.int32),
+        pltpu.SMEM((most,), jnp.int32),
+        pltpu.VMEM((4 * HELD, HD), bf16),
+    ]
+    scratch += [pltpu.VMEM((BATCH, ITEM * REQ_ROWS, HD), f32)] * 3
+    scratch += [pltpu.SemaphoreType.DMA((6,))]
+    cost = pl.CostEstimate(
+        flops=4 * rows * HD * 2048, bytes_accessed=8 << 20, transcendentals=rows * 2048
+    )
+    before = pl.pallas_call(
+        functools.partial(shared_kernel, False),
+        out_shape=state,
+        in_specs=[SMEM] + [ANY] * 2 + [VMEM] * (NX + 2),
+        out_specs=[VMEM] * 4,
+        scratch_shapes=scratch,
+        compiler_params=PARAMS,
+        cost_estimate=cost,
+    )(meta[0], *limbs, *quarters, *roots)
+    turned = out_weight.T
+    weights = [turned] + [swap(turned, "x", NX, k) for k in range(1, NX)]
+    before, weights, tied = lax.optimization_barrier((before, weights, normed))
     own, own_lse = pl.pallas_call(
         own_kernel,
         out_shape=[struct((PIECE, HD), f32), struct((8, PIECE), f32)],
@@ -371,50 +433,33 @@
         compiler_params=PARAMS,
     )(
         suffix_length,
-        normed,
+        tied,
         suffix_keys.reshape(OWN, SUF, HD),
         suffix_values.reshape(OWN, SUF, HD),
         new_keys.reshape(STEPS * OWN, HD),
         new_values.reshape(STEPS * OWN, HD),
     )
 
-    rows = LOCAL * REQ_ROWS
-    spare = rows + REQ_ROWS
-    branch_rows = SLOTS * BLK
+    far, own, own_lse = lax.optimization_barrier((far, own, own_lse))
+    far = [far, swap(far, "core", 2, 1)]
     partials = pl.pallas_call(
-        shared_kernel,
-        out_shape=[struct((NZ * PACK, HD), bf16)] * NX,
-        in_specs=[SMEM] + [VMEM] * 8 + [ANY] * 4,
+        functools.partial(shared_kernel, True),
+        out_shape=[struct((NEAR * PACK, HD), bf16)] * NX,
+        in_specs=[SMEM] + [ANY] * 6,
         out_specs=[VMEM] * NX,
-        scratch_shapes=[
-            pltpu.SMEM((SLOTS * LOCAL // ITEM + BATCH,), jnp.int32),
-            pltpu.SMEM((SLOTS * LOCAL // ITEM + BATCH,), jnp.int32),
-            pltpu.VMEM((branch_rows, HD), bf16),
-            pltpu.VMEM((branch_rows, HD), bf16),
-            pltpu.VMEM((spare, HD), bf16),
-            pltpu.VMEM((spare, HD), f32),
-            pltpu.VMEM((spare, HD), f32),
-            pltpu.VMEM((spare, HD), f32),
-            pltpu.VMEM((BATCH, ITEM * REQ_ROWS, HD), f32),
-            pltpu.VMEM((BATCH, ITEM * REQ_ROWS, HD), f32),
-            pltpu.VMEM((BATCH, ITEM * REQ_ROWS, HD), f32),
-            pltpu.SemaphoreType.DMA((4,)),
-        ],
-        compiler_params=PARAMS,
-        cost_estimate=pl.CostEstimate(
-            flops=4 * rows * HD * 2048, bytes_accessed=6 << 20, transcendentals=rows * 2048
-        ),
-    )(meta, *quarters, *shared)
-
+        scratch_shapes=[pltpu.VMEM(part.shape, part.dtype) for part in state] + scratch,
+        compiler_params=PARAMS,
+        cost_estimate=cost,
+    )(meta[1], *far, *before)
     returned = [partials[0]] + [swap(partials[k], "x", NX, k) for k in range(1, NX)]
     merged = pl.pallas_call(
         merge_kernel,
-        out_shape=[struct((PACK, HD), bf16)] * NZ,
+        out_shape=[struct((PACK, HD), bf16)] * NEAR,
         in_specs=[VMEM] * NX,
-        out_specs=[VMEM] * NZ,
+        out_specs=[VMEM] * NEAR,
         compiler_params=PARAMS,
     )(*returned)
-    landed = [merged[0]] + [swap(merged[k], "z", NZ, k) for k in range(1, NZ)]
+    landed = [merged[0]] + [swap(merged[k], "z", NZ, 2 * k) for k in range(1, NEAR)]
     attn, attn_low, lse = pl.pallas_call(
         final_kernel,
         out_shape=[
@@ -422,7 +467,7 @@
             struct((STEPS * OWN, GROUP * HD), bf16),
             struct((8, PIECE), f32),
         ],
-        in_specs=[VMEM] * (NZ + 2),
+        in_specs=[VMEM] * (NEAR + 2),
         out_specs=[VMEM] * 3,
         scratch_shapes=[pltpu.VMEM((PIECE, HD), f32)],
         compiler_params=PARAMS,
@@ -430,19 +475,24 @@
     attn_out = attn.reshape(STEPS, OWN, 1, GROUP * HD)
     log_total = lse[0].reshape(OWN, STEPS, GROUP).transpose(1, 0, 2).reshape(STEPS, OWN, 1, GROUP)
 
-    held = [attn_low] + [swap(attn_low, "z", NZ, k) for k in range(1, NZ)]
-    stacked = jnp.stack(held)
-    across = swap(stacked, "core", 2, 1)
+    pair = jnp.concatenate([attn_low, swap(attn_low, "core", 2, 1)], 0)
+    fetched = []
+    for k in range(1, NEAR):
+        moves = [(a * 2 + c, (a ^ (k + NEAR * c)) * 2 + c) for a in range(NZ) for c in range(2)]
+        fetched.append(lax.ppermute(pair, ("z", "core"), moves))
+    opposite = swap(attn_low, "z", NZ, NEAR)
+    fetched = jnp.concatenate(fetched + [opposite], 0)
+    rows = [pair, fetched, swap(fetched, "core", 2, 1)]
     columns = out_weight.shape[1]
     term = struct((NZ * STEPS * OWN, 2 * columns), f32)
     terms = pl.pallas_call(
         project_kernel,
         out_shape=[term] * NX,
-        in_specs=[SMEM] + [VMEM] * (2 * NZ + NX),
+        in_specs=[SMEM] + [VMEM] * (3 + NX),
         out_specs=[VMEM] * NX,
         scratch_shapes=[pltpu.VMEM((NX,) + term.shape, f32)],
         compiler_params=PARAMS,
-    )((x ^ kv).reshape(1), *held, *[across[k] for k in range(NZ)], *weights)
+    )(jnp.stack([x ^ kv, core]), *rows, *weights)
     arrived = []
     for k in range(NX):
         pairs = [(v * NX + c, c * NX + (v ^ k)) for v in range(NX) for c in range(NX)]

time: 152 us -> 121 us (0.80)
  starting transfers between devices: 69.4 us -> 49.5 us
  waiting for transfers between devices: 51 us -> 42.7 us
  local copies, waits for them, and re-layouts: 6.65 us -> 3.05 us
  Pallas kernels: 23.1 us -> 20.8 us
  other arithmetic: 1.55 us -> 3.43 us
    ppermute x35 -> x23, starting transfers between devices: 60.5 us -> 34.7 us  [swap(): return lax.ppermute(a, axis, [(i, i ^ k) for i in range(n)])]
    ppermute x35 -> x23, waiting for transfers between devices: 46.1 us -> 32.9 us  [swap(): return lax.ppermute(a, axis, [(i, i ^ k) for i in range(n)])]
    ppermute x0 -> x3, waiting for transfers between devices: none -> 4.88 us  [shards(): fetched.append(lax.ppermute(pair, ('z', 'core'), moves))]
    ppermute x0 -> x3, starting transfers between devices: none -> 4.48 us  [shards(): fetched.append(lax.ppermute(pair, ('z', 'core'), moves))]
    unnamed x45 -> x31, local copies, waits for them, and re-layouts: 4.3 us -> 0.69 us
    pallas_call x2 -> x3, Pallas kernels: 17.4 us -> 14.7 us  [the longest x1 10.3 us: shards(): pl.pallas_call(functools.partial(shared_kernel, False), out_shape=state,...]
    concatenate x3 -> x5, other arithmetic: 0.3 us -> 2.27 us  [the longest x1 1.16 us: shards(): jnp.concatenate([branch_keys.reshape(HELD, HD), branch_values.reshape(HEL...]
  transfers between devices with their start and end apart: 39 -> 30, of which waited for: 15 -> 17; matrix products, arithmetic and copies ran while one was open for 2% -> 4% of each run, Pallas kernels for 1% -> 10%
where the time goes in v2:
time: 121 us; the launch traced here: 120 us
  starting transfers between devices  49.5 us (41%)
  waiting for transfers between devices  42.7 us (35%)
  Pallas kernels  20.8 us (17%)
  other arithmetic  3.43 us (3%)
  local copies, waits for them, and re-layouts  3.05 us (3%)
    ppermute x23, starting transfers between devices, swap(): return lax.ppermute(a, axis, [(i, i ^ k) for i in range(n)])  34.7 us
    ppermute x23, waiting for transfers between devices, swap(): return lax.ppermute(a, axis, [(i, i ^ k) for i in range(n)])  32.9 us
    pallas_call x1, Pallas kernels, shards(): pl.pallas_call(functools.partial(shared_kernel, False), out_shape=state,...  10.3 us
    ppermute x4, starting transfers between devices, shards(): arrived.append(lax.ppermute(terms[k], ('kv', 'x'), pairs))  10.3 us
    ppermute x4, waiting for transfers between devices, shards(): arrived.append(lax.ppermute(terms[k], ('kv', 'x'), pairs))  4.89 us
    ppermute x3, waiting for transfers between devices, shards(): fetched.append(lax.ppermute(pair, ('z', 'core'), moves))  4.88 us
    ppermute x3, starting transfers between devices, shards(): fetched.append(lax.ppermute(pair, ('z', 'core'), moves))  4.48 us
    pallas_call x1, Pallas kernels, shards(): pl.pallas_call(functools.partial(shared_kernel, True), out_shape=[struct(...  3.93 us
  transfers between devices with their start and end apart: 30, of which 17 were waited for; matrix products, arithmetic and copies ran while one was open for 4% of the time, Pallas kernels for 10%

profile of v2, /device:TPU:40, one launch (start us, length us, event | category | flops | bytes accessed | tf_op | source)
XLA Modules:
  0.0 120.4 jit_solution(3325487945375525886)
XLA Ops:
  0.6 0.8 reshape.83
  1.5 0.6 copy.22
  2.1 1.5 %shard_map.166.q_ref = bf16[128,128]{1,0:T(8,128)(2,1)} custom-call(bf16[128,128]{1,0:T(8,128)(2,1)} %bitcast.35, f32[1,128]{1,0:T(1,128)} %bitcast.37), custom_call_target="tpu_custom_call" | custom-call | tf_op jit(solution)/shard_map/pallas_call | solution.py:388
  3.6 3.3 %collective-permute-start.2 = (bf16[128,128]{1,0:T(8,128)(2,1)}, bf16[128,128]{1,0:T(8,128)(2,1)S(1)}, u32[]{:S(2)}, u32[]{:S(2)}) collective-permute-start(bf16[128,128]{1,0:T(8,128)(2,1)} %shard_map.166.q_ref), channel_id=1, source_target_pairs={{0,4},{2,6},{4,0},{6,2},{8,12},{10,14},{12,8},{14,10},{1,5},{3,7},... | collective-permute-start | bytes 98312 | tf_op jit(solution)/shard_map/ppermute | solution.py:42
  6.9 4.5 %collective-permute-start.3 = (bf16[128,128]{1,0:T(8,128)(2,1)}, bf16[128,128]{1,0:T(8,128)(2,1)S(1)}, u32[]{:S(2)}, u32[]{:S(2)}) collective-permute-start(bf16[128,128]{1,0:T(8,128)(2,1)} %shard_map.166.q_ref), channel_id=1, source_target_pairs={{0,8},{2,10},{4,12},{6,14},{8,0},{10,2},{12,4},{14,6},{1,9},{3,11}... | collective-permute-start | bytes 98312 | tf_op jit(solution)/shard_map/ppermute | solution.py:42
  11.3 1.0 pad_maximum_fusion.2
  12.3 1.1 collective-permute-start.8
  13.5 1.2 pad_maximum_fusion.refs_0_
  15.6 5.2 %collective-permute-done.8 = bf16[1024,128]{1,0:T(8,128)(2,1)S(1)} collective-permute-done((bf16[1024,128]{1,0:T(8,128)(2,1)S(1)}, bf16[1024,128]{1,0:T(8,128)(2,1)S(1)}, u32[]{:S(2)}, u32[]{:S(2)}) %collective-permute-start.8) | collective-permute-done | bytes 262176 | tf_op jit(solution)/shard_map/ppermute | solution.py:42
  20.8 1.0 collective-permute-start
  22.0 1.6 %collective-permute-start.5 = (bf16[512,128]{1,0:T(8,128)(2,1)S(1)}, bf16[512,128]{1,0:T(8,128)(2,1)S(1)}, u32[]{:S(2)}, u32[]{:S(2)}) collective-permute-start(bf16[512,128]{1,0:T(8,128)(2,1)S(1)} %pad_maximum_fusion.3.refs_2_), channel_id=1, source_target_pairs={{0,16},{16,0},{32,48},{48,32},{1,17},{17,1},{33,49},{49,33},{2,18}... | collective-permute-start | bytes 393224 | tf_op jit(solution)/shard_map/ppermute | solution.py:42
  23.6 2.7 %collective-permute-start.6 = (bf16[512,128]{1,0:T(8,128)(2,1)S(1)}, bf16[512,128]{1,0:T(8,128)(2,1)S(1)}, u32[]{:S(2)}, u32[]{:S(2)}) collective-permute-start(bf16[512,128]{1,0:T(8,128)(2,1)S(1)} %pad_maximum_fusion.3.refs_2_), channel_id=1, source_target_pairs={{0,32},{16,48},{32,0},{48,16},{1,33},{17,49},{33,1},{49,17},{2,34}... | collective-permute-start | bytes 393224 | tf_op jit(solution)/shard_map/ppermute | solution.py:42
  26.4 2.0 %collective-permute-done.5.refs_3_ = bf16[512,128]{1,0:T(8,128)(2,1)S(1)} collective-permute-done((bf16[512,128]{1,0:T(8,128)(2,1)S(1)}, bf16[512,128]{1,0:T(8,128)(2,1)S(1)}, u32[]{:S(2)}, u32[]{:S(2)}) %collective-permute-start.5) | collective-permute-done | bytes 131104 | tf_op jit(solution)/shard_map/ppermute | solution.py:42
  28.4 2.8 %collective-permute-start.7 = (bf16[512,128]{1,0:T(8,128)(2,1)S(1)}, bf16[512,128]{1,0:T(8,128)(2,1)S(1)}, u32[]{:S(2)}, u32[]{:S(2)}) collective-permute-start(bf16[512,128]{1,0:T(8,128)(2,1)S(1)} %pad_maximum_fusion.3.refs_2_), channel_id=1, source_target_pairs={{0,48},{16,32},{32,16},{48,0},{1,49},{17,33},{33,17},{49,1},{2,50}... | collective-permute-start | bytes 393224 | tf_op jit(solution)/shard_map/ppermute | solution.py:42
  31.4 1.7 %collective-permute-done.6.refs_4_ = bf16[512,128]{1,0:T(8,128)(2,1)S(1)} collective-permute-done((bf16[512,128]{1,0:T(8,128)(2,1)S(1)}, bf16[512,128]{1,0:T(8,128)(2,1)S(1)}, u32[]{:S(2)}, u32[]{:S(2)}) %collective-permute-start.6) | collective-permute-done | bytes 131104 | tf_op jit(solution)/shard_map/ppermute | solution.py:42
  33.3 2.5 %collective-permute-done.7.refs_5_ = bf16[512,128]{1,0:T(8,128)(2,1)S(1)} collective-permute-done((bf16[512,128]{1,0:T(8,128)(2,1)S(1)}, bf16[512,128]{1,0:T(8,128)(2,1)S(1)}, u32[]{:S(2)}, u32[]{:S(2)}) %collective-permute-start.7) | collective-permute-done | bytes 131104 | tf_op jit(solution)/shard_map/ppermute | solution.py:42
  35.8 0.8 collective-permute-start.11
  36.6 2.1 %collective-permute-start.12 = (bf16[64,2048]{1,0:T(8,128)(2,1)S(1)}, bf16[64,2048]{1,0:T(8,128)(2,1)S(1)}, u32[]{:S(2)}, u32[]{:S(2)}) collective-permute-start(bf16[64,2048]{1,0:T(8,128)(2,1)S(1)} %bitcast.25), channel_id=1, source_target_pairs={{0,48},{16,32},{32,16},{48,0},{1,49},{17,33},{33,17},{49,1},{2,50}... | collective-permute-start | bytes 786440 | tf_op jit(solution)/shard_map/ppermute | solution.py:42
  38.8 10.3 %shard_map.167 = (bf16[2080,128]{1,0:T(8,128)(2,1)S(1)}, f32[2080,128]{1,0:T(8,128)S(1)}, f32[2080,128]{1,0:T(8,128)S(1)}, f32[2080,128]{1,0:T(8,128)S(1)}) custom-call(s32[96]{0:T(128)S(1)} %get-tuple-element.77.meta_ref, bf16[4096,128]{1,0:T(8,128)(2,1)S(1)} %pad_maximum_fusion.refs_0_, bf16[4096,128]{1,0:T(8,128)(2,1)S(1)} %collective-permute-done.1.refs_1_, ...), custom_call_target="tpu_custom_call" | custom-call | flops 2147483648 | bytes 8388608 | tf_op jit(solution)/shard_map/pallas_call | solution.py:416
  49.2 1.6 %collective-permute-done.12.refs_3_ = bf16[64,2048]{1,0:T(8,128)(2,1)S(1)} collective-permute-done((bf16[64,2048]{1,0:T(8,128)(2,1)S(1)}, bf16[64,2048]{1,0:T(8,128)(2,1)S(1)}, u32[]{:S(2)}, u32[]{:S(2)}) %collective-permute-start.12) | collective-permute-done | bytes 262176 | tf_op jit(solution)/shard_map/ppermute | solution.py:42
  50.8 1.8 %shard_map.168 = (f32[128,128]{1,0:T(8,128)S(1)}, f32[8,128]{1,0:T(8,128)S(1)}) custom-call(s32[4]{0:T(128)S(1)} %copy-done.6, bf16[128,128]{1,0:T(8,128)(2,1)S(1)} %copy-done.2, bf16[4,512,128]{2,1,0:T(8,128)(2,1)S(1)} %bitcast.21, bf16[4,512,128]{2,1,0:T(8,128)(2,1)S(1)} %bitcast.22, bf16[8,128]{1,0:T(8,128)(2,1)S(1)} %bitcast.27, bf16[8,128]{1,0:T(8,128)(2,1)S(1)} %bitcast.28), custom_call_target="tpu_custom_call" | custom-call | tf_op jit(solution)/shard_map/pallas_call | solution.py:428
  52.7 2.6 %collective-permute-done.13.refs_1_ = bf16[4096,128]{1,0:T(8,128)(2,1)S(1)} collective-permute-done((bf16[4096,128]{1,0:T(8,128)(2,1)S(1)}, bf16[4096,128]{1,0:T(8,128)(2,1)S(1)}, u32[]{:S(2)}, u32[]{:S(2)}) %collective-permute-start.13) | collective-permute-done | bytes 1048608 | tf_op jit(solution)/shard_map/ppermute | solution.py:42
  55.3 3.9 %shard_map.169 = (bf16[576,128]{1,0:T(8,128)(2,1)S(1)}, bf16[576,128]{1,0:T(8,128)(2,1)S(1)}, bf16[576,128]{1,0:T(8,128)(2,1)S(1)}, bf16[576,128]{1,0:T(8,128)(2,1)S(1)}) custom-call(s32[96]{0:T(128)S(1)} %get-tuple-element.78.meta_ref, bf16[4096,128]{1,0:T(8,128)(2,1)S(1)} %collective-permute-done.refs_0_, ...), custom_call_target="tpu_custom_call" | custom-call | flops 2147483648 | bytes 8388608 | tf_op jit(solution)/shard_map/pallas_call | solution.py:445
  59.6 3.9 %collective-permute-start.15 = (bf16[576,128]{1,0:T(8,128)(2,1)S(1)}, bf16[576,128]{1,0:T(8,128)(2,1)S(1)}, u32[]{:S(2)}, u32[]{:S(2)}) collective-permute-start(bf16[576,128]{1,0:T(8,128)(2,1)S(1)} %get-tuple-element.50), channel_id=1, source_target_pairs={{0,32},{16,48},{32,0},{48,16},{1,33},{17,49},{33,1},{49,17},{2,34}... | collective-permute-start | bytes 442376 | tf_op jit(solution)/shard_map/ppermute | solution.py:42
  64.0 1.7 %collective-permute-done.14.b = bf16[576,128]{1,0:T(8,128)(2,1)S(1)} collective-permute-done((bf16[576,128]{1,0:T(8,128)(2,1)S(1)}, bf16[576,128]{1,0:T(8,128)(2,1)S(1)}, u32[]{:S(2)}, u32[]{:S(2)}) %collective-permute-start.14) | collective-permute-done | bytes 147488 | tf_op jit(solution)/shard_map/ppermute | solution.py:42
  65.8 5.5 %collective-permute-done.15.c = bf16[576,128]{1,0:T(8,128)(2,1)S(1)} collective-permute-done((bf16[576,128]{1,0:T(8,128)(2,1)S(1)}, bf16[576,128]{1,0:T(8,128)(2,1)S(1)}, u32[]{:S(2)}, u32[]{:S(2)}) %collective-permute-start.15) | collective-permute-done | bytes 147488 | tf_op jit(solution)/shard_map/ppermute | solution.py:42
  71.2 2.9 %collective-permute-done.16.d = bf16[576,128]{1,0:T(8,128)(2,1)S(1)} collective-permute-done((bf16[576,128]{1,0:T(8,128)(2,1)S(1)}, bf16[576,128]{1,0:T(8,128)(2,1)S(1)}, u32[]{:S(2)}, u32[]{:S(2)}) %collective-permute-start.16) | collective-permute-done | bytes 147488 | tf_op jit(solution)/shard_map/ppermute | solution.py:42
  74.5 1.9 %collective-permute-start.17 = (bf16[144,128]{1,0:T(8,128)(2,1)S(1)}, bf16[144,128]{1,0:T(8,128)(2,1)S(1)}, u32[]{:S(2)}, u32[]{:S(2)}) collective-permute-start(bf16[144,128]{1,0:T(8,128)(2,1)S(1)} %get-tuple-element.53), channel_id=1, source_target_pairs={{0,4},{2,6},{4,0},{6,2},{8,12},{10,14},{12,8},{14,10},{1,5},{3,7},... | collective-permute-start | bytes 110600 | tf_op jit(solution)/shard_map/ppermute | solution.py:42
  76.4 3.7 %collective-permute-start.18 = (bf16[144,128]{1,0:T(8,128)(2,1)S(1)}, bf16[144,128]{1,0:T(8,128)(2,1)S(1)}, u32[]{:S(2)}, u32[]{:S(2)}) collective-permute-start(bf16[144,128]{1,0:T(8,128)(2,1)S(1)} %get-tuple-element.54), channel_id=1, source_target_pairs={{0,8},{2,10},{4,12},{6,14},{8,0},{10,2},{12,4},{14,6},{1,9},{3,11}... | collective-permute-start | bytes 110600 | tf_op jit(solution)/shard_map/ppermute | solution.py:42
  80.1 1.0 collective-permute-start.19
  81.1 3.2 %collective-permute-done.18.refs_2_ = bf16[144,128]{1,0:T(8,128)(2,1)S(1)} collective-permute-done((bf16[144,128]{1,0:T(8,128)(2,1)S(1)}, bf16[144,128]{1,0:T(8,128)(2,1)S(1)}, u32[]{:S(2)}, u32[]{:S(2)}) %collective-permute-start.18) | collective-permute-done | bytes 36896 | tf_op jit(solution)/shard_map/ppermute | solution.py:42
  84.3 1.9 %collective-permute-done.19.refs_3_ = bf16[144,128]{1,0:T(8,128)(2,1)S(1)} collective-permute-done((bf16[144,128]{1,0:T(8,128)(2,1)S(1)}, bf16[144,128]{1,0:T(8,128)(2,1)S(1)}, u32[]{:S(2)}, u32[]{:S(2)}) %collective-permute-start.19) | collective-permute-done | bytes 36896 | tf_op jit(solution)/shard_map/ppermute | solution.py:42
  86.5 1.2 collective-permute-done.20
  87.7 1.1 collective-permute-start.21
  88.8 1.8 %collective-permute-start.24 = (bf16[8,2048]{1,0:T(8,128)(2,1)S(1)}, bf16[8,2048]{1,0:T(8,128)(2,1)S(1)}, u32[]{:S(2)}, u32[]{:S(2)}) collective-permute-start(bf16[8,2048]{1,0:T(8,128)(2,1)S(1)} %get-tuple-element.60), channel_id=1, source_target_pairs={{0,8},{2,10},{4,12},{6,14},{8,0},{10,2},{12,4},{14,6},{1,9},{3,11}... | collective-permute-start | bytes 98312 | tf_op jit(solution)/shard_map/ppermute | solution.py:42
  90.6 1.6 %collective-permute-start.22 = (bf16[16,2048]{1,0:T(8,128)(2,1)S(1)}, bf16[16,2048]{1,0:T(8,128)(2,1)S(1)}, u32[]{:S(2)}, u32[]{:S(2)}) collective-permute-start(bf16[16,2048]{1,0:T(8,128)(2,1)S(1)} %constant_dynamic-update-slice_fusion.pair_ref), channel_id=1, source_target_pairs={{0,4},{1,13},{2,6},{3,15},{4,0},{5,9},{6,2},{7,11},{8,12},{9,5},{1... | collective-permute-start | bytes 196616 | tf_op jit(solution)/shard_map/ppermute | solution.py:482
  92.2 1.9 %collective-permute-start.23 = (bf16[16,2048]{1,0:T(8,128)(2,1)S(1)}, bf16[16,2048]{1,0:T(8,128)(2,1)S(1)}, u32[]{:S(2)}, u32[]{:S(2)}) collective-permute-start(bf16[16,2048]{1,0:T(8,128)(2,1)S(1)} %constant_dynamic-update-slice_fusion.pair_ref), channel_id=1, source_target_pairs={{0,6},{1,15},{2,4},{3,13},{4,2},{5,11},{6,0},{7,9},{8,14},{9,7},{1... | collective-permute-start | bytes 196616 | tf_op jit(solution)/shard_map/ppermute | solution.py:482
  94.0 2.9 %collective-permute-done.22 = bf16[16,2048]{1,0:T(8,128)(2,1)S(1)} collective-permute-done((bf16[16,2048]{1,0:T(8,128)(2,1)S(1)}, bf16[16,2048]{1,0:T(8,128)(2,1)S(1)}, u32[]{:S(2)}, u32[]{:S(2)}) %collective-permute-start.22) | collective-permute-done | bytes 65568 | tf_op jit(solution)/shard_map/ppermute | solution.py:482
  96.9 2.0 %collective-permute-done.23 = bf16[16,2048]{1,0:T(8,128)(2,1)S(1)} collective-permute-done((bf16[16,2048]{1,0:T(8,128)(2,1)S(1)}, bf16[16,2048]{1,0:T(8,128)(2,1)S(1)}, u32[]{:S(2)}, u32[]{:S(2)}) %collective-permute-start.23) | collective-permute-done | bytes 65568 | tf_op jit(solution)/shard_map/ppermute | solution.py:482
  98.9 1.1 collective-permute-start.25
  100.2 1.0 collective-permute-done.25.there_ref
  101.1 1.3 %shard_map.172 = (f32[64,128]{1,0:T(8,128)S(1)}, f32[64,128]{1,0:T(8,128)S(1)}, f32[64,128]{1,0:T(8,128)S(1)}, f32[64,128]{1,0:T(8,128)S(1)}) custom-call(s32[2]{0:T(128)S(1)} %pad_add_fusion.3.where_ref, bf16[16,2048]{1,0:T(8,128)(2,1)S(1)} %constant_dynamic-update-slice_fusion.pair_ref, bf16[56,2048]{1,0:T(8,128)(2,1)S(1)} %constant_dynamic-update-slice_fusion.2.here_ref, ...), custom_call_target="tpu_custom_call" | custom-call | tf_op jit(solution)/shard_map/pallas_call | solution.py:488
  102.5 2.0 %collective-permute-start.26 = (f32[64,128]{1,0:T(8,128)S(1)}, f32[64,128]{1,0:T(8,128)S(1)}, u32[]{:S(2)}, u32[]{:S(2)}) collective-permute-start(f32[64,128]{1,0:T(8,128)S(1)} %get-tuple-element.65), channel_id=1, source_target_pairs={{0,0},{16,64},{32,128},{48,192},{64,16},{80,80},{96,144},{112,208}... | collective-permute-start | bytes 98312 | tf_op jit(solution)/shard_map/ppermute | solution.py:499
  104.5 8.2 %collective-permute-start.28 = (f32[64,128]{1,0:T(8,128)S(1)}, f32[64,128]{1,0:T(8,128)S(1)}, u32[]{:S(2)}, u32[]{:S(2)}) collective-permute-start(f32[64,128]{1,0:T(8,128)S(1)} %get-tuple-element.67), channel_id=1, source_target_pairs={{0,32},{16,96},{32,160},{48,224},{64,48},{80,112},{96,176},{112,24... | collective-permute-start | bytes 98312 | tf_op jit(solution)/shard_map/ppermute | solution.py:499
  112.7 0.7 reshape.94
  113.5 0.6 copy.25
  114.3 4.7 %collective-permute-done.29.d = f32[64,128]{1,0:T(8,128)S(1)} collective-permute-done((f32[64,128]{1,0:T(8,128)S(1)}, f32[64,128]{1,0:T(8,128)S(1)}, u32[]{:S(2)}, u32[]{:S(2)}) %collective-permute-start.29) | collective-permute-done | bytes 32800 | tf_op jit(solution)/shard_map/ppermute | solution.py:499
  119.0 1.3 %shard_map.173 = f32[2,64,64]{2,1,0:T(8,128)} custom-call(s32[2]{0:T(128)S(1)} %pad_add_fusion.2.where_ref, f32[64,128]{1,0:T(8,128)S(1)} %collective-permute-done.26.a, f32[64,128]{1,0:T(8,128)S(1)} %collective-permute-done.27.b, f32[64,128]{1,0:T(8,128)S(1)} %collective-permute-done.28.c, f32[64,128]{1,0:T(8,128)S(1)} %collective-permute-done.29.d), custom_call_target="tpu_custom_call" | custom-call | tf_op jit(solution)/shard_map/pallas_call | solution.py:500
  (75 shorter events, 4.0 us)
Async XLA Ops:
  0.6 12.8 %copy-start.7 = (bf16[2048,1,128]{2,0,1:T(8,128)(2,1)S(1)}, bf16[2048,1,128]{2,0,1:T(8,128)(2,1)}, u32[]{:S(2)}) copy-start(bf16[2048,1,128]{2,0,1:T(8,128)(2,1)} %param.22) | copy-start | bytes 1572868
  3.6 18.3 %collective-permute-start.2 = (bf16[128,128]{1,0:T(8,128)(2,1)}, bf16[128,128]{1,0:T(8,128)(2,1)S(1)}, u32[]{:S(2)}, u32[]{:S(2)}) collective-permute-start(bf16[128,128]{1,0:T(8,128)(2,1)} %shard_map.166.q_ref), channel_id=1, source_target_pairs={{0,4},{2,6},{4,0},{6,2},{8,12},{10,14},{12,8},{14,10},{1,5},{3,7},... | collective-permute-start | bytes 98312 | tf_op jit(solution)/shard_map/ppermute | solution.py:42
  6.9 15.1 %collective-permute-start.3 = (bf16[128,128]{1,0:T(8,128)(2,1)}, bf16[128,128]{1,0:T(8,128)(2,1)S(1)}, u32[]{:S(2)}, u32[]{:S(2)}) collective-permute-start(bf16[128,128]{1,0:T(8,128)(2,1)} %shard_map.166.q_ref), channel_id=1, source_target_pairs={{0,8},{2,10},{4,12},{6,14},{8,0},{10,2},{12,4},{14,6},{1,9},{3,11}... | collective-permute-start | bytes 98312 | tf_op jit(solution)/shard_map/ppermute | solution.py:42
  11.3 10.6 %collective-permute-start.4 = (bf16[128,128]{1,0:T(8,128)(2,1)}, bf16[128,128]{1,0:T(8,128)(2,1)S(1)}, u32[]{:S(2)}, u32[]{:S(2)}) collective-permute-start(bf16[128,128]{1,0:T(8,128)(2,1)} %shard_map.166.q_ref), channel_id=1, source_target_pairs={{0,12},{2,14},{4,8},{6,10},{8,4},{10,6},{12,0},{14,2},{1,13},{3,15... | collective-permute-start | bytes 98312 | tf_op jit(solution)/shard_map/ppermute | solution.py:42
  12.3 2.5 %copy-start.11 = (s32[256]{0:T(256)S(1)}, s32[256]{0:T(256)}, u32[]{:S(2)}) copy-start(s32[256]{0:T(256)} %param.26) | copy-start | bytes 3076
  12.3 8.4 %collective-permute-start.8 = (bf16[1024,128]{1,0:T(8,128)(2,1)S(1)}, bf16[1024,128]{1,0:T(8,128)(2,1)S(1)}, u32[]{:S(2)}, u32[]{:S(2)}) collective-permute-start(bf16[1024,128]{1,0:T(8,128)(2,1)S(1)} %pad_maximum_fusion.2), channel_id=1, source_target_pairs={{0,2},{2,0},{4,6},{6,4},{8,10},{10,8},{12,14},{14,12},{1,3},{3,1},... | collective-permute-start | bytes 786440 | tf_op jit(solution)/shard_map/ppermute | solution.py:42
  13.4 1.5 %copy-start.10 = (s32[512]{0:T(512)S(1)}, s32[512]{0:T(512)}, u32[]{:S(2)}) copy-start(s32[512]{0:T(512)} %param.29) | copy-start | bytes 6148
  13.4 1.7 %copy-start.12 = (s32[16]{0:T(128)S(1)}, s32[16]{0:T(128)}, u32[]{:S(2)}) copy-start(s32[16]{0:T(128)} %param.27) | copy-start | bytes 196
  13.5 8.3 %copy-start.8 = (bf16[512,1,128]{2,0,1:T(8,128)(2,1)S(1)}, bf16[512,1,128]{2,0,1:T(8,128)(2,1)}, u32[]{:S(2)}) copy-start(bf16[512,1,128]{2,0,1:T(8,128)(2,1)} %param.20) | copy-start | bytes 393220
  13.5 8.3 %copy-start.9 = (bf16[512,1,128]{2,0,1:T(8,128)(2,1)S(1)}, bf16[512,1,128]{2,0,1:T(8,128)(2,1)}, u32[]{:S(2)}) copy-start(bf16[512,1,128]{2,0,1:T(8,128)(2,1)} %param.19) | copy-start | bytes 393220
  14.6 7.3 %copy-start.2 = (bf16[128,128]{1,0:T(8,128)(2,1)S(1)}, bf16[128,128]{1,0:T(8,128)(2,1)}, u32[]{:S(2)}) copy-start(bf16[128,128]{1,0:T(8,128)(2,1)} %shard_map.166.q_ref) | copy-start | bytes 98308
  14.6 18.4 %copy-start.3 = (bf16[2048,64]{0,1:T(8,128)(2,1)S(1)}, bf16[2048,64]{0,1:T(8,128)(2,1)}, u32[]{:S(2)}) copy-start(bf16[2048,64]{0,1:T(8,128)(2,1)} %param.25) | copy-start | bytes 786436
  14.7 24.1 %collective-permute-start.1 = (bf16[4096,128]{1,0:T(8,128)(2,1)S(1)}, bf16[4096,128]{1,0:T(8,128)(2,1)S(1)}, u32[]{:S(2)}, u32[]{:S(2)}) collective-permute-start(bf16[4096,128]{1,0:T(8,128)(2,1)S(1)} %pad_maximum_fusion.refs_0_), channel_id=1, source_target_pairs={{0,1},{1,0},{2,3},{3,2},{4,5},{5,4},{6,7},{7,6},{8,9},{9,8},{10,11... | collective-permute-start | bytes 3145736 | tf_op jit(solution)/shard_map/ppermute | solution.py:42
  20.8 31.8 %collective-permute-start = (bf16[4096,128]{1,0:T(8,128)(2,1)S(1)}, bf16[4096,128]{1,0:T(8,128)(2,1)S(1)}, u32[]{:S(2)}, u32[]{:S(2)}) collective-permute-start(bf16[4096,128]{1,0:T(8,128)(2,1)S(1)} %pad_maximum_fusion.refs_0_), channel_id=1, source_target_pairs={{0,2},{2,0},{4,6},{6,4},{8,10},{10,8},{12,14},{14,12},{1,3},{3,1},... | collective-permute-start | bytes 3145736 | tf_op jit(solution)/shard_map/ppermute | solution.py:42
  21.8 14.7 %collective-permute-start.9 = (bf16[2048,128]{1,0:T(8,128)(2,1)S(1)}, bf16[2048,128]{1,0:T(8,128)(2,1)S(1)}, u32[]{:S(2)}, u32[]{:S(2)}) collective-permute-start(bf16[2048,128]{1,0:T(8,128)(2,1)S(1)} %pad_maximum_fusion.1.refs_6_), channel_id=1, source_target_pairs={{0,1},{1,0},{2,3},{3,2},{4,5},{5,4},{6,7},{7,6},{8,9},{9,8},{10,11... | collective-permute-start | bytes 1572872 | tf_op jit(solution)/shard_map/ppermute | solution.py:42
  22.0 6.4 %collective-permute-start.5 = (bf16[512,128]{1,0:T(8,128)(2,1)S(1)}, bf16[512,128]{1,0:T(8,128)(2,1)S(1)}, u32[]{:S(2)}, u32[]{:S(2)}) collective-permute-start(bf16[512,128]{1,0:T(8,128)(2,1)S(1)} %pad_maximum_fusion.3.refs_2_), channel_id=1, source_target_pairs={{0,16},{16,0},{32,48},{48,32},{1,17},{17,1},{33,49},{49,33},{2,18}... | collective-permute-start | bytes 393224 | tf_op jit(solution)/shard_map/ppermute | solution.py:42
  23.6 9.4 %collective-permute-start.6 = (bf16[512,128]{1,0:T(8,128)(2,1)S(1)}, bf16[512,128]{1,0:T(8,128)(2,1)S(1)}, u32[]{:S(2)}, u32[]{:S(2)}) collective-permute-start(bf16[512,128]{1,0:T(8,128)(2,1)S(1)} %pad_maximum_fusion.3.refs_2_), channel_id=1, source_target_pairs={{0,32},{16,48},{32,0},{48,16},{1,33},{17,49},{33,1},{49,17},{2,34}... | collective-permute-start | bytes 393224 | tf_op jit(solution)/shard_map/ppermute | solution.py:42
  28.4 7.4 %collective-permute-start.7 = (bf16[512,128]{1,0:T(8,128)(2,1)S(1)}, bf16[512,128]{1,0:T(8,128)(2,1)S(1)}, u32[]{:S(2)}, u32[]{:S(2)}) collective-permute-start(bf16[512,128]{1,0:T(8,128)(2,1)S(1)} %pad_maximum_fusion.3.refs_2_), channel_id=1, source_target_pairs={{0,48},{16,32},{32,16},{48,0},{1,49},{17,33},{33,17},{49,1},{2,50}... | collective-permute-start | bytes 393224 | tf_op jit(solution)/shard_map/ppermute | solution.py:42
  33.1 16.1 %collective-permute-start.10 = (bf16[64,2048]{1,0:T(8,128)(2,1)S(1)}, bf16[64,2048]{1,0:T(8,128)(2,1)S(1)}, u32[]{:S(2)}, u32[]{:S(2)}) collective-permute-start(bf16[64,2048]{1,0:T(8,128)(2,1)S(1)} %bitcast.23), channel_id=1, source_target_pairs={{0,16},{16,0},{32,48},{48,32},{1,17},{17,1},{33,49},{49,33},{2,18}... | collective-permute-start | bytes 786440 | tf_op jit(solution)/shard_map/ppermute | solution.py:42
  35.8 13.4 %collective-permute-start.11 = (bf16[64,2048]{1,0:T(8,128)(2,1)S(1)}, bf16[64,2048]{1,0:T(8,128)(2,1)S(1)}, u32[]{:S(2)}, u32[]{:S(2)}) collective-permute-start(bf16[64,2048]{1,0:T(8,128)(2,1)S(1)} %bitcast.24), channel_id=1, source_target_pairs={{0,32},{16,48},{32,0},{48,16},{1,33},{17,49},{33,1},{49,17},{2,34}... | collective-permute-start | bytes 786440 | tf_op jit(solution)/shard_map/ppermute | solution.py:42
  36.6 14.2 %collective-permute-start.12 = (bf16[64,2048]{1,0:T(8,128)(2,1)S(1)}, bf16[64,2048]{1,0:T(8,128)(2,1)S(1)}, u32[]{:S(2)}, u32[]{:S(2)}) collective-permute-start(bf16[64,2048]{1,0:T(8,128)(2,1)S(1)} %bitcast.25), channel_id=1, source_target_pairs={{0,48},{16,32},{32,16},{48,0},{1,49},{17,33},{33,17},{49,1},{2,50}... | collective-permute-start | bytes 786440 | tf_op jit(solution)/shard_map/ppermute | solution.py:42
  38.8 12.0 %copy-start = (bf16[4,512,1,128]{3,1,2,0:T(8,128)(2,1)S(1)}, bf16[4,512,1,128]{3,1,2,0:T(8,128)(2,1)}, u32[]{:S(2)}) copy-start(bf16[4,512,1,128]{3,1,2,0:T(8,128)(2,1)} %param.23) | copy-start | bytes 1572868
  38.8 12.0 %copy-start.1 = (bf16[4,512,1,128]{3,1,2,0:T(8,128)(2,1)S(1)}, bf16[4,512,1,128]{3,1,2,0:T(8,128)(2,1)}, u32[]{:S(2)}) copy-start(bf16[4,512,1,128]{3,1,2,0:T(8,128)(2,1)} %param.24) | copy-start | bytes 1572868
  38.8 12.0 %copy-start.4 = (bf16[2,4,1,128]{3,1,2,0:T(4,128)(2,1)S(1)}, bf16[2,4,1,128]{3,1,2,0:T(4,128)(2,1)}, u32[]{:S(2)}) copy-start(bf16[2,4,1,128]{3,1,2,0:T(4,128)(2,1)} %param.17) | copy-start | bytes 6148
  38.8 12.0 %copy-start.5 = (bf16[2,4,1,128]{3,1,2,0:T(4,128)(2,1)S(1)}, bf16[2,4,1,128]{3,1,2,0:T(4,128)(2,1)}, u32[]{:S(2)}) copy-start(bf16[2,4,1,128]{3,1,2,0:T(4,128)(2,1)} %param.18) | copy-start | bytes 6148
  38.8 12.0 %copy-start.6 = (s32[4]{0:T(128)S(1)}, s32[4]{0:T(128)}, u32[]{:S(2)}) copy-start(s32[4]{0:T(128)} %length_ref.1) | copy-start | bytes 52
  52.6 2.7 %collective-permute-start.13 = (bf16[4096,128]{1,0:T(8,128)(2,1)S(1)}, bf16[4096,128]{1,0:T(8,128)(2,1)S(1)}, u32[]{:S(2)}, u32[]{:S(2)}) collective-permute-start(bf16[4096,128]{1,0:T(8,128)(2,1)S(1)} %collective-permute-done.refs_0_), channel_id=1, source_target_pairs={{0,1},{1,0},{2,3},{3,2},{4,5},{5,4},{6,7},{7,6},{8,9},{9,8},{10,11... | collective-permute-start | bytes 3145736 | tf_op jit(solution)/shard_map/ppermute | solution.py:42
  59.2 6.5 %collective-permute-start.14 = (bf16[576,128]{1,0:T(8,128)(2,1)S(1)}, bf16[576,128]{1,0:T(8,128)(2,1)S(1)}, u32[]{:S(2)}, u32[]{:S(2)}) collective-permute-start(bf16[576,128]{1,0:T(8,128)(2,1)S(1)} %get-tuple-element.49), channel_id=1, source_target_pairs={{0,16},{16,0},{32,48},{48,32},{1,17},{17,1},{33,49},{49,33},{2,18}... | collective-permute-start | bytes 442376 | tf_op jit(solution)/shard_map/ppermute | solution.py:42
  59.6 11.7 %collective-permute-start.15 = (bf16[576,128]{1,0:T(8,128)(2,1)S(1)}, bf16[576,128]{1,0:T(8,128)(2,1)S(1)}, u32[]{:S(2)}, u32[]{:S(2)}) collective-permute-start(bf16[576,128]{1,0:T(8,128)(2,1)S(1)} %get-tuple-element.50), channel_id=1, source_target_pairs={{0,32},{16,48},{32,0},{48,16},{1,33},{17,49},{33,1},{49,17},{2,34}... | collective-permute-start | bytes 442376 | tf_op jit(solution)/shard_map/ppermute | solution.py:42
  63.4 10.7 %collective-permute-start.16 = (bf16[576,128]{1,0:T(8,128)(2,1)S(1)}, bf16[576,128]{1,0:T(8,128)(2,1)S(1)}, u32[]{:S(2)}, u32[]{:S(2)}) collective-permute-start(bf16[576,128]{1,0:T(8,128)(2,1)S(1)} %get-tuple-element.51), channel_id=1, source_target_pairs={{0,48},{16,32},{32,16},{48,0},{1,49},{17,33},{33,17},{49,1},{2,50}... | collective-permute-start | bytes 442376 | tf_op jit(solution)/shard_map/ppermute | solution.py:42
  74.5 6.6 %collective-permute-start.17 = (bf16[144,128]{1,0:T(8,128)(2,1)S(1)}, bf16[144,128]{1,0:T(8,128)(2,1)S(1)}, u32[]{:S(2)}, u32[]{:S(2)}) collective-permute-start(bf16[144,128]{1,0:T(8,128)(2,1)S(1)} %get-tuple-element.53), channel_id=1, source_target_pairs={{0,4},{2,6},{4,0},{6,2},{8,12},{10,14},{12,8},{14,10},{1,5},{3,7},... | collective-permute-start | bytes 110600 | tf_op jit(solution)/shard_map/ppermute | solution.py:42
  76.4 7.9 %collective-permute-start.18 = (bf16[144,128]{1,0:T(8,128)(2,1)S(1)}, bf16[144,128]{1,0:T(8,128)(2,1)S(1)}, u32[]{:S(2)}, u32[]{:S(2)}) collective-permute-start(bf16[144,128]{1,0:T(8,128)(2,1)S(1)} %get-tuple-element.54), channel_id=1, source_target_pairs={{0,8},{2,10},{4,12},{6,14},{8,0},{10,2},{12,4},{14,6},{1,9},{3,11}... | collective-permute-start | bytes 110600 | tf_op jit(solution)/shard_map/ppermute | solution.py:42
  80.1 6.1 %collective-permute-start.19 = (bf16[144,128]{1,0:T(8,128)(2,1)S(1)}, bf16[144,128]{1,0:T(8,128)(2,1)S(1)}, u32[]{:S(2)}, u32[]{:S(2)}) collective-permute-start(bf16[144,128]{1,0:T(8,128)(2,1)S(1)} %get-tuple-element.55), channel_id=1, source_target_pairs={{0,12},{2,14},{4,8},{6,10},{8,4},{10,6},{12,0},{14,2},{1,13},{3,15... | collective-permute-start | bytes 110600 | tf_op jit(solution)/shard_map/ppermute | solution.py:42
  86.4 1.3 %collective-permute-start.20 = (bf16[8,2048]{1,0:T(8,128)(2,1)S(1)}, bf16[8,2048]{1,0:T(8,128)(2,1)S(1)}, u32[]{:S(2)}, u32[]{:S(2)}) collective-permute-start(bf16[8,2048]{1,0:T(8,128)(2,1)S(1)} %get-tuple-element.60), channel_id=1, source_target_pairs={{0,1},{1,0},{2,3},{3,2},{4,5},{5,4},{6,7},{7,6},{8,9},{9,8},{10,11... | collective-permute-start | bytes 98312 | tf_op jit(solution)/shard_map/ppermute | solution.py:42
  87.7 6.3 %collective-permute-start.21 = (bf16[16,2048]{1,0:T(8,128)(2,1)S(1)}, bf16[16,2048]{1,0:T(8,128)(2,1)S(1)}, u32[]{:S(2)}, u32[]{:S(2)}) collective-permute-start(bf16[16,2048]{1,0:T(8,128)(2,1)S(1)} %constant_dynamic-update-slice_fusion.pair_ref), channel_id=1, source_target_pairs={{0,2},{1,11},{2,0},{3,9},{4,6},{5,15},{6,4},{7,13},{8,10},{9,3},{1... | collective-permute-start | bytes 196616 | tf_op jit(solution)/shard_map/ppermute | solution.py:482
  88.8 10.2 %collective-permute-start.24 = (bf16[8,2048]{1,0:T(8,128)(2,1)S(1)}, bf16[8,2048]{1,0:T(8,128)(2,1)S(1)}, u32[]{:S(2)}, u32[]{:S(2)}) collective-permute-start(bf16[8,2048]{1,0:T(8,128)(2,1)S(1)} %get-tuple-element.60), channel_id=1, source_target_pairs={{0,8},{2,10},{4,12},{6,14},{8,0},{10,2},{12,4},{14,6},{1,9},{3,11}... | collective-permute-start | bytes 98312 | tf_op jit(solution)/shard_map/ppermute | solution.py:42
  90.6 6.3 %collective-permute-start.22 = (bf16[16,2048]{1,0:T(8,128)(2,1)S(1)}, bf16[16,2048]{1,0:T(8,128)(2,1)S(1)}, u32[]{:S(2)}, u32[]{:S(2)}) collective-permute-start(bf16[16,2048]{1,0:T(8,128)(2,1)S(1)} %constant_dynamic-update-slice_fusion.pair_ref), channel_id=1, source_target_pairs={{0,4},{1,13},{2,6},{3,15},{4,0},{5,9},{6,2},{7,11},{8,12},{9,5},{1... | collective-permute-start | bytes 196616 | tf_op jit(solution)/shard_map/ppermute | solution.py:482
  92.2 6.8 %collective-permute-start.23 = (bf16[16,2048]{1,0:T(8,128)(2,1)S(1)}, bf16[16,2048]{1,0:T(8,128)(2,1)S(1)}, u32[]{:S(2)}, u32[]{:S(2)}) collective-permute-start(bf16[16,2048]{1,0:T(8,128)(2,1)S(1)} %constant_dynamic-update-slice_fusion.pair_ref), channel_id=1, source_target_pairs={{0,6},{1,15},{2,4},{3,13},{4,2},{5,11},{6,0},{7,9},{8,14},{9,7},{1... | collective-permute-start | bytes 196616 | tf_op jit(solution)/shard_map/ppermute | solution.py:482
  98.9 2.2 %collective-permute-start.25 = (bf16[56,2048]{1,0:T(8,128)(2,1)S(1)}, bf16[56,2048]{1,0:T(8,128)(2,1)S(1)}, u32[]{:S(2)}, u32[]{:S(2)}) collective-permute-start(bf16[56,2048]{1,0:T(8,128)(2,1)S(1)} %constant_dynamic-update-slice_fusion.2.here_ref), channel_id=1, source_target_pairs={{0,1},{1,0},{2,3},{3,2},{4,5},{5,4},{6,7},{7,6},{8,9},{9,8},{10,11... | collective-permute-start | bytes 688136 | tf_op jit(solution)/shard_map/ppermute | solution.py:42
  102.5 11.7 %collective-permute-start.26 = (f32[64,128]{1,0:T(8,128)S(1)}, f32[64,128]{1,0:T(8,128)S(1)}, u32[]{:S(2)}, u32[]{:S(2)}) collective-permute-start(f32[64,128]{1,0:T(8,128)S(1)} %get-tuple-element.65), channel_id=1, source_target_pairs={{0,0},{16,64},{32,128},{48,192},{64,16},{80,80},{96,144},{112,208}... | collective-permute-start | bytes 98312 | tf_op jit(solution)/shard_map/ppermute | solution.py:499
  104.4 9.7 %collective-permute-start.27 = (f32[64,128]{1,0:T(8,128)S(1)}, f32[64,128]{1,0:T(8,128)S(1)}, u32[]{:S(2)}, u32[]{:S(2)}) collective-permute-start(f32[64,128]{1,0:T(8,128)S(1)} %get-tuple-element.66), channel_id=1, source_target_pairs={{0,16},{16,80},{32,144},{48,208},{64,0},{80,64},{96,128},{112,192}... | collective-permute-start | bytes 98312 | tf_op jit(solution)/shard_map/ppermute | solution.py:499
  104.5 9.8 %collective-permute-start.28 = (f32[64,128]{1,0:T(8,128)S(1)}, f32[64,128]{1,0:T(8,128)S(1)}, u32[]{:S(2)}, u32[]{:S(2)}) collective-permute-start(f32[64,128]{1,0:T(8,128)S(1)} %get-tuple-element.67), channel_id=1, source_target_pairs={{0,32},{16,96},{32,160},{48,224},{64,48},{80,112},{96,176},{112,24... | collective-permute-start | bytes 98312 | tf_op jit(solution)/shard_map/ppermute | solution.py:499
  112.7 6.3 %collective-permute-start.29 = (f32[64,128]{1,0:T(8,128)S(1)}, f32[64,128]{1,0:T(8,128)S(1)}, u32[]{:S(2)}, u32[]{:S(2)}) collective-permute-start(f32[64,128]{1,0:T(8,128)S(1)} %get-tuple-element.68), channel_id=1, source_target_pairs={{0,48},{16,112},{32,176},{48,240},{64,32},{80,96},{96,160},{112,22... | collective-permute-start | bytes 98312 | tf_op jit(solution)/shard_map/ppermute | solution.py:499

commit v3 on v2

--- a/solution.py
+++ b/solution.py
@@ -26,9 +26,9 @@
 EXP2 = SCALE * math.log2(math.e)
 ITEM = 4
 BATCH = 8
-SLOTS = 16
+SLOTS = 8
 ROOT = 512
-HELD = SLOTS // 2 * BLK
+HELD = SLOTS * BLK
 CHUNKS = 4
 QUARTER = NEAR * PIECE
 VMEM = pl.BlockSpec(memory_space=pltpu.VMEM)
@@ -87,8 +87,12 @@
     return out, top + jnp.log(total)
 
 
-def norm_kernel(q_ref, gain_ref, out_ref):
-    x = q_ref[...].astype(f32)
+def norm_kernel(q_ref, gain_ref, out_ref, rows):
+    for s in range(STEPS):
+        for h in range(GROUP):
+            x = q_ref[s, :, h * HD:(h + 1) * HD].astype(f32)
+            rows[pl.ds(s * GROUP + h, OWN, stride=REQ_ROWS), :] = x
+    x = rows[...]
     mean_square = jnp.mean(x * x, axis=-1, keepdims=True)
     out_ref[...] = (x * lax.rsqrt(mean_square + 1e-06) * gain_ref[...]).astype(bf16)
 
@@ -126,25 +130,27 @@
 
 
 def shared_kernel(second, meta_ref, *refs):
-    limbs, refs = refs[:2], refs[2:]
+    count = CHUNKS - 1 if second else 1
+    slots = count * SLOTS
+    limbs, refs = refs[:count], refs[count:]
     if second:
         before, outs = refs[:4], refs[4:4 + NX]
         q_all, acc, top_all, sum_all = refs[4 + NX:8 + NX]
         refs = refs[8 + NX:]
     else:
-        qs, roots = refs[:NX], refs[NX:NX + 2]
-        q_all, acc, top_all, sum_all = refs[2 + NX:6 + NX]
-        refs = refs[6 + NX:]
+        qs, roots = refs[:NX], refs[NX:NX + CHUNKS]
+        q_all, acc, top_all, sum_all = refs[NX + CHUNKS:NX + CHUNKS + 4]
+        refs = refs[NX + CHUNKS + 4:]
     item_block, item_part, held, part, part_top, part_sum, sems = refs
 
     copies = []
-    for n in range(2):
+    for n in range(count):
         copies.append(
             pltpu.make_async_copy(limbs[n], held.at[pl.ds(n * 2 * HELD, 2 * HELD)], sems.at[n])
         )
     if second:
         for n, (src, dst) in enumerate(zip(before, (q_all, acc, top_all, sum_all))):
-            copies.append(pltpu.make_async_copy(src, dst, sems.at[2 + n]))
+            copies.append(pltpu.make_async_copy(src, dst, sems.at[count + n]))
     for copy in copies:
         copy.start()
 
@@ -159,7 +165,7 @@
         lax.fori_loop(0, parts, put, 0)
         return n + parts
 
-    items = lax.fori_loop(0, SLOTS, list_block, 0)
+    items = lax.fori_loop(0, slots, list_block, 0)
     for u in range(BATCH - 1):
         item_block[items + u] = 0
         item_part[items + u] = LOCAL
@@ -171,11 +177,8 @@
         acc[spare, :] = jnp.zeros((REQ_ROWS, HD), f32)
         top_all[spare, :] = jnp.zeros((REQ_ROWS, HD), f32)
         sum_all[spare, :] = jnp.ones((REQ_ROWS, HD), f32)
-        keys, values = [], []
-        for ref in roots:
-            for n in range(CHUNKS // 2):
-                keys.append(ref.at[pl.ds(2 * n * ROOT, ROOT)])
-                values.append(ref.at[pl.ds((2 * n + 1) * ROOT, ROOT)])
+        keys = [ref.at[pl.ds(0, ROOT)] for ref in roots]
+        values = [ref.at[pl.ds(ROOT, ROOT)] for ref in roots]
         for g, q_ref in enumerate(qs):
 
             def root_tile(t, carry):
@@ -198,7 +201,7 @@
         copy.wait()
 
     def request_rows(block, index):
-        place = meta_ref[LOCAL + SLOTS + block] + index
+        place = meta_ref[LOCAL + slots + block] + index
         found = meta_ref[jnp.minimum(place, LOCAL - 1)]
         request = jnp.where(index < meta_ref[LOCAL + block], found, LOCAL)
         return pl.ds(pl.multiple_of(request * REQ_ROWS, REQ_ROWS), REQ_ROWS)
@@ -334,9 +337,9 @@
 
 def plan(request_branch, branch_blocks, block_slot, x, z, core):
     leaf = (x * NZ + z) * 2 + core
-    here = SLOTS // 2
+    here = SLOTS
     block_ids = jnp.arange(block_slot.shape[0], dtype=jnp.int32)
-    j = jnp.arange(2 * SLOTS, dtype=jnp.int32)
+    j = jnp.arange(CHUNKS * SLOTS, dtype=jnp.int32)
     slot_ids = (leaf ^ (j >> 3)) * here + (j & (here - 1))
     slot_block = jnp.sum(
         jnp.where(block_slot[:, None] == slot_ids[None, :], block_ids[:, None], 0), axis=0
@@ -358,7 +361,7 @@
     start = jnp.sum((branch[None, :] < slot_branch[:, None]).astype(jnp.int32), axis=1)
     return [
         jnp.concatenate([ordered, count[half], start[half]]).astype(jnp.int32)
-        for half in (slice(0, SLOTS), slice(SLOTS, 2 * SLOTS))
+        for half in (slice(0, SLOTS), slice(SLOTS, CHUNKS * SLOTS))
     ]
 
 
@@ -384,44 +387,48 @@
     block_slot,
 ):
     kv, x, z, core = (lax.axis_index(name) for name in ("kv", "x", "z", "core"))
-    raw = queries.reshape(STEPS, OWN, GROUP, HD).transpose(1, 0, 2, 3).reshape(PIECE, HD)
     normed = pl.pallas_call(
-        norm_kernel, out_shape=struct((PIECE, HD), bf16), in_specs=[VMEM, VMEM], out_specs=VMEM
-    )(raw, query_gain.reshape(1, HD))
+        norm_kernel,
+        out_shape=struct((PIECE, HD), bf16),
+        in_specs=[VMEM, VMEM],
+        out_specs=VMEM,
+        scratch_shapes=[pltpu.VMEM((PIECE, HD), f32)],
+    )(queries.reshape(STEPS, OWN, GROUP * HD), query_gain.reshape(1, HD))
+    root = jnp.concatenate([root_keys.reshape(ROOT, HD), root_values.reshape(ROOT, HD)], 0)
+    limb = jnp.concatenate([branch_keys.reshape(HELD, HD), branch_values.reshape(HELD, HD)], 0)
+    side_root, limb = lax.optimization_barrier((swap(root, "core", 2, 1), limb))
+    far_root, far = swap(root, "z", NZ, 1), swap(limb, "z", NZ, 1)
     near = jnp.concatenate([normed] + [swap(normed, "z", NZ, 2 * k) for k in range(1, NEAR)], 0)
     quarters = [near] + [swap(near, "x", NX, k) for k in range(1, NX)]
 
-    root = jnp.concatenate([root_keys.reshape(ROOT, HD), root_values.reshape(ROOT, HD)], 0)
-    limb = jnp.concatenate([branch_keys.reshape(HELD, HD), branch_values.reshape(HELD, HD)], 0)
-    far = swap(limb, "z", NZ, 1)
-    roots = jnp.concatenate([root, swap(root, "z", NZ, 1)], 0)
-    roots = [roots, swap(roots, "core", 2, 1)]
-    limbs = [limb, swap(limb, "core", 2, 1)]
+    roots = [root, far_root, side_root, swap(far_root, "core", 2, 1)]
+    quarters[2], side = lax.optimization_barrier((quarters[2], limb))
+    side = swap(side, "core", 2, 1)
     meta = plan(request_branch, branch_blocks, block_slot, x, z, core)
 
     rows = LOCAL * REQ_ROWS
     spare = rows + REQ_ROWS
     state = [struct((spare, HD), bf16)] + [struct((spare, HD), f32)] * 3
-    most = SLOTS * LOCAL // ITEM + BATCH
-    scratch = [
-        pltpu.SMEM((most,), jnp.int32),
-        pltpu.SMEM((most,), jnp.int32),
-        pltpu.VMEM((4 * HELD, HD), bf16),
-    ]
-    scratch += [pltpu.VMEM((BATCH, ITEM * REQ_ROWS, HD), f32)] * 3
-    scratch += [pltpu.SemaphoreType.DMA((6,))]
+
+    def scratch(count):
+        most = count * SLOTS * LOCAL // ITEM + BATCH
+        lists = [pltpu.SMEM((most,), jnp.int32)] * 2
+        parts = [pltpu.VMEM((BATCH, ITEM * REQ_ROWS, HD), f32)] * 3
+        held = [pltpu.VMEM((count * 2 * HELD, HD), bf16)]
+        return lists + held + parts + [pltpu.SemaphoreType.DMA((CHUNKS + 3,))]
+
     cost = pl.CostEstimate(
         flops=4 * rows * HD * 2048, bytes_accessed=8 << 20, transcendentals=rows * 2048
     )
     before = pl.pallas_call(
         functools.partial(shared_kernel, False),
         out_shape=state,
-        in_specs=[SMEM] + [ANY] * 2 + [VMEM] * (NX + 2),
+        in_specs=[SMEM] + [ANY] + [VMEM] * (NX + CHUNKS),
         out_specs=[VMEM] * 4,
-        scratch_shapes=scratch,
+        scratch_shapes=scratch(1),
         compiler_params=PARAMS,
         cost_estimate=cost,
-    )(meta[0], *limbs, *quarters, *roots)
+    )(meta[0], limb, *quarters, *roots)
     turned = out_weight.T
     weights = [turned] + [swap(turned, "x", NX, k) for k in range(1, NX)]
     before, weights, tied = lax.optimization_barrier((before, weights, normed))
@@ -441,16 +448,16 @@
     )
 
     far, own, own_lse = lax.optimization_barrier((far, own, own_lse))
-    far = [far, swap(far, "core", 2, 1)]
+    limbs = [side, far, swap(far, "core", 2, 1)]
     partials = pl.pallas_call(
         functools.partial(shared_kernel, True),
         out_shape=[struct((NEAR * PACK, HD), bf16)] * NX,
-        in_specs=[SMEM] + [ANY] * 6,
+        in_specs=[SMEM] + [ANY] * (CHUNKS + 3),
         out_specs=[VMEM] * NX,
-        scratch_shapes=[pltpu.VMEM(part.shape, part.dtype) for part in state] + scratch,
+        scratch_shapes=[pltpu.VMEM(part.shape, part.dtype) for part in state] + scratch(CHUNKS - 1),
         compiler_params=PARAMS,
         cost_estimate=cost,
-    )(meta[1], *far, *before)
+    )(meta[1], *limbs, *before)
     returned = [partials[0]] + [swap(partials[k], "x", NX, k) for k in range(1, NX)]
     merged = pl.pallas_call(
         merge_kernel,

time: 121 us -> 114 us (0.942); the launches traced: 120 us -> 115 us
  waiting for transfers between devices: 42.7 us -> 37.7 us
  local copies, waits for them, and re-layouts: 3.05 us -> 1.63 us
    ppermute x23 -> x24, waiting for transfers between devices: 32.9 us -> 27.8 us  [swap(): return lax.ppermute(a, axis, [(i, i ^ k) for i in range(n)])]
    pallas_call x1, Pallas kernels: 10.3 us -> 8.08 us  [shards(): pl.pallas_call(functools.partial(shared_kernel, False), out_shape=state,...]
    pallas_call x1, Pallas kernels: 3.93 us -> 6.13 us  [shards(): pl.pallas_call(functools.partial(shared_kernel, True), out_shape=[struct(...]
    reshape x2 -> x0, local copies, waits for them, and re-layouts: 1.46 us -> none  [shards(): queries.reshape(STEPS, OWN, GROUP, HD).transpose(1, 0, 2, 3)]
    ppermute x23 -> x24, starting transfers between devices: 34.7 us -> 35.3 us  [swap(): return lax.ppermute(a, axis, [(i, i ^ k) for i in range(n)])]
  transfers between devices with their start and end apart: 30 -> 31, of which waited for: 17 -> 18; matrix products, arithmetic and copies ran while one was open for 4% -> 5% of each run, Pallas kernels for 10% -> 9%
where the time goes in v3:
time: 114 us; the launch traced here: 115 us
  starting transfers between devices  50.1 us (44%)
  waiting for transfers between devices  37.7 us (33%)
  Pallas kernels  20.8 us (18%)
  other arithmetic  3.62 us (3%)
  local copies, waits for them, and re-layouts  1.63 us (1%)
    ppermute x24, starting transfers between devices, swap(): return lax.ppermute(a, axis, [(i, i ^ k) for i in range(n)])  35.3 us
    ppermute x24, waiting for transfers between devices, swap(): return lax.ppermute(a, axis, [(i, i ^ k) for i in range(n)])  27.8 us
    ppermute x4, starting transfers between devices, shards(): arrived.append(lax.ppermute(terms[k], ('kv', 'x'), pairs))  11.3 us
    pallas_call x1, Pallas kernels, shards(): pl.pallas_call(functools.partial(shared_kernel, False), out_shape=state,...  8.08 us
    pallas_call x1, Pallas kernels, shards(): pl.pallas_call(functools.partial(shared_kernel, True), out_shape=[struct(...  6.13 us
    ppermute x3, waiting for transfers between devices, shards(): fetched.append(lax.ppermute(pair, ('z', 'core'), moves))  5.03 us
    ppermute x4, waiting for transfers between devices, shards(): arrived.append(lax.ppermute(terms[k], ('kv', 'x'), pairs))  4.89 us
    ppermute x3, starting transfers between devices, shards(): fetched.append(lax.ppermute(pair, ('z', 'core'), moves))  3.56 us
  transfers between devices with their start and end apart: 31, of which 18 were waited for; matrix products, arithmetic and copies ran while one was open for 5% of the time, Pallas kernels for 9%

profile of v3, /device:TPU:40, one launch (start us, length us, event | category | flops | bytes accessed | tf_op | source)
XLA Modules:
  0.0 114.7 jit_solution(2817983089052967412)
XLA Ops:
  0.6 1.5 %shard_map.166.q_ref = bf16[128,128]{1,0:T(8,128)(2,1)} custom-call(bf16[2,4,2048]{2,1,0:T(4,128)(2,1)} %bitcast.31, f32[1,128]{1,0:T(1,128)} %bitcast.35), custom_call_target="tpu_custom_call" | custom-call | tf_op jit(solution)/shard_map/pallas_call | solution.py:390
  2.1 5.4 %collective-permute-start.2 = (bf16[128,128]{1,0:T(8,128)(2,1)}, bf16[128,128]{1,0:T(8,128)(2,1)S(1)}, u32[]{:S(2)}, u32[]{:S(2)}) collective-permute-start(bf16[128,128]{1,0:T(8,128)(2,1)} %shard_map.166.q_ref), channel_id=1, source_target_pairs={{0,12},{2,14},{4,8},{6,10},{8,4},{10,6},{12,0},{14,2},{1,13},{3,15... | collective-permute-start | bytes 98312 | tf_op jit(solution)/shard_map/ppermute | solution.py:42
  7.6 1.4 %collective-permute-start.1 = (bf16[128,128]{1,0:T(8,128)(2,1)}, bf16[128,128]{1,0:T(8,128)(2,1)S(1)}, u32[]{:S(2)}, u32[]{:S(2)}) collective-permute-start(bf16[128,128]{1,0:T(8,128)(2,1)} %shard_map.166.q_ref), channel_id=1, source_target_pairs={{0,8},{2,10},{4,12},{6,14},{8,0},{10,2},{12,4},{14,6},{1,9},{3,11}... | collective-permute-start | bytes 98312 | tf_op jit(solution)/shard_map/ppermute | solution.py:42
  9.0 0.9 collective-permute-start
  9.9 1.0 pad_maximum_fusion.1.refs_5_
  11.0 1.1 collective-permute-start.9
  12.1 1.3 %pad_maximum_fusion.refs_0_ = bf16[4096,128]{1,0:T(8,128)(2,1)S(1)} fusion(bf16[2048,128]{1,0:T(8,128)(2,1)} %bitcast.27, bf16[2048,128]{1,0:T(8,128)(2,1)} %bitcast.28), kind=kLoop, calls=%fused_computation | loop fusion | flops 2097152 | bytes 2097152 | tf_op jit(solution)/shard_map/concatenate | solution.py:398
  13.9 1.1 collective-permute-start.6
  15.3 0.7 collective-permute-done.1
  16.1 3.1 %collective-permute-start.3 = (bf16[512,128]{1,0:T(8,128)(2,1)S(1)}, bf16[512,128]{1,0:T(8,128)(2,1)S(1)}, u32[]{:S(2)}, u32[]{:S(2)}) collective-permute-start(bf16[512,128]{1,0:T(8,128)(2,1)S(1)} %pad_maximum_fusion.2.refs_1_), channel_id=1, source_target_pairs={{0,32},{16,48},{32,0},{48,16},{1,33},{17,49},{33,1},{49,17},{2,34}... | collective-permute-start | bytes 393224 | tf_op jit(solution)/shard_map/ppermute | solution.py:42
  19.2 0.6 collective-permute-start.7
  19.8 0.6 collective-permute-start.8
  20.8 3.1 %collective-permute-done.3.refs_3_ = bf16[512,128]{1,0:T(8,128)(2,1)S(1)} collective-permute-done((bf16[512,128]{1,0:T(8,128)(2,1)S(1)}, bf16[512,128]{1,0:T(8,128)(2,1)S(1)}, u32[]{:S(2)}, u32[]{:S(2)}) %collective-permute-start.3) | collective-permute-done | bytes 131104 | tf_op jit(solution)/shard_map/ppermute | solution.py:42
  24.0 1.3 %collective-permute-start.11 = (bf16[64,2048]{1,0:T(8,128)(2,1)S(1)}, bf16[64,2048]{1,0:T(8,128)(2,1)S(1)}, u32[]{:S(2)}, u32[]{:S(2)}) collective-permute-start(bf16[64,2048]{1,0:T(8,128)(2,1)S(1)} %bitcast.21), channel_id=1, source_target_pairs={{0,16},{16,0},{32,48},{48,32},{1,17},{17,1},{33,49},{49,33},{2,18}... | collective-permute-start | bytes 786440 | tf_op jit(solution)/shard_map/ppermute | solution.py:42
  25.3 0.9 collective-permute-done.7.refs_2_
  26.2 1.8 %collective-permute-start.12 = (bf16[64,2048]{1,0:T(8,128)(2,1)S(1)}, bf16[64,2048]{1,0:T(8,128)(2,1)S(1)}, u32[]{:S(2)}, u32[]{:S(2)}) collective-permute-start(bf16[64,2048]{1,0:T(8,128)(2,1)S(1)} %bitcast.22), channel_id=1, source_target_pairs={{0,32},{16,48},{32,0},{48,16},{1,33},{17,49},{33,1},{49,17},{2,34}... | collective-permute-start | bytes 786440 | tf_op jit(solution)/shard_map/ppermute | solution.py:42
  27.9 2.3 %collective-permute-start.13 = (bf16[64,2048]{1,0:T(8,128)(2,1)S(1)}, bf16[64,2048]{1,0:T(8,128)(2,1)S(1)}, u32[]{:S(2)}, u32[]{:S(2)}) collective-permute-start(bf16[64,2048]{1,0:T(8,128)(2,1)S(1)} %bitcast.23), channel_id=1, source_target_pairs={{0,48},{16,32},{32,16},{48,0},{1,49},{17,33},{33,17},{49,1},{2,50}... | collective-permute-start | bytes 786440 | tf_op jit(solution)/shard_map/ppermute | solution.py:42
  30.6 8.1 %shard_map.167 = (bf16[2080,128]{1,0:T(8,128)(2,1)S(1)}, f32[2080,128]{1,0:T(8,128)S(1)}, f32[2080,128]{1,0:T(8,128)S(1)}, f32[2080,128]{1,0:T(8,128)S(1)}) custom-call(s32[80]{0:T(128)S(1)} %pad_add_fusion.1.meta_ref, bf16[4096,128]{1,0:T(8,128)(2,1)S(1)} %pad_maximum_fusion.refs_0_, bf16[512,128]{1,0:T(8,128)(2,1)S(1)} %pad_maximum_fusion.2.refs_1_, ...), custom_call_target="tpu_custom_call" | custom-call | flops 2147483648 | bytes 8388608 | tf_op jit(solution)/shard_map/pallas_call | solution.py:423
  38.7 1.5 %collective-permute-done.13.refs_3_ = bf16[64,2048]{1,0:T(8,128)(2,1)S(1)} collective-permute-done((bf16[64,2048]{1,0:T(8,128)(2,1)S(1)}, bf16[64,2048]{1,0:T(8,128)(2,1)S(1)}, u32[]{:S(2)}, u32[]{:S(2)}) %collective-permute-start.13) | collective-permute-done | bytes 262176 | tf_op jit(solution)/shard_map/ppermute | solution.py:42
  40.2 1.8 %shard_map.168 = (f32[128,128]{1,0:T(8,128)S(1)}, f32[8,128]{1,0:T(8,128)S(1)}) custom-call(s32[4]{0:T(128)S(1)} %copy-done.6, bf16[128,128]{1,0:T(8,128)(2,1)S(1)} %copy-done.2, bf16[4,512,128]{2,1,0:T(8,128)(2,1)S(1)} %bitcast.19, bf16[4,512,128]{2,1,0:T(8,128)(2,1)S(1)} %bitcast.20, bf16[8,128]{1,0:T(8,128)(2,1)S(1)} %bitcast.25, bf16[8,128]{1,0:T(8,128)(2,1)S(1)} %bitcast.26), custom_call_target="tpu_custom_call" | custom-call | tf_op jit(solution)/shard_map/pallas_call | solution.py:435
  42.0 0.6 collective-permute-done.6.refs_1_
  42.8 2.4 %collective-permute-done.14.refs_2_ = bf16[4096,128]{1,0:T(8,128)(2,1)S(1)} collective-permute-done((bf16[4096,128]{1,0:T(8,128)(2,1)S(1)}, bf16[4096,128]{1,0:T(8,128)(2,1)S(1)}, u32[]{:S(2)}, u32[]{:S(2)}) %collective-permute-start.14) | collective-permute-done | bytes 1048608 | tf_op jit(solution)/shard_map/ppermute | solution.py:42
  45.2 6.1 %shard_map.169 = (bf16[576,128]{1,0:T(8,128)(2,1)S(1)}, bf16[576,128]{1,0:T(8,128)(2,1)S(1)}, bf16[576,128]{1,0:T(8,128)(2,1)S(1)}, bf16[576,128]{1,0:T(8,128)(2,1)S(1)}) custom-call(s32[112]{0:T(128)S(1)} %pad_add_fusion.meta_ref, bf16[4096,128]{1,0:T(8,128)(2,1)S(1)} %collective-permute-done.5.refs_0_, ...), custom_call_target="tpu_custom_call" | custom-call | flops 2147483648 | bytes 8388608 | tf_op jit(solution)/shard_map/pallas_call | solution.py:452
  51.4 2.6 %collective-permute-start.15 = (bf16[576,128]{1,0:T(8,128)(2,1)S(1)}, bf16[576,128]{1,0:T(8,128)(2,1)S(1)}, u32[]{:S(2)}, u32[]{:S(2)}) collective-permute-start(bf16[576,128]{1,0:T(8,128)(2,1)S(1)} %get-tuple-element.57), channel_id=1, source_target_pairs={{0,16},{16,0},{32,48},{48,32},{1,17},{17,1},{33,49},{49,33},{2,18}... | collective-permute-start | bytes 442376 | tf_op jit(solution)/shard_map/ppermute | solution.py:42
  53.9 2.7 %collective-permute-start.16 = (bf16[576,128]{1,0:T(8,128)(2,1)S(1)}, bf16[576,128]{1,0:T(8,128)(2,1)S(1)}, u32[]{:S(2)}, u32[]{:S(2)}) collective-permute-start(bf16[576,128]{1,0:T(8,128)(2,1)S(1)} %get-tuple-element.58), channel_id=1, source_target_pairs={{0,32},{16,48},{32,0},{48,16},{1,33},{17,49},{33,1},{49,17},{2,34}... | collective-permute-start | bytes 442376 | tf_op jit(solution)/shard_map/ppermute | solution.py:42
  56.7 0.6 collective-permute-done.15.b
  57.4 6.1 %collective-permute-done.16.c = bf16[576,128]{1,0:T(8,128)(2,1)S(1)} collective-permute-done((bf16[576,128]{1,0:T(8,128)(2,1)S(1)}, bf16[576,128]{1,0:T(8,128)(2,1)S(1)}, u32[]{:S(2)}, u32[]{:S(2)}) %collective-permute-start.16) | collective-permute-done | bytes 147488 | tf_op jit(solution)/shard_map/ppermute | solution.py:42
  63.5 3.4 %collective-permute-done.17.d = bf16[576,128]{1,0:T(8,128)(2,1)S(1)} collective-permute-done((bf16[576,128]{1,0:T(8,128)(2,1)S(1)}, bf16[576,128]{1,0:T(8,128)(2,1)S(1)}, u32[]{:S(2)}, u32[]{:S(2)}) %collective-permute-start.17) | collective-permute-done | bytes 147488 | tf_op jit(solution)/shard_map/ppermute | solution.py:42
  67.2 1.7 %collective-permute-start.18 = (bf16[144,128]{1,0:T(8,128)(2,1)S(1)}, bf16[144,128]{1,0:T(8,128)(2,1)S(1)}, u32[]{:S(2)}, u32[]{:S(2)}) collective-permute-start(bf16[144,128]{1,0:T(8,128)(2,1)S(1)} %get-tuple-element.61), channel_id=1, source_target_pairs={{0,4},{2,6},{4,0},{6,2},{8,12},{10,14},{12,8},{14,10},{1,5},{3,7},... | collective-permute-start | bytes 110600 | tf_op jit(solution)/shard_map/ppermute | solution.py:42
  68.9 5.0 %collective-permute-start.19 = (bf16[144,128]{1,0:T(8,128)(2,1)S(1)}, bf16[144,128]{1,0:T(8,128)(2,1)S(1)}, u32[]{:S(2)}, u32[]{:S(2)}) collective-permute-start(bf16[144,128]{1,0:T(8,128)(2,1)S(1)} %get-tuple-element.62), channel_id=1, source_target_pairs={{0,8},{2,10},{4,12},{6,14},{8,0},{10,2},{12,4},{14,6},{1,9},{3,11}... | collective-permute-start | bytes 110600 | tf_op jit(solution)/shard_map/ppermute | solution.py:42
  74.0 2.9 %collective-permute-done.19.refs_2_ = bf16[144,128]{1,0:T(8,128)(2,1)S(1)} collective-permute-done((bf16[144,128]{1,0:T(8,128)(2,1)S(1)}, bf16[144,128]{1,0:T(8,128)(2,1)S(1)}, u32[]{:S(2)}, u32[]{:S(2)}) %collective-permute-start.19) | collective-permute-done | bytes 36896 | tf_op jit(solution)/shard_map/ppermute | solution.py:42
  76.9 3.2 %collective-permute-done.20.refs_3_ = bf16[144,128]{1,0:T(8,128)(2,1)S(1)} collective-permute-done((bf16[144,128]{1,0:T(8,128)(2,1)S(1)}, bf16[144,128]{1,0:T(8,128)(2,1)S(1)}, u32[]{:S(2)}, u32[]{:S(2)}) %collective-permute-start.20) | collective-permute-done | bytes 36896 | tf_op jit(solution)/shard_map/ppermute | solution.py:42
  80.4 1.2 %collective-permute-done.21 = bf16[8,2048]{1,0:T(8,128)(2,1)S(1)} collective-permute-done((bf16[8,2048]{1,0:T(8,128)(2,1)S(1)}, bf16[8,2048]{1,0:T(8,128)(2,1)S(1)}, u32[]{:S(2)}, u32[]{:S(2)}) %collective-permute-start.21) | collective-permute-done | bytes 32800 | tf_op jit(solution)/shard_map/ppermute | solution.py:42
  81.6 0.9 collective-permute-start.22
  82.5 1.7 %collective-permute-start.25 = (bf16[8,2048]{1,0:T(8,128)(2,1)S(1)}, bf16[8,2048]{1,0:T(8,128)(2,1)S(1)}, u32[]{:S(2)}, u32[]{:S(2)}) collective-permute-start(bf16[8,2048]{1,0:T(8,128)(2,1)S(1)} %get-tuple-element.68), channel_id=1, source_target_pairs={{0,8},{2,10},{4,12},{6,14},{8,0},{10,2},{12,4},{14,6},{1,9},{3,11}... | collective-permute-start | bytes 98312 | tf_op jit(solution)/shard_map/ppermute | solution.py:42
  84.3 0.9 collective-permute-start.23
  85.1 1.7 %collective-permute-start.24 = (bf16[16,2048]{1,0:T(8,128)(2,1)S(1)}, bf16[16,2048]{1,0:T(8,128)(2,1)S(1)}, u32[]{:S(2)}, u32[]{:S(2)}) collective-permute-start(bf16[16,2048]{1,0:T(8,128)(2,1)S(1)} %constant_dynamic-update-slice_fusion.pair_ref), channel_id=1, source_target_pairs={{0,6},{1,15},{2,4},{3,13},{4,2},{5,11},{6,0},{7,9},{8,14},{9,7},{1... | collective-permute-start | bytes 196616 | tf_op jit(solution)/shard_map/ppermute | solution.py:489
  86.9 3.0 %collective-permute-done.23 = bf16[16,2048]{1,0:T(8,128)(2,1)S(1)} collective-permute-done((bf16[16,2048]{1,0:T(8,128)(2,1)S(1)}, bf16[16,2048]{1,0:T(8,128)(2,1)S(1)}, u32[]{:S(2)}, u32[]{:S(2)}) %collective-permute-start.23) | collective-permute-done | bytes 65568 | tf_op jit(solution)/shard_map/ppermute | solution.py:489
  89.8 2.1 %collective-permute-done.24 = bf16[16,2048]{1,0:T(8,128)(2,1)S(1)} collective-permute-done((bf16[16,2048]{1,0:T(8,128)(2,1)S(1)}, bf16[16,2048]{1,0:T(8,128)(2,1)S(1)}, u32[]{:S(2)}, u32[]{:S(2)}) %collective-permute-start.24) | collective-permute-done | bytes 65568 | tf_op jit(solution)/shard_map/ppermute | solution.py:489
  91.9 1.4 %collective-permute-start.26 = (bf16[56,2048]{1,0:T(8,128)(2,1)S(1)}, bf16[56,2048]{1,0:T(8,128)(2,1)S(1)}, u32[]{:S(2)}, u32[]{:S(2)}) collective-permute-start(bf16[56,2048]{1,0:T(8,128)(2,1)S(1)} %constant_dynamic-update-slice_fusion.2.here_ref), channel_id=1, source_target_pairs={{0,1},{1,0},{2,3},{3,2},{4,5},{5,4},{6,7},{7,6},{8,9},{9,8},{10,11... | collective-permute-start | bytes 688136 | tf_op jit(solution)/shard_map/ppermute | solution.py:42
  93.5 1.0 collective-permute-done.26.there_ref
  94.5 1.3 %shard_map.172 = (f32[64,128]{1,0:T(8,128)S(1)}, f32[64,128]{1,0:T(8,128)S(1)}, f32[64,128]{1,0:T(8,128)S(1)}, f32[64,128]{1,0:T(8,128)S(1)}) custom-call(s32[2]{0:T(128)S(1)} %pad_add_fusion.3.where_ref, bf16[16,2048]{1,0:T(8,128)(2,1)S(1)} %constant_dynamic-update-slice_fusion.pair_ref, bf16[56,2048]{1,0:T(8,128)(2,1)S(1)} %constant_dynamic-update-slice_fusion.2.here_ref, ...), custom_call_target="tpu_custom_call" | custom-call | tf_op jit(solution)/shard_map/pallas_call | solution.py:495
  95.8 2.2 %collective-permute-start.27 = (f32[64,128]{1,0:T(8,128)S(1)}, f32[64,128]{1,0:T(8,128)S(1)}, u32[]{:S(2)}, u32[]{:S(2)}) collective-permute-start(f32[64,128]{1,0:T(8,128)S(1)} %get-tuple-element.73), channel_id=1, source_target_pairs={{0,0},{16,64},{32,128},{48,192},{64,16},{80,80},{96,144},{112,208}... | collective-permute-start | bytes 98312 | tf_op jit(solution)/shard_map/ppermute | solution.py:506
  98.1 9.0 %collective-permute-start.29 = (f32[64,128]{1,0:T(8,128)S(1)}, f32[64,128]{1,0:T(8,128)S(1)}, u32[]{:S(2)}, u32[]{:S(2)}) collective-permute-start(f32[64,128]{1,0:T(8,128)S(1)} %get-tuple-element.75), channel_id=1, source_target_pairs={{0,32},{16,96},{32,160},{48,224},{64,48},{80,112},{96,176},{112,24... | collective-permute-start | bytes 98312 | tf_op jit(solution)/shard_map/ppermute | solution.py:506
  107.1 0.7 reshape.90
  107.9 0.6 copy.23
  108.7 4.7 %collective-permute-done.30.d = f32[64,128]{1,0:T(8,128)S(1)} collective-permute-done((f32[64,128]{1,0:T(8,128)S(1)}, f32[64,128]{1,0:T(8,128)S(1)}, u32[]{:S(2)}, u32[]{:S(2)}) %collective-permute-start.30) | collective-permute-done | bytes 32800 | tf_op jit(solution)/shard_map/ppermute | solution.py:506
  113.4 1.3 %shard_map.173 = f32[2,64,64]{2,1,0:T(8,128)} custom-call(s32[2]{0:T(128)S(1)} %pad_add_fusion.2.where_ref, f32[64,128]{1,0:T(8,128)S(1)} %collective-permute-done.27.a, f32[64,128]{1,0:T(8,128)S(1)} %collective-permute-done.28.b, f32[64,128]{1,0:T(8,128)S(1)} %collective-permute-done.29.c, f32[64,128]{1,0:T(8,128)S(1)} %collective-permute-done.30.d), custom_call_target="tpu_custom_call" | custom-call | tf_op jit(solution)/shard_map/pallas_call | solution.py:507
  (70 shorter events, 3.3 us)
Async XLA Ops:
  2.1 13.2 %collective-permute-start.2 = (bf16[128,128]{1,0:T(8,128)(2,1)}, bf16[128,128]{1,0:T(8,128)(2,1)S(1)}, u32[]{:S(2)}, u32[]{:S(2)}) collective-permute-start(bf16[128,128]{1,0:T(8,128)(2,1)} %shard_map.166.q_ref), channel_id=1, source_target_pairs={{0,12},{2,14},{4,8},{6,10},{8,4},{10,6},{12,0},{14,2},{1,13},{3,15... | collective-permute-start | bytes 98312 | tf_op jit(solution)/shard_map/ppermute | solution.py:42
  7.6 8.5 %collective-permute-start.1 = (bf16[128,128]{1,0:T(8,128)(2,1)}, bf16[128,128]{1,0:T(8,128)(2,1)S(1)}, u32[]{:S(2)}, u32[]{:S(2)}) collective-permute-start(bf16[128,128]{1,0:T(8,128)(2,1)} %shard_map.166.q_ref), channel_id=1, source_target_pairs={{0,8},{2,10},{4,12},{6,14},{8,0},{10,2},{12,4},{14,6},{1,9},{3,11}... | collective-permute-start | bytes 98312 | tf_op jit(solution)/shard_map/ppermute | solution.py:42
  9.0 7.1 %collective-permute-start = (bf16[128,128]{1,0:T(8,128)(2,1)}, bf16[128,128]{1,0:T(8,128)(2,1)S(1)}, u32[]{:S(2)}, u32[]{:S(2)}) collective-permute-start(bf16[128,128]{1,0:T(8,128)(2,1)} %shard_map.166.q_ref), channel_id=1, source_target_pairs={{0,4},{2,6},{4,0},{6,2},{8,12},{10,14},{12,8},{14,10},{1,5},{3,7},... | collective-permute-start | bytes 98312 | tf_op jit(solution)/shard_map/ppermute | solution.py:42
  10.9 2.6 %copy-start.8 = (s32[256]{0:T(256)S(1)}, s32[256]{0:T(256)}, u32[]{:S(2)}) copy-start(s32[256]{0:T(256)} %param.26) | copy-start | bytes 3076
  10.9 2.9 %collective-permute-start.4 = (bf16[1024,128]{1,0:T(8,128)(2,1)S(1)}, bf16[1024,128]{1,0:T(8,128)(2,1)S(1)}, u32[]{:S(2)}, u32[]{:S(2)}) collective-permute-start(bf16[1024,128]{1,0:T(8,128)(2,1)S(1)} %pad_maximum_fusion.1.refs_5_), channel_id=1, source_target_pairs={{0,1},{1,0},{2,3},{3,2},{4,5},{5,4},{6,7},{7,6},{8,9},{9,8},{10,11... | collective-permute-start | bytes 786440 | tf_op jit(solution)/shard_map/ppermute | solution.py:42
  11.0 9.6 %collective-permute-start.9 = (bf16[1024,128]{1,0:T(8,128)(2,1)S(1)}, bf16[1024,128]{1,0:T(8,128)(2,1)S(1)}, u32[]{:S(2)}, u32[]{:S(2)}) collective-permute-start(bf16[1024,128]{1,0:T(8,128)(2,1)S(1)} %pad_maximum_fusion.1.refs_5_), channel_id=1, source_target_pairs={{0,2},{2,0},{4,6},{6,4},{8,10},{10,8},{12,14},{14,12},{1,3},{3,1},... | collective-permute-start | bytes 786440 | tf_op jit(solution)/shard_map/ppermute | solution.py:42
  12.1 2.9 %copy-start.7 = (s32[512]{0:T(512)S(1)}, s32[512]{0:T(512)}, u32[]{:S(2)}) copy-start(s32[512]{0:T(512)} %param.29) | copy-start | bytes 6148
  12.1 3.0 %copy-start.9 = (s32[16]{0:T(128)S(1)}, s32[16]{0:T(128)}, u32[]{:S(2)}) copy-start(s32[16]{0:T(128)} %param.27) | copy-start | bytes 196
  12.1 3.9 %copy-start.2 = (bf16[128,128]{1,0:T(8,128)(2,1)S(1)}, bf16[128,128]{1,0:T(8,128)(2,1)}, u32[]{:S(2)}) copy-start(bf16[128,128]{1,0:T(8,128)(2,1)} %shard_map.166.q_ref) | copy-start | bytes 98308
  12.1 11.9 %copy-start.3 = (bf16[2048,64]{0,1:T(8,128)(2,1)S(1)}, bf16[2048,64]{0,1:T(8,128)(2,1)}, u32[]{:S(2)}) copy-start(bf16[2048,64]{0,1:T(8,128)(2,1)} %param.25) | copy-start | bytes 786436
  13.9 28.7 %collective-permute-start.6 = (bf16[4096,128]{1,0:T(8,128)(2,1)S(1)}, bf16[4096,128]{1,0:T(8,128)(2,1)S(1)}, u32[]{:S(2)}, u32[]{:S(2)}) collective-permute-start(bf16[4096,128]{1,0:T(8,128)(2,1)S(1)} %pad_maximum_fusion.refs_0_), channel_id=1, source_target_pairs={{0,2},{2,0},{4,6},{6,4},{8,10},{10,8},{12,14},{14,12},{1,3},{3,1},... | collective-permute-start | bytes 3145736 | tf_op jit(solution)/shard_map/ppermute | solution.py:42
  16.1 7.9 %collective-permute-start.3 = (bf16[512,128]{1,0:T(8,128)(2,1)S(1)}, bf16[512,128]{1,0:T(8,128)(2,1)S(1)}, u32[]{:S(2)}, u32[]{:S(2)}) collective-permute-start(bf16[512,128]{1,0:T(8,128)(2,1)S(1)} %pad_maximum_fusion.2.refs_1_), channel_id=1, source_target_pairs={{0,32},{16,48},{32,0},{48,16},{1,33},{17,49},{33,1},{49,17},{2,34}... | collective-permute-start | bytes 393224 | tf_op jit(solution)/shard_map/ppermute | solution.py:42
  19.2 7.0 %collective-permute-start.7 = (bf16[512,128]{1,0:T(8,128)(2,1)S(1)}, bf16[512,128]{1,0:T(8,128)(2,1)S(1)}, u32[]{:S(2)}, u32[]{:S(2)}) collective-permute-start(bf16[512,128]{1,0:T(8,128)(2,1)S(1)} %pad_maximum_fusion.2.refs_1_), channel_id=1, source_target_pairs={{0,16},{16,0},{32,48},{48,32},{1,17},{17,1},{33,49},{49,33},{2,18}... | collective-permute-start | bytes 393224 | tf_op jit(solution)/shard_map/ppermute | solution.py:42
  19.8 8.2 %collective-permute-start.8 = (bf16[512,128]{1,0:T(8,128)(2,1)S(1)}, bf16[512,128]{1,0:T(8,128)(2,1)S(1)}, u32[]{:S(2)}, u32[]{:S(2)}) collective-permute-start(bf16[512,128]{1,0:T(8,128)(2,1)S(1)} %pad_maximum_fusion.2.refs_1_), channel_id=1, source_target_pairs={{0,48},{16,32},{32,16},{48,0},{1,49},{17,33},{33,17},{49,1},{2,50}... | collective-permute-start | bytes 393224 | tf_op jit(solution)/shard_map/ppermute | solution.py:42
  20.6 9.8 %collective-permute-start.10 = (bf16[1024,128]{1,0:T(8,128)(2,1)S(1)}, bf16[1024,128]{1,0:T(8,128)(2,1)S(1)}, u32[]{:S(2)}, u32[]{:S(2)}) collective-permute-start(bf16[1024,128]{1,0:T(8,128)(2,1)S(1)} %collective-permute-done.9.refs_6_), channel_id=1, source_target_pairs={{0,1},{1,0},{2,3},{3,2},{4,5},{5,4},{6,7},{7,6},{8,9},{9,8},{10,11... | collective-permute-start | bytes 786440 | tf_op jit(solution)/shard_map/ppermute | solution.py:42
  24.0 14.7 %collective-permute-start.11 = (bf16[64,2048]{1,0:T(8,128)(2,1)S(1)}, bf16[64,2048]{1,0:T(8,128)(2,1)S(1)}, u32[]{:S(2)}, u32[]{:S(2)}) collective-permute-start(bf16[64,2048]{1,0:T(8,128)(2,1)S(1)} %bitcast.21), channel_id=1, source_target_pairs={{0,16},{16,0},{32,48},{48,32},{1,17},{17,1},{33,49},{49,33},{2,18}... | collective-permute-start | bytes 786440 | tf_op jit(solution)/shard_map/ppermute | solution.py:42
  26.2 12.6 %collective-permute-start.12 = (bf16[64,2048]{1,0:T(8,128)(2,1)S(1)}, bf16[64,2048]{1,0:T(8,128)(2,1)S(1)}, u32[]{:S(2)}, u32[]{:S(2)}) collective-permute-start(bf16[64,2048]{1,0:T(8,128)(2,1)S(1)} %bitcast.22), channel_id=1, source_target_pairs={{0,32},{16,48},{32,0},{48,16},{1,33},{17,49},{33,1},{49,17},{2,34}... | collective-permute-start | bytes 786440 | tf_op jit(solution)/shard_map/ppermute | solution.py:42
  27.9 12.3 %collective-permute-start.13 = (bf16[64,2048]{1,0:T(8,128)(2,1)S(1)}, bf16[64,2048]{1,0:T(8,128)(2,1)S(1)}, u32[]{:S(2)}, u32[]{:S(2)}) collective-permute-start(bf16[64,2048]{1,0:T(8,128)(2,1)S(1)} %bitcast.23), channel_id=1, source_target_pairs={{0,48},{16,32},{32,16},{48,0},{1,49},{17,33},{33,17},{49,1},{2,50}... | collective-permute-start | bytes 786440 | tf_op jit(solution)/shard_map/ppermute | solution.py:42
  30.3 9.9 %copy-start = (bf16[4,512,1,128]{3,1,2,0:T(8,128)(2,1)S(1)}, bf16[4,512,1,128]{3,1,2,0:T(8,128)(2,1)}, u32[]{:S(2)}) copy-start(bf16[4,512,1,128]{3,1,2,0:T(8,128)(2,1)} %param.23) | copy-start | bytes 1572868
  30.3 9.9 %copy-start.1 = (bf16[4,512,1,128]{3,1,2,0:T(8,128)(2,1)S(1)}, bf16[4,512,1,128]{3,1,2,0:T(8,128)(2,1)}, u32[]{:S(2)}) copy-start(bf16[4,512,1,128]{3,1,2,0:T(8,128)(2,1)} %param.24) | copy-start | bytes 1572868
  30.3 9.9 %copy-start.4 = (bf16[2,4,1,128]{3,1,2,0:T(4,128)(2,1)S(1)}, bf16[2,4,1,128]{3,1,2,0:T(4,128)(2,1)}, u32[]{:S(2)}) copy-start(bf16[2,4,1,128]{3,1,2,0:T(4,128)(2,1)} %param.17) | copy-start | bytes 6148
  30.3 9.9 %copy-start.5 = (bf16[2,4,1,128]{3,1,2,0:T(4,128)(2,1)S(1)}, bf16[2,4,1,128]{3,1,2,0:T(4,128)(2,1)}, u32[]{:S(2)}) copy-start(bf16[2,4,1,128]{3,1,2,0:T(4,128)(2,1)} %param.18) | copy-start | bytes 6148
  30.3 9.9 %copy-start.6 = (s32[4]{0:T(128)S(1)}, s32[4]{0:T(128)}, u32[]{:S(2)}) copy-start(s32[4]{0:T(128)} %length_ref.1) | copy-start | bytes 52
  30.4 12.4 %collective-permute-start.5 = (bf16[4096,128]{1,0:T(8,128)(2,1)S(1)}, bf16[4096,128]{1,0:T(8,128)(2,1)S(1)}, u32[]{:S(2)}, u32[]{:S(2)}) collective-permute-start(bf16[4096,128]{1,0:T(8,128)(2,1)S(1)} %pad_maximum_fusion.refs_0_), channel_id=1, source_target_pairs={{0,1},{1,0},{2,3},{3,2},{4,5},{5,4},{6,7},{7,6},{8,9},{9,8},{10,11... | collective-permute-start | bytes 3145736 | tf_op jit(solution)/shard_map/ppermute | solution.py:42
  42.6 2.7 %collective-permute-start.14 = (bf16[4096,128]{1,0:T(8,128)(2,1)S(1)}, bf16[4096,128]{1,0:T(8,128)(2,1)S(1)}, u32[]{:S(2)}, u32[]{:S(2)}) collective-permute-start(bf16[4096,128]{1,0:T(8,128)(2,1)S(1)} %collective-permute-done.6.refs_1_), channel_id=1, source_target_pairs={{0,1},{1,0},{2,3},{3,2},{4,5},{5,4},{6,7},{7,6},{8,9},{9,8},{10,11... | collective-permute-start | bytes 3145736 | tf_op jit(solution)/shard_map/ppermute | solution.py:42
  51.4 6.0 %collective-permute-start.15 = (bf16[576,128]{1,0:T(8,128)(2,1)S(1)}, bf16[576,128]{1,0:T(8,128)(2,1)S(1)}, u32[]{:S(2)}, u32[]{:S(2)}) collective-permute-start(bf16[576,128]{1,0:T(8,128)(2,1)S(1)} %get-tuple-element.57), channel_id=1, source_target_pairs={{0,16},{16,0},{32,48},{48,32},{1,17},{17,1},{33,49},{49,33},{2,18}... | collective-permute-start | bytes 442376 | tf_op jit(solution)/shard_map/ppermute | solution.py:42
  53.9 9.5 %collective-permute-start.16 = (bf16[576,128]{1,0:T(8,128)(2,1)S(1)}, bf16[576,128]{1,0:T(8,128)(2,1)S(1)}, u32[]{:S(2)}, u32[]{:S(2)}) collective-permute-start(bf16[576,128]{1,0:T(8,128)(2,1)S(1)} %get-tuple-element.58), channel_id=1, source_target_pairs={{0,32},{16,48},{32,0},{48,16},{1,33},{17,49},{33,1},{49,17},{2,34}... | collective-permute-start | bytes 442376 | tf_op jit(solution)/shard_map/ppermute | solution.py:42
  56.7 10.2 %collective-permute-start.17 = (bf16[576,128]{1,0:T(8,128)(2,1)S(1)}, bf16[576,128]{1,0:T(8,128)(2,1)S(1)}, u32[]{:S(2)}, u32[]{:S(2)}) collective-permute-start(bf16[576,128]{1,0:T(8,128)(2,1)S(1)} %get-tuple-element.59), channel_id=1, source_target_pairs={{0,48},{16,32},{32,16},{48,0},{1,49},{17,33},{33,17},{49,1},{2,50}... | collective-permute-start | bytes 442376 | tf_op jit(solution)/shard_map/ppermute | solution.py:42
  67.2 6.7 %collective-permute-start.18 = (bf16[144,128]{1,0:T(8,128)(2,1)S(1)}, bf16[144,128]{1,0:T(8,128)(2,1)S(1)}, u32[]{:S(2)}, u32[]{:S(2)}) collective-permute-start(bf16[144,128]{1,0:T(8,128)(2,1)S(1)} %get-tuple-element.61), channel_id=1, source_target_pairs={{0,4},{2,6},{4,0},{6,2},{8,12},{10,14},{12,8},{14,10},{1,5},{3,7},... | collective-permute-start | bytes 110600 | tf_op jit(solution)/shard_map/ppermute | solution.py:42
  68.9 7.9 %collective-permute-start.19 = (bf16[144,128]{1,0:T(8,128)(2,1)S(1)}, bf16[144,128]{1,0:T(8,128)(2,1)S(1)}, u32[]{:S(2)}, u32[]{:S(2)}) collective-permute-start(bf16[144,128]{1,0:T(8,128)(2,1)S(1)} %get-tuple-element.62), channel_id=1, source_target_pairs={{0,8},{2,10},{4,12},{6,14},{8,0},{10,2},{12,4},{14,6},{1,9},{3,11}... | collective-permute-start | bytes 110600 | tf_op jit(solution)/shard_map/ppermute | solution.py:42
  74.0 6.1 %collective-permute-start.20 = (bf16[144,128]{1,0:T(8,128)(2,1)S(1)}, bf16[144,128]{1,0:T(8,128)(2,1)S(1)}, u32[]{:S(2)}, u32[]{:S(2)}) collective-permute-start(bf16[144,128]{1,0:T(8,128)(2,1)S(1)} %get-tuple-element.63), channel_id=1, source_target_pairs={{0,12},{2,14},{4,8},{6,10},{8,4},{10,6},{12,0},{14,2},{1,13},{3,15... | collective-permute-start | bytes 110600 | tf_op jit(solution)/shard_map/ppermute | solution.py:42
  80.3 1.3 %collective-permute-start.21 = (bf16[8,2048]{1,0:T(8,128)(2,1)S(1)}, bf16[8,2048]{1,0:T(8,128)(2,1)S(1)}, u32[]{:S(2)}, u32[]{:S(2)}) collective-permute-start(bf16[8,2048]{1,0:T(8,128)(2,1)S(1)} %get-tuple-element.68), channel_id=1, source_target_pairs={{0,1},{1,0},{2,3},{3,2},{4,5},{5,4},{6,7},{7,6},{8,9},{9,8},{10,11... | collective-permute-start | bytes 98312 | tf_op jit(solution)/shard_map/ppermute | solution.py:42
  81.6 5.3 %collective-permute-start.22 = (bf16[16,2048]{1,0:T(8,128)(2,1)S(1)}, bf16[16,2048]{1,0:T(8,128)(2,1)S(1)}, u32[]{:S(2)}, u32[]{:S(2)}) collective-permute-start(bf16[16,2048]{1,0:T(8,128)(2,1)S(1)} %constant_dynamic-update-slice_fusion.pair_ref), channel_id=1, source_target_pairs={{0,2},{1,11},{2,0},{3,9},{4,6},{5,15},{6,4},{7,13},{8,10},{9,3},{1... | collective-permute-start | bytes 196616 | tf_op jit(solution)/shard_map/ppermute | solution.py:489
  82.5 9.4 %collective-permute-start.25 = (bf16[8,2048]{1,0:T(8,128)(2,1)S(1)}, bf16[8,2048]{1,0:T(8,128)(2,1)S(1)}, u32[]{:S(2)}, u32[]{:S(2)}) collective-permute-start(bf16[8,2048]{1,0:T(8,128)(2,1)S(1)} %get-tuple-element.68), channel_id=1, source_target_pairs={{0,8},{2,10},{4,12},{6,14},{8,0},{10,2},{12,4},{14,6},{1,9},{3,11}... | collective-permute-start | bytes 98312 | tf_op jit(solution)/shard_map/ppermute | solution.py:42
  84.3 5.6 %collective-permute-start.23 = (bf16[16,2048]{1,0:T(8,128)(2,1)S(1)}, bf16[16,2048]{1,0:T(8,128)(2,1)S(1)}, u32[]{:S(2)}, u32[]{:S(2)}) collective-permute-start(bf16[16,2048]{1,0:T(8,128)(2,1)S(1)} %constant_dynamic-update-slice_fusion.pair_ref), channel_id=1, source_target_pairs={{0,4},{1,13},{2,6},{3,15},{4,0},{5,9},{6,2},{7,11},{8,12},{9,5},{1... | collective-permute-start | bytes 196616 | tf_op jit(solution)/shard_map/ppermute | solution.py:489
  85.1 6.8 %collective-permute-start.24 = (bf16[16,2048]{1,0:T(8,128)(2,1)S(1)}, bf16[16,2048]{1,0:T(8,128)(2,1)S(1)}, u32[]{:S(2)}, u32[]{:S(2)}) collective-permute-start(bf16[16,2048]{1,0:T(8,128)(2,1)S(1)} %constant_dynamic-update-slice_fusion.pair_ref), channel_id=1, source_target_pairs={{0,6},{1,15},{2,4},{3,13},{4,2},{5,11},{6,0},{7,9},{8,14},{9,7},{1... | collective-permute-start | bytes 196616 | tf_op jit(solution)/shard_map/ppermute | solution.py:489
  91.9 2.6 %collective-permute-start.26 = (bf16[56,2048]{1,0:T(8,128)(2,1)S(1)}, bf16[56,2048]{1,0:T(8,128)(2,1)S(1)}, u32[]{:S(2)}, u32[]{:S(2)}) collective-permute-start(bf16[56,2048]{1,0:T(8,128)(2,1)S(1)} %constant_dynamic-update-slice_fusion.2.here_ref), channel_id=1, source_target_pairs={{0,1},{1,0},{2,3},{3,2},{4,5},{5,4},{6,7},{7,6},{8,9},{9,8},{10,11... | collective-permute-start | bytes 688136 | tf_op jit(solution)/shard_map/ppermute | solution.py:42
  95.8 12.7 %collective-permute-start.27 = (f32[64,128]{1,0:T(8,128)S(1)}, f32[64,128]{1,0:T(8,128)S(1)}, u32[]{:S(2)}, u32[]{:S(2)}) collective-permute-start(f32[64,128]{1,0:T(8,128)S(1)} %get-tuple-element.73), channel_id=1, source_target_pairs={{0,0},{16,64},{32,128},{48,192},{64,16},{80,80},{96,144},{112,208}... | collective-permute-start | bytes 98312 | tf_op jit(solution)/shard_map/ppermute | solution.py:506
  98.0 10.5 %collective-permute-start.28 = (f32[64,128]{1,0:T(8,128)S(1)}, f32[64,128]{1,0:T(8,128)S(1)}, u32[]{:S(2)}, u32[]{:S(2)}) collective-permute-start(f32[64,128]{1,0:T(8,128)S(1)} %get-tuple-element.74), channel_id=1, source_target_pairs={{0,16},{16,80},{32,144},{48,208},{64,0},{80,64},{96,128},{112,192}... | collective-permute-start | bytes 98312 | tf_op jit(solution)/shard_map/ppermute | solution.py:506
  98.1 10.6 %collective-permute-start.29 = (f32[64,128]{1,0:T(8,128)S(1)}, f32[64,128]{1,0:T(8,128)S(1)}, u32[]{:S(2)}, u32[]{:S(2)}) collective-permute-start(f32[64,128]{1,0:T(8,128)S(1)} %get-tuple-element.75), channel_id=1, source_target_pairs={{0,32},{16,96},{32,160},{48,224},{64,48},{80,112},{96,176},{112,24... | collective-permute-start | bytes 98312 | tf_op jit(solution)/shard_map/ppermute | solution.py:506
  107.1 6.3 %collective-permute-start.30 = (f32[64,128]{1,0:T(8,128)S(1)}, f32[64,128]{1,0:T(8,128)S(1)}, u32[]{:S(2)}, u32[]{:S(2)}) collective-permute-start(f32[64,128]{1,0:T(8,128)S(1)} %get-tuple-element.76), channel_id=1, source_target_pairs={{0,48},{16,112},{32,176},{48,240},{64,32},{80,96},{96,160},{112,22... | collective-permute-start | bytes 98312 | tf_op jit(solution)/shard_map/ppermute | solution.py:506

commit v4 on v3

--- a/solution.py
+++ b/solution.py
@@ -25,7 +25,7 @@
 SCALE = 1.0 / math.sqrt(HD)
 EXP2 = SCALE * math.log2(math.e)
 ITEM = 4
-BATCH = 8
+BATCH = 16
 SLOTS = 8
 ROOT = 512
 HELD = SLOTS * BLK
@@ -312,9 +312,10 @@
             left.append(here[2 * (NEAR - 1) * one:])
             other.append(there[2 * (NEAR - 1) * one:])
     left = jnp.concatenate(left + other, 0).astype(bf16)
-    for n, weight in enumerate(weights):
-        term = nt(left, weight[...])
-        count = term.shape[0] // 2
+    every = nt(left, jnp.concatenate([weight[...] for weight in weights], 0))
+    count, columns = every.shape[0] // 2, every.shape[1] // NX
+    for n in range(NX):
+        term = every[:, n * columns:(n + 1) * columns]
         terms[n] = jnp.concatenate([term[:count], term[count:]], 1)
     for n, out in enumerate(outs):
         out[...] = terms[where_ref[0] ^ n]
@@ -324,13 +325,12 @@
     total = a[...] + b[...] + c[...] + d[...]
     columns = out.shape[2]
     first = where_ref[1] == 0
+    low = jnp.where(first, total[:, :columns], total[:, columns:])
+    high = jnp.where(first, total[:, columns:], total[:, :columns])
     for n in range(NZ):
         for s in range(STEPS):
             rows = slice(n * STEPS * OWN + s * OWN, n * STEPS * OWN + (s + 1) * OWN)
-            mine, other = total[rows, :columns], total[rows, columns:]
-            pair = jnp.concatenate(
-                [jnp.where(first, mine, other), jnp.where(first, other, mine)], 0
-            )
+            pair = jnp.concatenate([low[rows], high[rows]], 0)
             place = pl.multiple_of((where_ref[0] ^ n) * 2 * OWN, 2 * OWN)
             out[s, pl.ds(place, 2 * OWN), :] = pair
 
@@ -458,7 +458,7 @@
         compiler_params=PARAMS,
         cost_estimate=cost,
     )(meta[1], *limbs, *before)
-    returned = [partials[0]] + [swap(partials[k], "x", NX, k) for k in range(1, NX)]
+    returned = [partials[0]] + [swap(partials[k], "x", NX, k) for k in (2, 1, 3)]
     merged = pl.pallas_call(
         merge_kernel,
         out_shape=[struct((PACK, HD), bf16)] * NEAR,
@@ -466,7 +466,7 @@
         out_specs=[VMEM] * NEAR,
         compiler_params=PARAMS,
     )(*returned)
-    landed = [merged[0]] + [swap(merged[k], "z", NZ, 2 * k) for k in range(1, NEAR)]
+    landed = [merged[0]] + [swap(merged[k], "z", NZ, 2 * k) for k in (2, 1, 3)]
     attn, attn_low, lse = pl.pallas_call(
         final_kernel,
         out_shape=[

time: 114 us -> 111 us (0.974); the launches traced: 115 us -> 110 us
  waiting for transfers between devices: 37.7 us -> 33.4 us
  starting transfers between devices: 50.1 us -> 48 us
  Pallas kernels: 20.8 us -> 22 us
    ppermute x24, waiting for transfers between devices: 27.8 us -> 22.2 us  [swap(): return lax.ppermute(a, axis, [(i, i ^ k) for i in range(n)])]
    pallas_call x1, Pallas kernels: 8.08 us -> 10.3 us  [shards(): pl.pallas_call(functools.partial(shared_kernel, False), out_shape=state,...]
    ppermute x3, waiting for transfers between devices: 5.03 us -> 6.3 us  [shards(): fetched.append(lax.ppermute(pair, ('z', 'core'), moves))]
  transfers between devices with their start and end apart: 31 -> 31, of which waited for: 18 -> 17; matrix products, arithmetic and copies ran while one was open for 5% -> 5% of each run, Pallas kernels for 9% -> 11%
where the time goes in v4:
time: 111 us; the launch traced here: 110 us
  starting transfers between devices  48 us (43%)
  waiting for transfers between devices  33.4 us (30%)
  Pallas kernels  22 us (20%)
  other arithmetic  3.62 us (3%)
  local copies, waits for them, and re-layouts  1.63 us (1%)
    ppermute x24, starting transfers between devices, swap(): return lax.ppermute(a, axis, [(i, i ^ k) for i in range(n)])  34.4 us
    ppermute x24, waiting for transfers between devices, swap(): return lax.ppermute(a, axis, [(i, i ^ k) for i in range(n)])  22.2 us
    ppermute x4, starting transfers between devices, shards(): arrived.append(lax.ppermute(terms[k], ('kv', 'x'), pairs))  10.7 us
    pallas_call x1, Pallas kernels, shards(): pl.pallas_call(functools.partial(shared_kernel, False), out_shape=state,...  10.3 us
    ppermute x3, waiting for transfers between devices, shards(): fetched.append(lax.ppermute(pair, ('z', 'core'), moves))  6.3 us
    pallas_call x1, Pallas kernels, shards(): pl.pallas_call(functools.partial(shared_kernel, True), out_shape=[struct(...  5.44 us
    ppermute x4, waiting for transfers between devices, shards(): arrived.append(lax.ppermute(terms[k], ('kv', 'x'), pairs))  4.89 us
    ppermute x3, starting transfers between devices, shards(): fetched.append(lax.ppermute(pair, ('z', 'core'), moves))  2.84 us
  transfers between devices with their start and end apart: 31, of which 17 were waited for; matrix products, arithmetic and copies ran while one was open for 5% of the time, Pallas kernels for 11%

profile of v4, /device:TPU:40, one launch (start us, length us, event | category | flops | bytes accessed | tf_op | source)
XLA Modules:
  0.0 109.6 jit_solution(7931533051823593083)
XLA Ops:
  0.6 1.5 %shard_map.166.q_ref = bf16[128,128]{1,0:T(8,128)(2,1)} custom-call(bf16[2,4,2048]{2,1,0:T(4,128)(2,1)} %bitcast.31, f32[1,128]{1,0:T(1,128)} %bitcast.35), custom_call_target="tpu_custom_call" | custom-call | tf_op jit(solution)/shard_map/pallas_call | solution.py:390
  2.1 5.4 %collective-permute-start.2 = (bf16[128,128]{1,0:T(8,128)(2,1)}, bf16[128,128]{1,0:T(8,128)(2,1)S(1)}, u32[]{:S(2)}, u32[]{:S(2)}) collective-permute-start(bf16[128,128]{1,0:T(8,128)(2,1)} %shard_map.166.q_ref), channel_id=1, source_target_pairs={{0,12},{2,14},{4,8},{6,10},{8,4},{10,6},{12,0},{14,2},{1,13},{3,15... | collective-permute-start | bytes 98312 | tf_op jit(solution)/shard_map/ppermute | solution.py:42
  7.6 1.4 %collective-permute-start.1 = (bf16[128,128]{1,0:T(8,128)(2,1)}, bf16[128,128]{1,0:T(8,128)(2,1)S(1)}, u32[]{:S(2)}, u32[]{:S(2)}) collective-permute-start(bf16[128,128]{1,0:T(8,128)(2,1)} %shard_map.166.q_ref), channel_id=1, source_target_pairs={{0,8},{2,10},{4,12},{6,14},{8,0},{10,2},{12,4},{14,6},{1,9},{3,11}... | collective-permute-start | bytes 98312 | tf_op jit(solution)/shard_map/ppermute | solution.py:42
  9.0 0.9 collective-permute-start
  9.9 1.0 pad_maximum_fusion.1.refs_5_
  11.0 1.1 collective-permute-start.9
  12.1 1.3 %pad_maximum_fusion.refs_0_ = bf16[4096,128]{1,0:T(8,128)(2,1)S(1)} fusion(bf16[2048,128]{1,0:T(8,128)(2,1)} %bitcast.27, bf16[2048,128]{1,0:T(8,128)(2,1)} %bitcast.28), kind=kLoop, calls=%fused_computation | loop fusion | flops 2097152 | bytes 2097152 | tf_op jit(solution)/shard_map/concatenate | solution.py:398
  13.9 1.1 %collective-permute-start.6 = (bf16[4096,128]{1,0:T(8,128)(2,1)S(1)}, bf16[4096,128]{1,0:T(8,128)(2,1)S(1)}, u32[]{:S(2)}, u32[]{:S(2)}) collective-permute-start(bf16[4096,128]{1,0:T(8,128)(2,1)S(1)} %pad_maximum_fusion.refs_0_), channel_id=1, source_target_pairs={{0,2},{2,0},{4,6},{6,4},{8,10},{10,8},{12,14},{14,12},{1,3},{3,1},... | collective-permute-start | bytes 3145736 | tf_op jit(solution)/shard_map/ppermute | solution.py:42
  15.3 0.7 collective-permute-done.1
  16.1 3.1 %collective-permute-start.3 = (bf16[512,128]{1,0:T(8,128)(2,1)S(1)}, bf16[512,128]{1,0:T(8,128)(2,1)S(1)}, u32[]{:S(2)}, u32[]{:S(2)}) collective-permute-start(bf16[512,128]{1,0:T(8,128)(2,1)S(1)} %pad_maximum_fusion.2.refs_1_), channel_id=1, source_target_pairs={{0,32},{16,48},{32,0},{48,16},{1,33},{17,49},{33,1},{49,17},{2,34}... | collective-permute-start | bytes 393224 | tf_op jit(solution)/shard_map/ppermute | solution.py:42
  19.2 0.6 collective-permute-start.7
  19.8 0.6 collective-permute-start.8
  20.8 3.1 %collective-permute-done.3.refs_3_ = bf16[512,128]{1,0:T(8,128)(2,1)S(1)} collective-permute-done((bf16[512,128]{1,0:T(8,128)(2,1)S(1)}, bf16[512,128]{1,0:T(8,128)(2,1)S(1)}, u32[]{:S(2)}, u32[]{:S(2)}) %collective-permute-start.3) | collective-permute-done | bytes 131104 | tf_op jit(solution)/shard_map/ppermute | solution.py:42
  24.0 1.3 %collective-permute-start.11 = (bf16[64,2048]{1,0:T(8,128)(2,1)S(1)}, bf16[64,2048]{1,0:T(8,128)(2,1)S(1)}, u32[]{:S(2)}, u32[]{:S(2)}) collective-permute-start(bf16[64,2048]{1,0:T(8,128)(2,1)S(1)} %bitcast.21), channel_id=1, source_target_pairs={{0,16},{16,0},{32,48},{48,32},{1,17},{17,1},{33,49},{49,33},{2,18}... | collective-permute-start | bytes 786440 | tf_op jit(solution)/shard_map/ppermute | solution.py:42
  25.3 0.9 collective-permute-done.7.refs_2_
  26.2 1.8 %collective-permute-start.12 = (bf16[64,2048]{1,0:T(8,128)(2,1)S(1)}, bf16[64,2048]{1,0:T(8,128)(2,1)S(1)}, u32[]{:S(2)}, u32[]{:S(2)}) collective-permute-start(bf16[64,2048]{1,0:T(8,128)(2,1)S(1)} %bitcast.22), channel_id=1, source_target_pairs={{0,32},{16,48},{32,0},{48,16},{1,33},{17,49},{33,1},{49,17},{2,34}... | collective-permute-start | bytes 786440 | tf_op jit(solution)/shard_map/ppermute | solution.py:42
  27.9 2.3 %collective-permute-start.13 = (bf16[64,2048]{1,0:T(8,128)(2,1)S(1)}, bf16[64,2048]{1,0:T(8,128)(2,1)S(1)}, u32[]{:S(2)}, u32[]{:S(2)}) collective-permute-start(bf16[64,2048]{1,0:T(8,128)(2,1)S(1)} %bitcast.23), channel_id=1, source_target_pairs={{0,48},{16,32},{32,16},{48,0},{1,49},{17,33},{33,17},{49,1},{2,50}... | collective-permute-start | bytes 786440 | tf_op jit(solution)/shard_map/ppermute | solution.py:42
  30.4 0.3 collective-permute-start.5
  30.6 10.3 %shard_map.167 = (bf16[2080,128]{1,0:T(8,128)(2,1)S(1)}, f32[2080,128]{1,0:T(8,128)S(1)}, f32[2080,128]{1,0:T(8,128)S(1)}, f32[2080,128]{1,0:T(8,128)S(1)}) custom-call(s32[80]{0:T(128)S(1)} %pad_add_fusion.1.meta_ref, bf16[4096,128]{1,0:T(8,128)(2,1)S(1)} %pad_maximum_fusion.refs_0_, bf16[512,128]{1,0:T(8,128)(2,1)S(1)} %pad_maximum_fusion.2.refs_1_, ...), custom_call_target="tpu_custom_call" | custom-call | flops 2147483648 | bytes 8388608 | tf_op jit(solution)/shard_map/pallas_call | solution.py:423
  41.0 1.8 %shard_map.168 = (f32[128,128]{1,0:T(8,128)S(1)}, f32[8,128]{1,0:T(8,128)S(1)}) custom-call(s32[4]{0:T(128)S(1)} %copy-done.6, bf16[128,128]{1,0:T(8,128)(2,1)S(1)} %copy-done.2, bf16[4,512,128]{2,1,0:T(8,128)(2,1)S(1)} %bitcast.19, bf16[4,512,128]{2,1,0:T(8,128)(2,1)S(1)} %bitcast.20, bf16[8,128]{1,0:T(8,128)(2,1)S(1)} %bitcast.25, bf16[8,128]{1,0:T(8,128)(2,1)S(1)} %bitcast.26), custom_call_target="tpu_custom_call" | custom-call | tf_op jit(solution)/shard_map/pallas_call | solution.py:435
  43.1 2.4 %collective-permute-done.14.refs_2_ = bf16[4096,128]{1,0:T(8,128)(2,1)S(1)} collective-permute-done((bf16[4096,128]{1,0:T(8,128)(2,1)S(1)}, bf16[4096,128]{1,0:T(8,128)(2,1)S(1)}, u32[]{:S(2)}, u32[]{:S(2)}) %collective-permute-start.14) | collective-permute-done | bytes 1048608 | tf_op jit(solution)/shard_map/ppermute | solution.py:42
  45.5 5.4 %shard_map.169 = (bf16[576,128]{1,0:T(8,128)(2,1)S(1)}, bf16[576,128]{1,0:T(8,128)(2,1)S(1)}, bf16[576,128]{1,0:T(8,128)(2,1)S(1)}, bf16[576,128]{1,0:T(8,128)(2,1)S(1)}) custom-call(s32[112]{0:T(128)S(1)} %pad_add_fusion.meta_ref, bf16[4096,128]{1,0:T(8,128)(2,1)S(1)} %collective-permute-done.5.refs_0_, ...), custom_call_target="tpu_custom_call" | custom-call | flops 2147483648 | bytes 8388608 | tf_op jit(solution)/shard_map/pallas_call | solution.py:452
  50.9 2.9 %collective-permute-start.15 = (bf16[576,128]{1,0:T(8,128)(2,1)S(1)}, bf16[576,128]{1,0:T(8,128)(2,1)S(1)}, u32[]{:S(2)}, u32[]{:S(2)}) collective-permute-start(bf16[576,128]{1,0:T(8,128)(2,1)S(1)} %get-tuple-element.57), channel_id=1, source_target_pairs={{0,32},{16,48},{32,0},{48,16},{1,33},{17,49},{33,1},{49,17},{2,34}... | collective-permute-start | bytes 442376 | tf_op jit(solution)/shard_map/ppermute | solution.py:42
  53.8 0.6 collective-permute-start.16
  54.4 0.7 collective-permute-start.17
  55.1 3.4 %collective-permute-done.15.b = bf16[576,128]{1,0:T(8,128)(2,1)S(1)} collective-permute-done((bf16[576,128]{1,0:T(8,128)(2,1)S(1)}, bf16[576,128]{1,0:T(8,128)(2,1)S(1)}, u32[]{:S(2)}, u32[]{:S(2)}) %collective-permute-start.15) | collective-permute-done | bytes 147488 | tf_op jit(solution)/shard_map/ppermute | solution.py:42
  58.5 2.9 %collective-permute-done.16.c = bf16[576,128]{1,0:T(8,128)(2,1)S(1)} collective-permute-done((bf16[576,128]{1,0:T(8,128)(2,1)S(1)}, bf16[576,128]{1,0:T(8,128)(2,1)S(1)}, u32[]{:S(2)}, u32[]{:S(2)}) %collective-permute-start.16) | collective-permute-done | bytes 147488 | tf_op jit(solution)/shard_map/ppermute | solution.py:42
  61.6 0.4 shard_map.170
  62.0 5.2 %collective-permute-start.18 = (bf16[144,128]{1,0:T(8,128)(2,1)S(1)}, bf16[144,128]{1,0:T(8,128)(2,1)S(1)}, u32[]{:S(2)}, u32[]{:S(2)}) collective-permute-start(bf16[144,128]{1,0:T(8,128)(2,1)S(1)} %get-tuple-element.61), channel_id=1, source_target_pairs={{0,8},{2,10},{4,12},{6,14},{8,0},{10,2},{12,4},{14,6},{1,9},{3,11}... | collective-permute-start | bytes 110600 | tf_op jit(solution)/shard_map/ppermute | solution.py:42
  67.2 1.6 %collective-permute-start.19 = (bf16[144,128]{1,0:T(8,128)(2,1)S(1)}, bf16[144,128]{1,0:T(8,128)(2,1)S(1)}, u32[]{:S(2)}, u32[]{:S(2)}) collective-permute-start(bf16[144,128]{1,0:T(8,128)(2,1)S(1)} %get-tuple-element.62), channel_id=1, source_target_pairs={{0,4},{2,6},{4,0},{6,2},{8,12},{10,14},{12,8},{14,10},{1,5},{3,7},... | collective-permute-start | bytes 110600 | tf_op jit(solution)/shard_map/ppermute | solution.py:42
  68.8 1.3 %collective-permute-done.18.refs_1_ = bf16[144,128]{1,0:T(8,128)(2,1)S(1)} collective-permute-done((bf16[144,128]{1,0:T(8,128)(2,1)S(1)}, bf16[144,128]{1,0:T(8,128)(2,1)S(1)}, u32[]{:S(2)}, u32[]{:S(2)}) %collective-permute-start.18) | collective-permute-done | bytes 36896 | tf_op jit(solution)/shard_map/ppermute | solution.py:42
  70.1 2.1 %collective-permute-done.19.refs_2_ = bf16[144,128]{1,0:T(8,128)(2,1)S(1)} collective-permute-done((bf16[144,128]{1,0:T(8,128)(2,1)S(1)}, bf16[144,128]{1,0:T(8,128)(2,1)S(1)}, u32[]{:S(2)}, u32[]{:S(2)}) %collective-permute-start.19) | collective-permute-done | bytes 36896 | tf_op jit(solution)/shard_map/ppermute | solution.py:42
  72.2 2.7 %collective-permute-done.20.refs_3_ = bf16[144,128]{1,0:T(8,128)(2,1)S(1)} collective-permute-done((bf16[144,128]{1,0:T(8,128)(2,1)S(1)}, bf16[144,128]{1,0:T(8,128)(2,1)S(1)}, u32[]{:S(2)}, u32[]{:S(2)}) %collective-permute-start.20) | collective-permute-done | bytes 36896 | tf_op jit(solution)/shard_map/ppermute | solution.py:42
  75.2 1.2 %collective-permute-done.21 = bf16[8,2048]{1,0:T(8,128)(2,1)S(1)} collective-permute-done((bf16[8,2048]{1,0:T(8,128)(2,1)S(1)}, bf16[8,2048]{1,0:T(8,128)(2,1)S(1)}, u32[]{:S(2)}, u32[]{:S(2)}) %collective-permute-start.21) | collective-permute-done | bytes 32800 | tf_op jit(solution)/shard_map/ppermute | solution.py:42
  76.4 1.3 %collective-permute-start.22 = (bf16[16,2048]{1,0:T(8,128)(2,1)S(1)}, bf16[16,2048]{1,0:T(8,128)(2,1)S(1)}, u32[]{:S(2)}, u32[]{:S(2)}) collective-permute-start(bf16[16,2048]{1,0:T(8,128)(2,1)S(1)} %constant_dynamic-update-slice_fusion.pair_ref), channel_id=1, source_target_pairs={{0,2},{1,11},{2,0},{3,9},{4,6},{5,15},{6,4},{7,13},{8,10},{9,3},{1... | collective-permute-start | bytes 196616 | tf_op jit(solution)/shard_map/ppermute | solution.py:489
  77.7 1.5 %collective-permute-start.25 = (bf16[8,2048]{1,0:T(8,128)(2,1)S(1)}, bf16[8,2048]{1,0:T(8,128)(2,1)S(1)}, u32[]{:S(2)}, u32[]{:S(2)}) collective-permute-start(bf16[8,2048]{1,0:T(8,128)(2,1)S(1)} %get-tuple-element.68), channel_id=1, source_target_pairs={{0,8},{2,10},{4,12},{6,14},{8,0},{10,2},{12,4},{14,6},{1,9},{3,11}... | collective-permute-start | bytes 98312 | tf_op jit(solution)/shard_map/ppermute | solution.py:42
  79.2 1.4 %collective-permute-start.23 = (bf16[16,2048]{1,0:T(8,128)(2,1)S(1)}, bf16[16,2048]{1,0:T(8,128)(2,1)S(1)}, u32[]{:S(2)}, u32[]{:S(2)}) collective-permute-start(bf16[16,2048]{1,0:T(8,128)(2,1)S(1)} %constant_dynamic-update-slice_fusion.pair_ref), channel_id=1, source_target_pairs={{0,4},{1,13},{2,6},{3,15},{4,0},{5,9},{6,2},{7,11},{8,12},{9,5},{1... | collective-permute-start | bytes 196616 | tf_op jit(solution)/shard_map/ppermute | solution.py:489
  80.7 4.5 %collective-permute-done.23 = bf16[16,2048]{1,0:T(8,128)(2,1)S(1)} collective-permute-done((bf16[16,2048]{1,0:T(8,128)(2,1)S(1)}, bf16[16,2048]{1,0:T(8,128)(2,1)S(1)}, u32[]{:S(2)}, u32[]{:S(2)}) %collective-permute-start.23) | collective-permute-done | bytes 65568 | tf_op jit(solution)/shard_map/ppermute | solution.py:489
  85.2 1.9 %collective-permute-done.24 = bf16[16,2048]{1,0:T(8,128)(2,1)S(1)} collective-permute-done((bf16[16,2048]{1,0:T(8,128)(2,1)S(1)}, bf16[16,2048]{1,0:T(8,128)(2,1)S(1)}, u32[]{:S(2)}, u32[]{:S(2)}) %collective-permute-start.24) | collective-permute-done | bytes 65568 | tf_op jit(solution)/shard_map/ppermute | solution.py:489
  87.1 1.9 %collective-permute-start.26 = (bf16[56,2048]{1,0:T(8,128)(2,1)S(1)}, bf16[56,2048]{1,0:T(8,128)(2,1)S(1)}, u32[]{:S(2)}, u32[]{:S(2)}) collective-permute-start(bf16[56,2048]{1,0:T(8,128)(2,1)S(1)} %constant_dynamic-update-slice_fusion.2.here_ref), channel_id=1, source_target_pairs={{0,1},{1,0},{2,3},{3,2},{4,5},{5,4},{6,7},{7,6},{8,9},{9,8},{10,11... | collective-permute-start | bytes 688136 | tf_op jit(solution)/shard_map/ppermute | solution.py:42
  89.1 1.0 collective-permute-done.26.there_ref
  90.1 1.1 %shard_map.172 = (f32[64,128]{1,0:T(8,128)S(1)}, f32[64,128]{1,0:T(8,128)S(1)}, f32[64,128]{1,0:T(8,128)S(1)}, f32[64,128]{1,0:T(8,128)S(1)}) custom-call(s32[2]{0:T(128)S(1)} %pad_add_fusion.3.where_ref, bf16[16,2048]{1,0:T(8,128)(2,1)S(1)} %constant_dynamic-update-slice_fusion.pair_ref, bf16[56,2048]{1,0:T(8,128)(2,1)S(1)} %constant_dynamic-update-slice_fusion.2.here_ref, ...), custom_call_target="tpu_custom_call" | custom-call | tf_op jit(solution)/shard_map/pallas_call | solution.py:495
  91.2 3.7 %collective-permute-start.27 = (f32[64,128]{1,0:T(8,128)S(1)}, f32[64,128]{1,0:T(8,128)S(1)}, u32[]{:S(2)}, u32[]{:S(2)}) collective-permute-start(f32[64,128]{1,0:T(8,128)S(1)} %get-tuple-element.73), channel_id=1, source_target_pairs={{0,0},{16,64},{32,128},{48,192},{64,16},{80,80},{96,144},{112,208}... | collective-permute-start | bytes 98312 | tf_op jit(solution)/shard_map/ppermute | solution.py:506
  95.0 7.0 %collective-permute-start.29 = (f32[64,128]{1,0:T(8,128)S(1)}, f32[64,128]{1,0:T(8,128)S(1)}, u32[]{:S(2)}, u32[]{:S(2)}) collective-permute-start(f32[64,128]{1,0:T(8,128)S(1)} %get-tuple-element.75), channel_id=1, source_target_pairs={{0,32},{16,96},{32,160},{48,224},{64,48},{80,112},{96,176},{112,24... | collective-permute-start | bytes 98312 | tf_op jit(solution)/shard_map/ppermute | solution.py:506
  102.0 0.7 reshape.90
  102.8 0.6 copy.23
  103.5 4.7 %collective-permute-done.30.d = f32[64,128]{1,0:T(8,128)S(1)} collective-permute-done((f32[64,128]{1,0:T(8,128)S(1)}, f32[64,128]{1,0:T(8,128)S(1)}, u32[]{:S(2)}, u32[]{:S(2)}) %collective-permute-start.30) | collective-permute-done | bytes 32800 | tf_op jit(solution)/shard_map/ppermute | solution.py:506
  108.3 1.3 %shard_map.173 = f32[2,64,64]{2,1,0:T(8,128)} custom-call(s32[2]{0:T(128)S(1)} %pad_add_fusion.2.where_ref, f32[64,128]{1,0:T(8,128)S(1)} %collective-permute-done.27.a, f32[64,128]{1,0:T(8,128)S(1)} %collective-permute-done.28.b, f32[64,128]{1,0:T(8,128)S(1)} %collective-permute-done.29.c, f32[64,128]{1,0:T(8,128)S(1)} %collective-permute-done.30.d), custom_call_target="tpu_custom_call" | custom-call | tf_op jit(solution)/shard_map/pallas_call | solution.py:507
  (70 shorter events, 3.0 us)
Async XLA Ops:
  2.1 13.2 %collective-permute-start.2 = (bf16[128,128]{1,0:T(8,128)(2,1)}, bf16[128,128]{1,0:T(8,128)(2,1)S(1)}, u32[]{:S(2)}, u32[]{:S(2)}) collective-permute-start(bf16[128,128]{1,0:T(8,128)(2,1)} %shard_map.166.q_ref), channel_id=1, source_target_pairs={{0,12},{2,14},{4,8},{6,10},{8,4},{10,6},{12,0},{14,2},{1,13},{3,15... | collective-permute-start | bytes 98312 | tf_op jit(solution)/shard_map/ppermute | solution.py:42
  7.6 8.5 %collective-permute-start.1 = (bf16[128,128]{1,0:T(8,128)(2,1)}, bf16[128,128]{1,0:T(8,128)(2,1)S(1)}, u32[]{:S(2)}, u32[]{:S(2)}) collective-permute-start(bf16[128,128]{1,0:T(8,128)(2,1)} %shard_map.166.q_ref), channel_id=1, source_target_pairs={{0,8},{2,10},{4,12},{6,14},{8,0},{10,2},{12,4},{14,6},{1,9},{3,11}... | collective-permute-start | bytes 98312 | tf_op jit(solution)/shard_map/ppermute | solution.py:42
  9.0 7.1 %collective-permute-start = (bf16[128,128]{1,0:T(8,128)(2,1)}, bf16[128,128]{1,0:T(8,128)(2,1)S(1)}, u32[]{:S(2)}, u32[]{:S(2)}) collective-permute-start(bf16[128,128]{1,0:T(8,128)(2,1)} %shard_map.166.q_ref), channel_id=1, source_target_pairs={{0,4},{2,6},{4,0},{6,2},{8,12},{10,14},{12,8},{14,10},{1,5},{3,7},... | collective-permute-start | bytes 98312 | tf_op jit(solution)/shard_map/ppermute | solution.py:42
  10.9 2.6 %copy-start.8 = (s32[256]{0:T(256)S(1)}, s32[256]{0:T(256)}, u32[]{:S(2)}) copy-start(s32[256]{0:T(256)} %param.26) | copy-start | bytes 3076
  10.9 2.9 %collective-permute-start.4 = (bf16[1024,128]{1,0:T(8,128)(2,1)S(1)}, bf16[1024,128]{1,0:T(8,128)(2,1)S(1)}, u32[]{:S(2)}, u32[]{:S(2)}) collective-permute-start(bf16[1024,128]{1,0:T(8,128)(2,1)S(1)} %pad_maximum_fusion.1.refs_5_), channel_id=1, source_target_pairs={{0,1},{1,0},{2,3},{3,2},{4,5},{5,4},{6,7},{7,6},{8,9},{9,8},{10,11... | collective-permute-start | bytes 786440 | tf_op jit(solution)/shard_map/ppermute | solution.py:42
  11.0 9.6 %collective-permute-start.9 = (bf16[1024,128]{1,0:T(8,128)(2,1)S(1)}, bf16[1024,128]{1,0:T(8,128)(2,1)S(1)}, u32[]{:S(2)}, u32[]{:S(2)}) collective-permute-start(bf16[1024,128]{1,0:T(8,128)(2,1)S(1)} %pad_maximum_fusion.1.refs_5_), channel_id=1, source_target_pairs={{0,2},{2,0},{4,6},{6,4},{8,10},{10,8},{12,14},{14,12},{1,3},{3,1},... | collective-permute-start | bytes 786440 | tf_op jit(solution)/shard_map/ppermute | solution.py:42
  12.1 2.9 %copy-start.7 = (s32[512]{0:T(512)S(1)}, s32[512]{0:T(512)}, u32[]{:S(2)}) copy-start(s32[512]{0:T(512)} %param.29) | copy-start | bytes 6148
  12.1 3.0 %copy-start.9 = (s32[16]{0:T(128)S(1)}, s32[16]{0:T(128)}, u32[]{:S(2)}) copy-start(s32[16]{0:T(128)} %param.27) | copy-start | bytes 196
  12.1 3.9 %copy-start.2 = (bf16[128,128]{1,0:T(8,128)(2,1)S(1)}, bf16[128,128]{1,0:T(8,128)(2,1)}, u32[]{:S(2)}) copy-start(bf16[128,128]{1,0:T(8,128)(2,1)} %shard_map.166.q_ref) | copy-start | bytes 98308
  12.1 11.9 %copy-start.3 = (bf16[2048,64]{0,1:T(8,128)(2,1)S(1)}, bf16[2048,64]{0,1:T(8,128)(2,1)}, u32[]{:S(2)}) copy-start(bf16[2048,64]{0,1:T(8,128)(2,1)} %param.25) | copy-start | bytes 786436
  13.9 28.9 %collective-permute-start.6 = (bf16[4096,128]{1,0:T(8,128)(2,1)S(1)}, bf16[4096,128]{1,0:T(8,128)(2,1)S(1)}, u32[]{:S(2)}, u32[]{:S(2)}) collective-permute-start(bf16[4096,128]{1,0:T(8,128)(2,1)S(1)} %pad_maximum_fusion.refs_0_), channel_id=1, source_target_pairs={{0,2},{2,0},{4,6},{6,4},{8,10},{10,8},{12,14},{14,12},{1,3},{3,1},... | collective-permute-start | bytes 3145736 | tf_op jit(solution)/shard_map/ppermute | solution.py:42
  16.1 7.9 %collective-permute-start.3 = (bf16[512,128]{1,0:T(8,128)(2,1)S(1)}, bf16[512,128]{1,0:T(8,128)(2,1)S(1)}, u32[]{:S(2)}, u32[]{:S(2)}) collective-permute-start(bf16[512,128]{1,0:T(8,128)(2,1)S(1)} %pad_maximum_fusion.2.refs_1_), channel_id=1, source_target_pairs={{0,32},{16,48},{32,0},{48,16},{1,33},{17,49},{33,1},{49,17},{2,34}... | collective-permute-start | bytes 393224 | tf_op jit(solution)/shard_map/ppermute | solution.py:42
  19.2 7.0 %collective-permute-start.7 = (bf16[512,128]{1,0:T(8,128)(2,1)S(1)}, bf16[512,128]{1,0:T(8,128)(2,1)S(1)}, u32[]{:S(2)}, u32[]{:S(2)}) collective-permute-start(bf16[512,128]{1,0:T(8,128)(2,1)S(1)} %pad_maximum_fusion.2.refs_1_), channel_id=1, source_target_pairs={{0,16},{16,0},{32,48},{48,32},{1,17},{17,1},{33,49},{49,33},{2,18}... | collective-permute-start | bytes 393224 | tf_op jit(solution)/shard_map/ppermute | solution.py:42
  19.8 8.2 %collective-permute-start.8 = (bf16[512,128]{1,0:T(8,128)(2,1)S(1)}, bf16[512,128]{1,0:T(8,128)(2,1)S(1)}, u32[]{:S(2)}, u32[]{:S(2)}) collective-permute-start(bf16[512,128]{1,0:T(8,128)(2,1)S(1)} %pad_maximum_fusion.2.refs_1_), channel_id=1, source_target_pairs={{0,48},{16,32},{32,16},{48,0},{1,49},{17,33},{33,17},{49,1},{2,50}... | collective-permute-start | bytes 393224 | tf_op jit(solution)/shard_map/ppermute | solution.py:42
  20.6 9.8 %collective-permute-start.10 = (bf16[1024,128]{1,0:T(8,128)(2,1)S(1)}, bf16[1024,128]{1,0:T(8,128)(2,1)S(1)}, u32[]{:S(2)}, u32[]{:S(2)}) collective-permute-start(bf16[1024,128]{1,0:T(8,128)(2,1)S(1)} %collective-permute-done.9.refs_6_), channel_id=1, source_target_pairs={{0,1},{1,0},{2,3},{3,2},{4,5},{5,4},{6,7},{7,6},{8,9},{9,8},{10,11... | collective-permute-start | bytes 786440 | tf_op jit(solution)/shard_map/ppermute | solution.py:42
  24.0 16.9 %collective-permute-start.11 = (bf16[64,2048]{1,0:T(8,128)(2,1)S(1)}, bf16[64,2048]{1,0:T(8,128)(2,1)S(1)}, u32[]{:S(2)}, u32[]{:S(2)}) collective-permute-start(bf16[64,2048]{1,0:T(8,128)(2,1)S(1)} %bitcast.21), channel_id=1, source_target_pairs={{0,16},{16,0},{32,48},{48,32},{1,17},{17,1},{33,49},{49,33},{2,18}... | collective-permute-start | bytes 786440 | tf_op jit(solution)/shard_map/ppermute | solution.py:42
  26.2 14.7 %collective-permute-start.12 = (bf16[64,2048]{1,0:T(8,128)(2,1)S(1)}, bf16[64,2048]{1,0:T(8,128)(2,1)S(1)}, u32[]{:S(2)}, u32[]{:S(2)}) collective-permute-start(bf16[64,2048]{1,0:T(8,128)(2,1)S(1)} %bitcast.22), channel_id=1, source_target_pairs={{0,32},{16,48},{32,0},{48,16},{1,33},{17,49},{33,1},{49,17},{2,34}... | collective-permute-start | bytes 786440 | tf_op jit(solution)/shard_map/ppermute | solution.py:42
  27.9 13.0 %collective-permute-start.13 = (bf16[64,2048]{1,0:T(8,128)(2,1)S(1)}, bf16[64,2048]{1,0:T(8,128)(2,1)S(1)}, u32[]{:S(2)}, u32[]{:S(2)}) collective-permute-start(bf16[64,2048]{1,0:T(8,128)(2,1)S(1)} %bitcast.23), channel_id=1, source_target_pairs={{0,48},{16,32},{32,16},{48,0},{1,49},{17,33},{33,17},{49,1},{2,50}... | collective-permute-start | bytes 786440 | tf_op jit(solution)/shard_map/ppermute | solution.py:42
  30.3 10.6 %copy-start = (bf16[4,512,1,128]{3,1,2,0:T(8,128)(2,1)S(1)}, bf16[4,512,1,128]{3,1,2,0:T(8,128)(2,1)}, u32[]{:S(2)}) copy-start(bf16[4,512,1,128]{3,1,2,0:T(8,128)(2,1)} %param.23) | copy-start | bytes 1572868
  30.3 10.6 %copy-start.1 = (bf16[4,512,1,128]{3,1,2,0:T(8,128)(2,1)S(1)}, bf16[4,512,1,128]{3,1,2,0:T(8,128)(2,1)}, u32[]{:S(2)}) copy-start(bf16[4,512,1,128]{3,1,2,0:T(8,128)(2,1)} %param.24) | copy-start | bytes 1572868
  30.3 10.6 %copy-start.4 = (bf16[2,4,1,128]{3,1,2,0:T(4,128)(2,1)S(1)}, bf16[2,4,1,128]{3,1,2,0:T(4,128)(2,1)}, u32[]{:S(2)}) copy-start(bf16[2,4,1,128]{3,1,2,0:T(4,128)(2,1)} %param.17) | copy-start | bytes 6148
  30.3 10.6 %copy-start.5 = (bf16[2,4,1,128]{3,1,2,0:T(4,128)(2,1)S(1)}, bf16[2,4,1,128]{3,1,2,0:T(4,128)(2,1)}, u32[]{:S(2)}) copy-start(bf16[2,4,1,128]{3,1,2,0:T(4,128)(2,1)} %param.18) | copy-start | bytes 6148
  30.3 10.6 %copy-start.6 = (s32[4]{0:T(128)S(1)}, s32[4]{0:T(128)}, u32[]{:S(2)}) copy-start(s32[4]{0:T(128)} %length_ref.1) | copy-start | bytes 52
  30.4 12.7 %collective-permute-start.5 = (bf16[4096,128]{1,0:T(8,128)(2,1)S(1)}, bf16[4096,128]{1,0:T(8,128)(2,1)S(1)}, u32[]{:S(2)}, u32[]{:S(2)}) collective-permute-start(bf16[4096,128]{1,0:T(8,128)(2,1)S(1)} %pad_maximum_fusion.refs_0_), channel_id=1, source_target_pairs={{0,1},{1,0},{2,3},{3,2},{4,5},{5,4},{6,7},{7,6},{8,9},{9,8},{10,11... | collective-permute-start | bytes 3145736 | tf_op jit(solution)/shard_map/ppermute | solution.py:42
  42.8 2.7 %collective-permute-start.14 = (bf16[4096,128]{1,0:T(8,128)(2,1)S(1)}, bf16[4096,128]{1,0:T(8,128)(2,1)S(1)}, u32[]{:S(2)}, u32[]{:S(2)}) collective-permute-start(bf16[4096,128]{1,0:T(8,128)(2,1)S(1)} %collective-permute-done.6.refs_1_), channel_id=1, source_target_pairs={{0,1},{1,0},{2,3},{3,2},{4,5},{5,4},{6,7},{7,6},{8,9},{9,8},{10,11... | collective-permute-start | bytes 3145736 | tf_op jit(solution)/shard_map/ppermute | solution.py:42
  50.9 7.6 %collective-permute-start.15 = (bf16[576,128]{1,0:T(8,128)(2,1)S(1)}, bf16[576,128]{1,0:T(8,128)(2,1)S(1)}, u32[]{:S(2)}, u32[]{:S(2)}) collective-permute-start(bf16[576,128]{1,0:T(8,128)(2,1)S(1)} %get-tuple-element.57), channel_id=1, source_target_pairs={{0,32},{16,48},{32,0},{48,16},{1,33},{17,49},{33,1},{49,17},{2,34}... | collective-permute-start | bytes 442376 | tf_op jit(solution)/shard_map/ppermute | solution.py:42
  53.8 7.6 %collective-permute-start.16 = (bf16[576,128]{1,0:T(8,128)(2,1)S(1)}, bf16[576,128]{1,0:T(8,128)(2,1)S(1)}, u32[]{:S(2)}, u32[]{:S(2)}) collective-permute-start(bf16[576,128]{1,0:T(8,128)(2,1)S(1)} %get-tuple-element.58), channel_id=1, source_target_pairs={{0,16},{16,0},{32,48},{48,32},{1,17},{17,1},{33,49},{49,33},{2,18}... | collective-permute-start | bytes 442376 | tf_op jit(solution)/shard_map/ppermute | solution.py:42
  54.4 7.2 %collective-permute-start.17 = (bf16[576,128]{1,0:T(8,128)(2,1)S(1)}, bf16[576,128]{1,0:T(8,128)(2,1)S(1)}, u32[]{:S(2)}, u32[]{:S(2)}) collective-permute-start(bf16[576,128]{1,0:T(8,128)(2,1)S(1)} %get-tuple-element.59), channel_id=1, source_target_pairs={{0,48},{16,32},{32,16},{48,0},{1,49},{17,33},{33,17},{49,1},{2,50}... | collective-permute-start | bytes 442376 | tf_op jit(solution)/shard_map/ppermute | solution.py:42
  62.0 8.1 %collective-permute-start.18 = (bf16[144,128]{1,0:T(8,128)(2,1)S(1)}, bf16[144,128]{1,0:T(8,128)(2,1)S(1)}, u32[]{:S(2)}, u32[]{:S(2)}) collective-permute-start(bf16[144,128]{1,0:T(8,128)(2,1)S(1)} %get-tuple-element.61), channel_id=1, source_target_pairs={{0,8},{2,10},{4,12},{6,14},{8,0},{10,2},{12,4},{14,6},{1,9},{3,11}... | collective-permute-start | bytes 110600 | tf_op jit(solution)/shard_map/ppermute | solution.py:42
  67.2 5.0 %collective-permute-start.19 = (bf16[144,128]{1,0:T(8,128)(2,1)S(1)}, bf16[144,128]{1,0:T(8,128)(2,1)S(1)}, u32[]{:S(2)}, u32[]{:S(2)}) collective-permute-start(bf16[144,128]{1,0:T(8,128)(2,1)S(1)} %get-tuple-element.62), channel_id=1, source_target_pairs={{0,4},{2,6},{4,0},{6,2},{8,12},{10,14},{12,8},{14,10},{1,5},{3,7},... | collective-permute-start | bytes 110600 | tf_op jit(solution)/shard_map/ppermute | solution.py:42
  68.8 6.1 %collective-permute-start.20 = (bf16[144,128]{1,0:T(8,128)(2,1)S(1)}, bf16[144,128]{1,0:T(8,128)(2,1)S(1)}, u32[]{:S(2)}, u32[]{:S(2)}) collective-permute-start(bf16[144,128]{1,0:T(8,128)(2,1)S(1)} %get-tuple-element.63), channel_id=1, source_target_pairs={{0,12},{2,14},{4,8},{6,10},{8,4},{10,6},{12,0},{14,2},{1,13},{3,15... | collective-permute-start | bytes 110600 | tf_op jit(solution)/shard_map/ppermute | solution.py:42
  75.1 1.3 %collective-permute-start.21 = (bf16[8,2048]{1,0:T(8,128)(2,1)S(1)}, bf16[8,2048]{1,0:T(8,128)(2,1)S(1)}, u32[]{:S(2)}, u32[]{:S(2)}) collective-permute-start(bf16[8,2048]{1,0:T(8,128)(2,1)S(1)} %get-tuple-element.68), channel_id=1, source_target_pairs={{0,1},{1,0},{2,3},{3,2},{4,5},{5,4},{6,7},{7,6},{8,9},{9,8},{10,11... | collective-permute-start | bytes 98312 | tf_op jit(solution)/shard_map/ppermute | solution.py:42
  76.4 4.4 %collective-permute-start.22 = (bf16[16,2048]{1,0:T(8,128)(2,1)S(1)}, bf16[16,2048]{1,0:T(8,128)(2,1)S(1)}, u32[]{:S(2)}, u32[]{:S(2)}) collective-permute-start(bf16[16,2048]{1,0:T(8,128)(2,1)S(1)} %constant_dynamic-update-slice_fusion.pair_ref), channel_id=1, source_target_pairs={{0,2},{1,11},{2,0},{3,9},{4,6},{5,15},{6,4},{7,13},{8,10},{9,3},{1... | collective-permute-start | bytes 196616 | tf_op jit(solution)/shard_map/ppermute | solution.py:489
  77.7 9.4 %collective-permute-start.25 = (bf16[8,2048]{1,0:T(8,128)(2,1)S(1)}, bf16[8,2048]{1,0:T(8,128)(2,1)S(1)}, u32[]{:S(2)}, u32[]{:S(2)}) collective-permute-start(bf16[8,2048]{1,0:T(8,128)(2,1)S(1)} %get-tuple-element.68), channel_id=1, source_target_pairs={{0,8},{2,10},{4,12},{6,14},{8,0},{10,2},{12,4},{14,6},{1,9},{3,11}... | collective-permute-start | bytes 98312 | tf_op jit(solution)/shard_map/ppermute | solution.py:42
  79.2 6.0 %collective-permute-start.23 = (bf16[16,2048]{1,0:T(8,128)(2,1)S(1)}, bf16[16,2048]{1,0:T(8,128)(2,1)S(1)}, u32[]{:S(2)}, u32[]{:S(2)}) collective-permute-start(bf16[16,2048]{1,0:T(8,128)(2,1)S(1)} %constant_dynamic-update-slice_fusion.pair_ref), channel_id=1, source_target_pairs={{0,4},{1,13},{2,6},{3,15},{4,0},{5,9},{6,2},{7,11},{8,12},{9,5},{1... | collective-permute-start | bytes 196616 | tf_op jit(solution)/shard_map/ppermute | solution.py:489
  80.6 6.4 %collective-permute-start.24 = (bf16[16,2048]{1,0:T(8,128)(2,1)S(1)}, bf16[16,2048]{1,0:T(8,128)(2,1)S(1)}, u32[]{:S(2)}, u32[]{:S(2)}) collective-permute-start(bf16[16,2048]{1,0:T(8,128)(2,1)S(1)} %constant_dynamic-update-slice_fusion.pair_ref), channel_id=1, source_target_pairs={{0,6},{1,15},{2,4},{3,13},{4,2},{5,11},{6,0},{7,9},{8,14},{9,7},{1... | collective-permute-start | bytes 196616 | tf_op jit(solution)/shard_map/ppermute | solution.py:489
  87.1 3.0 %collective-permute-start.26 = (bf16[56,2048]{1,0:T(8,128)(2,1)S(1)}, bf16[56,2048]{1,0:T(8,128)(2,1)S(1)}, u32[]{:S(2)}, u32[]{:S(2)}) collective-permute-start(bf16[56,2048]{1,0:T(8,128)(2,1)S(1)} %constant_dynamic-update-slice_fusion.2.here_ref), channel_id=1, source_target_pairs={{0,1},{1,0},{2,3},{3,2},{4,5},{5,4},{6,7},{7,6},{8,9},{9,8},{10,11... | collective-permute-start | bytes 688136 | tf_op jit(solution)/shard_map/ppermute | solution.py:42
  91.2 12.2 %collective-permute-start.27 = (f32[64,128]{1,0:T(8,128)S(1)}, f32[64,128]{1,0:T(8,128)S(1)}, u32[]{:S(2)}, u32[]{:S(2)}) collective-permute-start(f32[64,128]{1,0:T(8,128)S(1)} %get-tuple-element.73), channel_id=1, source_target_pairs={{0,0},{16,64},{32,128},{48,192},{64,16},{80,80},{96,144},{112,208}... | collective-permute-start | bytes 98312 | tf_op jit(solution)/shard_map/ppermute | solution.py:506
  94.9 8.5 %collective-permute-start.28 = (f32[64,128]{1,0:T(8,128)S(1)}, f32[64,128]{1,0:T(8,128)S(1)}, u32[]{:S(2)}, u32[]{:S(2)}) collective-permute-start(f32[64,128]{1,0:T(8,128)S(1)} %get-tuple-element.74), channel_id=1, source_target_pairs={{0,16},{16,80},{32,144},{48,208},{64,0},{80,64},{96,128},{112,192}... | collective-permute-start | bytes 98312 | tf_op jit(solution)/shard_map/ppermute | solution.py:506
  95.0 8.6 %collective-permute-start.29 = (f32[64,128]{1,0:T(8,128)S(1)}, f32[64,128]{1,0:T(8,128)S(1)}, u32[]{:S(2)}, u32[]{:S(2)}) collective-permute-start(f32[64,128]{1,0:T(8,128)S(1)} %get-tuple-element.75), channel_id=1, source_target_pairs={{0,32},{16,96},{32,160},{48,224},{64,48},{80,112},{96,176},{112,24... | collective-permute-start | bytes 98312 | tf_op jit(solution)/shard_map/ppermute | solution.py:506
  101.9 6.3 %collective-permute-start.30 = (f32[64,128]{1,0:T(8,128)S(1)}, f32[64,128]{1,0:T(8,128)S(1)}, u32[]{:S(2)}, u32[]{:S(2)}) collective-permute-start(f32[64,128]{1,0:T(8,128)S(1)} %get-tuple-element.76), channel_id=1, source_target_pairs={{0,48},{16,112},{32,176},{48,240},{64,32},{80,96},{96,160},{112,22... | collective-permute-start | bytes 98312 | tf_op jit(solution)/shard_map/ppermute | solution.py:506
